TPU v7x, 32 devices: a whole 2x2x4 slice. The times are simulated.
32 devices in a mesh: scene: 4 (over y, core), tp: 8 (over z, x).
Axes of the slice: x: 2, y: 2, z: 4, core: 2. Of those that a mesh axis runs over, the one named last changes fastest.
Arguments:
- frames_in: bfloat16 [4, 2048, 1024], P('scene', 'tp'), may hold values from -6 to 6
- qkv_weight: bfloat16 [2, 1024, 3072], P(None, None, 'tp'), may hold values from -0.1875 to 0.1875
- qkv_bias: bfloat16 [2, 3072], P(None, 'tp'), may hold values from -1.796875 to 1.796875
- out_weight: bfloat16 [2, 1024, 1024], P(None, 'tp'), may hold values from -0.75 to 0.75
- up_weight: bfloat16 [2, 1024, 4096], P(None, None, 'tp'), may hold values from -0.1875 to 0.1875
- up_bias: bfloat16 [2, 4096], P(None, 'tp'), may hold values from -1.796875 to 1.796875
- down_weight: bfloat16 [2, 4096, 1024], P(None, 'tp'), may hold values from -0.09375 to 0.09375
- norm_gain: float32 [2, 4, 1024], replicated, may hold values from 0.5 to 1.5
- norm_offset: float32 [2, 4, 1024], replicated, may hold values from -1.8 to 1.8
- head_gain: float32 [2, 2, 64], replicated, may hold values from 0.5 to 1.5
- head_offset: float32 [2, 2, 64], replicated, may hold values from -1.8 to 1.8
- cotangent: bfloat16 [4, 2048, 1024], P('scene', 'tp'), may hold values from -6 to 6
- visible: int32 [4, 2048], P('scene', 'tp'), may hold values 0 or 1
- query_count: int32 [4], P('scene'), may hold values from 128 to 512
Outputs:
- layer_out: bfloat16 [4, 2048, 1024], P('scene', 'tp')
- input_grad: bfloat16 [4, 2048, 1024], P('scene', 'tp')
- qkv_weight_grad: float32 [2, 1024, 3072], P(None, None, 'tp')
- qkv_bias_grad: float32 [2, 3072], P(None, 'tp')
- out_weight_grad: float32 [2, 1024, 1024], P(None, 'tp')
- up_weight_grad: float32 [2, 1024, 4096], P(None, None, 'tp')
- up_bias_grad: float32 [2, 4096], P(None, 'tp')
- down_weight_grad: float32 [2, 4096, 1024], P(None, 'tp')
- norm_gain_grad: float32 [2, 4, 1024], replicated
- norm_offset_grad: float32 [2, 4, 1024], replicated
- head_gain_grad: float32 [2, 2, 64], replicated
- head_offset_grad: float32 [2, 2, 64], replicated
All inputs are finite; a program needn't handle non-finite values. No bound on the sum of `visible` on one device may be relied on, other than what follows from the above.
Results may differ from a plain program's by a relative error of at most 0.03.
Values may be sent and summed in bfloat16 or wider, within the bound.
A program may use at most 256 MiB of HBM per device.

v0:
```python
import jax
import jax.numpy as jnp
from jax import lax
from jax.sharding import PartitionSpec as P

HD = 64
QMAX = 512
FRAME_TOK = 1024


EPSILON = 1e-06


def layer_norm(values, norm_scale, norm_bias):
    average = jnp.mean(values, axis=-1, keepdims=True)
    centered = values - average
    variance = jnp.mean(centered * centered, axis=-1, keepdims=True)
    return centered * lax.rsqrt(variance + EPSILON) * norm_scale + norm_bias


def exact_gelu(values):
    return jax.nn.gelu(values, approximate=False)


def attend_rows(query_rows, key_rows, value_rows, score_scale):
    scores = (
        jnp.einsum("qhe,khe->hqk", query_rows, key_rows, preferred_element_type=jnp.float32)
        * score_scale
    )
    largest = jnp.max(scores, axis=-1, keepdims=True)
    unnormed = jnp.exp(scores - largest)
    denominator = jnp.sum(unnormed, axis=-1, keepdims=True)
    weights = (unnormed / denominator).astype(jnp.bfloat16)
    mixed = jnp.einsum("hqk,khe->qhe", weights, value_rows, preferred_element_type=jnp.float32)
    return (mixed, (largest + jnp.log(denominator))[:, :, 0])


def attend_back(query_rows, key_rows, value_rows, log_total, grad_rows, score_scale):
    scores = (
        jnp.einsum("qhe,khe->hqk", query_rows, key_rows, preferred_element_type=jnp.float32)
        * score_scale
    )
    probs = jnp.exp(scores - log_total[:, :, None])
    grad_probs = jnp.einsum(
        "qhe,khe->hqk", grad_rows, value_rows, preferred_element_type=jnp.float32
    )
    grad_scores = probs * (grad_probs - jnp.sum(probs * grad_probs, axis=-1, keepdims=True))
    grad_scores = grad_scores.astype(jnp.bfloat16)
    grad_query = (
        jnp.einsum("hqk,khe->qhe", grad_scores, key_rows, preferred_element_type=jnp.float32)
        * score_scale
    )
    grad_key = (
        jnp.einsum("hqk,qhe->khe", grad_scores, query_rows, preferred_element_type=jnp.float32)
        * score_scale
    )
    grad_value = jnp.einsum(
        "hqk,qhe->khe", probs.astype(jnp.bfloat16), grad_rows, preferred_element_type=jnp.float32
    )
    return (grad_query, grad_key, grad_value)


def attention_forward(queries, key_all, value_all, frame_only, score_scale):
    frame_shape = (queries.shape[0] // FRAME_TOK, FRAME_TOK) + queries.shape[1:]
    query_frames = queries.reshape(frame_shape)
    if frame_only:
        mixed, log_total = lax.map(
            lambda triple: attend_rows(triple[0], triple[1], triple[2], score_scale),
            (query_frames, key_all.reshape(frame_shape), value_all.reshape(frame_shape)),
        )
    else:
        mixed, log_total = lax.map(
            lambda query_block: attend_rows(query_block, key_all, value_all, score_scale),
            query_frames,
        )
    return (mixed.reshape(queries.shape), log_total)


def attention_backward(queries, key_all, value_all, log_total, grad_mixed, frame_only, score_scale):
    frame_shape = (queries.shape[0] // FRAME_TOK, FRAME_TOK) + queries.shape[1:]
    query_frames = queries.reshape(frame_shape)
    grad_frames = grad_mixed.reshape(frame_shape)
    if frame_only:
        grad_query, grad_key, grad_value = lax.map(
            lambda group_in: attend_back(
                group_in[0], group_in[1], group_in[2], group_in[3], group_in[4], score_scale
            ),
            (
                query_frames,
                key_all.reshape(frame_shape),
                value_all.reshape(frame_shape),
                log_total,
                grad_frames,
            ),
        )
        return (
            grad_query.reshape(queries.shape),
            grad_key.reshape(queries.shape),
            grad_value.reshape(queries.shape),
        )

    def visit_frame(running, group_in):
        grad_query, grad_key, grad_value = attend_back(
            group_in[0], key_all, value_all, group_in[1], group_in[2], score_scale
        )
        return ((running[0] + grad_key, running[1] + grad_value), grad_query)

    zero_keys = jnp.zeros(key_all.shape, jnp.float32)
    (grad_key, grad_value), grad_query = lax.scan(
        visit_frame, (zero_keys, zero_keys), (query_frames, log_total, grad_frames)
    )
    return (grad_query.reshape(queries.shape), grad_key, grad_value)


def body(
    frames_in,
    qkv_weight,
    qkv_bias,
    out_weight,
    up_weight,
    up_bias,
    down_weight,
    norm_gain,
    norm_offset,
    head_gain,
    head_offset,
    cotangent,
    visible,
    query_count,
):
    score_scale = HD ** (-0.5)

    def backward_block(grad_out, block_index, frame_only, saved):
        (
            hidden,
            gathered,
            split,
            queries,
            key_all,
            value_all,
            log_total,
            mixed_flat,
            branch,
            middle,
            gathered_two,
            hidden_up,
            activated,
            branch_two,
        ) = saved
        gains = norm_gain[block_index]
        offsets = norm_offset[block_index]
        total_rows = split.shape[0]
        grad_branch_two = gains[3] * grad_out
        offset_grad_three = jnp.sum(grad_branch_two, axis=0)
        gain_grad_three = jnp.sum(grad_out * branch_two, axis=0)
        shard_rows = lax.all_gather(grad_branch_two.astype(jnp.bfloat16), "tp", axis=0, tiled=True)
        down_grad = jnp.einsum(
            "tf,td->fd", activated, shard_rows, preferred_element_type=jnp.float32
        )
        act_grad = jnp.einsum(
            "td,fd->tf", shard_rows, down_weight[block_index], preferred_element_type=jnp.float32
        )
        up_grad = jax.vjp(exact_gelu, hidden_up)[1](act_grad)[0].astype(jnp.bfloat16)
        down_grad, up_grads = (down_grad, up_grad)
        up_weight_grad = jnp.einsum(
            "td,tf->df", gathered_two, up_grads, preferred_element_type=jnp.float32
        )
        up_bias_grad = jnp.sum(up_grads.astype(jnp.float32), axis=0)
        second_grad = lax.psum_scatter(
            jnp.einsum(
                "tf,df->td", up_grads, up_weight[block_index], preferred_element_type=jnp.float32
            ).astype(jnp.bfloat16),
            "tp",
            scatter_dimension=0,
            tiled=True,
        ).astype(jnp.float32)
        middle_grad, gain_grad_one, offset_grad_one = jax.vjp(
            layer_norm, middle, gains[1], offsets[1]
        )[1](second_grad)
        middle_grad = middle_grad + grad_out
        grad_branch = gains[2] * middle_grad
        offset_grad_two = jnp.sum(grad_branch, axis=0)
        gain_grad_two = jnp.sum(middle_grad * branch, axis=0)
        shard_rows = lax.all_gather(grad_branch.astype(jnp.bfloat16), "tp", axis=0, tiled=True)
        out_grad = jnp.einsum(
            "tc,td->cd", mixed_flat, shard_rows, preferred_element_type=jnp.float32
        )
        mixed_grad = jnp.einsum(
            "td,cd->tc", shard_rows, out_weight[block_index], preferred_element_type=jnp.float32
        ).astype(jnp.bfloat16)
        out_grad, mixed_grads = (out_grad, mixed_grad)
        grad_query, grad_key, grad_value = attention_backward(
            queries,
            key_all,
            value_all,
            log_total,
            mixed_grads.reshape(queries.shape),
            frame_only,
            score_scale,
        )
        raw_query_grad, query_gain_grad, query_offset_grad = jax.vjp(
            layer_norm, split[:, :, 0], head_gain[block_index, 0], head_offset[block_index, 0]
        )[1](grad_query)
        raw_key_grad, key_gain_grad, key_offset_grad = jax.vjp(
            layer_norm, split[:, :, 1], head_gain[block_index, 1], head_offset[block_index, 1]
        )[1](grad_key)
        projected_grad = (
            jnp.stack([raw_query_grad, raw_key_grad, grad_value], axis=2)
            .reshape(total_rows, -1)
            .astype(jnp.bfloat16)
        )
        qkv_weight_grad = jnp.einsum(
            "td,tc->dc", gathered, projected_grad, preferred_element_type=jnp.float32
        )
        qkv_bias_grad = jnp.sum(projected_grad.astype(jnp.float32), axis=0)
        normed_grad = lax.psum_scatter(
            jnp.einsum(
                "tc,dc->td",
                projected_grad,
                qkv_weight[block_index],
                preferred_element_type=jnp.float32,
            ).astype(jnp.bfloat16),
            "tp",
            scatter_dimension=0,
            tiled=True,
        ).astype(jnp.float32)
        hidden_grad, gain_grad_zero, offset_grad_zero = jax.vjp(
            layer_norm, hidden, gains[0], offsets[0]
        )[1](normed_grad)
        hidden_grad = hidden_grad + middle_grad
        large_grads = (
            qkv_weight_grad,
            qkv_bias_grad,
            out_grad,
            up_weight_grad,
            up_bias_grad,
            down_grad,
        )
        small_grads = (
            jnp.stack([gain_grad_zero, gain_grad_one, gain_grad_two, gain_grad_three]),
            jnp.stack([offset_grad_zero, offset_grad_one, offset_grad_two, offset_grad_three]),
            jnp.stack([query_gain_grad, key_gain_grad]),
            jnp.stack([query_offset_grad, key_offset_grad]),
        )
        return (hidden_grad, large_grads, small_grads)

    hidden = frames_in[0].astype(jnp.float32)
    kept_states = []
    for block_index in range(2):
        forward_frame_only = block_index == 0
        forward_gains = norm_gain[block_index]
        forward_offsets = norm_offset[block_index]
        normed = layer_norm(hidden, forward_gains[0], forward_offsets[0]).astype(jnp.bfloat16)
        forward_gathered = lax.all_gather(normed, "tp", axis=0, tiled=True)
        projected = jnp.dot(
            forward_gathered, qkv_weight[block_index], preferred_element_type=jnp.float32
        )
        projected = projected + qkv_bias[block_index].astype(jnp.float32)
        forward_total_rows = projected.shape[0]
        forward_split = projected.reshape(forward_total_rows, -1, 3, HD)
        forward_queries = layer_norm(
            forward_split[:, :, 0], head_gain[block_index, 0], head_offset[block_index, 0]
        ).astype(jnp.bfloat16)
        forward_key_all = layer_norm(
            forward_split[:, :, 1], head_gain[block_index, 1], head_offset[block_index, 1]
        ).astype(jnp.bfloat16)
        forward_value_all = forward_split[:, :, 2].astype(jnp.bfloat16)
        mixed, forward_log_total = attention_forward(
            forward_queries, forward_key_all, forward_value_all, forward_frame_only, score_scale
        )
        forward_mixed_flat = mixed.reshape(forward_total_rows, -1).astype(jnp.bfloat16)
        forward_branch = (
            lax.psum_scatter(
                jnp.dot(
                    forward_mixed_flat, out_weight[block_index], preferred_element_type=jnp.float32
                ).astype(jnp.bfloat16),
                "tp",
                scatter_dimension=0,
                tiled=True,
            ).astype(jnp.float32)
            + forward_offsets[2]
        )
        forward_middle = hidden + forward_gains[2] * forward_branch
        second = layer_norm(forward_middle, forward_gains[1], forward_offsets[1]).astype(
            jnp.bfloat16
        )
        forward_gathered_two = lax.all_gather(second, "tp", axis=0, tiled=True)
        forward_hidden_up = jnp.dot(
            forward_gathered_two, up_weight[block_index], preferred_element_type=jnp.float32
        )
        forward_hidden_up = forward_hidden_up + up_bias[block_index].astype(jnp.float32)
        forward_activated = exact_gelu(forward_hidden_up).astype(jnp.bfloat16)
        forward_branch_two = (
            lax.psum_scatter(
                jnp.dot(
                    forward_activated, down_weight[block_index], preferred_element_type=jnp.float32
                ).astype(jnp.bfloat16),
                "tp",
                scatter_dimension=0,
                tiled=True,
            ).astype(jnp.float32)
            + forward_offsets[3]
        )
        result = forward_middle + forward_gains[3] * forward_branch_two
        forward_saved = (
            hidden,
            forward_gathered,
            forward_split,
            forward_queries,
            forward_key_all,
            forward_value_all,
            forward_log_total,
            forward_mixed_flat,
            forward_branch,
            forward_middle,
            forward_gathered_two,
            forward_hidden_up,
            forward_activated,
            forward_branch_two,
        )
        hidden = result
        saved = forward_saved
        kept_states.append(saved)
    layer_out = hidden.astype(jnp.bfloat16)[None]
    grad_hidden = (
        cotangent[0].astype(jnp.float32)
        * visible[0].astype(jnp.float32)[:, None]
        * (query_count[0].astype(jnp.float32) / QMAX)
    )
    grad_hidden, large_one, small_one = backward_block(grad_hidden, 1, False, kept_states[1])
    grad_hidden, large_zero, small_zero = backward_block(grad_hidden, 0, True, kept_states[0])
    input_grad = grad_hidden.astype(jnp.bfloat16)[None]

    def stack_pair(first, later):
        return jnp.stack([first, later])

    qkv_w_part, qkv_b_part, out_w_part, up_w_part, up_b_part, down_w_part = jax.tree.map(
        stack_pair, large_zero, large_one
    )
    gain_part, offset_part, head_gain_part, head_offset_part = jax.tree.map(
        stack_pair, small_zero, small_one
    )
    summed = (
        lax.psum(qkv_w_part.astype(jnp.bfloat16), "scene").astype(jnp.float32),
        lax.psum(qkv_b_part.astype(jnp.bfloat16), "scene").astype(jnp.float32),
        lax.psum(out_w_part.astype(jnp.bfloat16), "scene").astype(jnp.float32),
        lax.psum(up_w_part.astype(jnp.bfloat16), "scene").astype(jnp.float32),
        lax.psum(up_b_part.astype(jnp.bfloat16), "scene").astype(jnp.float32),
        lax.psum(down_w_part.astype(jnp.bfloat16), "scene").astype(jnp.float32),
    )
    summed = tuple(summed) + tuple(
        lax.psum((gain_part, offset_part, head_gain_part, head_offset_part), ("scene", "tp"))
    )
    return (
        layer_out,
        input_grad,
        summed[0],
        summed[1],
        summed[2],
        summed[3],
        summed[4],
        summed[5],
        summed[6],
        summed[7],
        summed[8],
        summed[9],
    )


def solution(mesh):
    return jax.shard_map(
        body,
        mesh=mesh,
        in_specs=(
            P("scene", "tp", None),
            P(None, None, "tp"),
            P(None, "tp"),
            P(None, "tp", None),
            P(None, None, "tp"),
            P(None, "tp"),
            P(None, "tp", None),
            P(),
            P(),
            P(),
            P(),
            P("scene", "tp", None),
            P("scene", "tp"),
            P("scene"),
        ),
        out_specs=(
            P("scene", "tp", None),
            P("scene", "tp", None),
            P(None, None, "tp"),
            P(None, "tp"),
            P(None, "tp", None),
            P(None, None, "tp"),
            P(None, "tp"),
            P(None, "tp", None),
            P(),
            P(),
            P(),
            P(),
        ),
        check_vma=False,
    )
```

profile of v0, /device:TPU:0, one launch (start us, length us, event | category | flops | bytes accessed | tf_op | source)
XLA Modules:
  0.0 1921.5 jit_solution(9734424653389365406)
XLA Ops:
  18.0 73.9 %all-gather.9.cloned.1.call-done = bf16[2048,1024]{1,0:T(8,128)(2,1)} async-done(((bf16[256,1024]{1,0:T(8,128)(2,1)}), bf16[2048,1024]{1,0:T(8,128)(2,1)}) %all-gather.9.cloned.1.call-update) | async-done | bytes 4194320 | tf_op jit(solution)/shard_map/all_gather | solution.py:254
  106.2 10.9 while.53
  123.4 86.3 %reduce-scatter.9.cloned.1.call-done = bf16[256,1024]{1,0:T(8,128)(2,1)} async-done(((bf16[2048,1024]{1,0:T(8,128)(2,1)}), bf16[256,1024]{1,0:T(8,128)(2,1)}) %reduce-scatter.9.cloned.1.call-update) | async-done | bytes 524304 | tf_op jit(solution)/shard_map/reduce_scatter | solution.py:273
  215.3 72.6 %all-gather.11.cloned.1.call-done = bf16[2048,1024]{1,0:T(8,128)(2,1)} async-done(((bf16[256,1024]{1,0:T(8,128)(2,1)}), bf16[2048,1024]{1,0:T(8,128)(2,1)}) %all-gather.11.cloned.1.call-update) | async-done | bytes 4194320 | tf_op jit(solution)/shard_map/all_gather | solution.py:287
  288.0 15.1 multiply_convert_fusion.3
  308.8 86.3 %reduce-scatter.11.cloned.1.call-done = bf16[256,1024]{1,0:T(8,128)(2,1)} async-done(((bf16[2048,1024]{1,0:T(8,128)(2,1)}), bf16[256,1024]{1,0:T(8,128)(2,1)}) %reduce-scatter.11.cloned.1.call-update) | async-done | bytes 524304 | tf_op jit(solution)/shard_map/reduce_scatter | solution.py:294
  398.7 73.3 %all-gather.13.cloned.1.call-done = bf16[2048,1024]{1,0:T(8,128)(2,1)} async-done(((bf16[256,1024]{1,0:T(8,128)(2,1)}), bf16[2048,1024]{1,0:T(8,128)(2,1)}) %all-gather.13.cloned.1.call-update) | async-done | bytes 4194320 | tf_op jit(solution)/shard_map/all_gather | solution.py:254
  483.3 20.8 %while.54 = (s32[]{:T(128)}, bf16[2,1024,2,64]{1,3,2,0:T(8,128)(2,1)S(1)}, f32[2,2,1024]{2,1,0:T(2,128)S(1)}, bf16[2,1024,2,64]{1,3,2,0:T(8,128)(2,1)S(1)}, bf16...) while((s32[]{:T(128)}, bf16[2,1024,2,64]{1,3,2,0:T(8,128)(2,1)S(1)}, ...), condition=%wide.region_23.24_spmd, body=%wide.region_20.23_spmd.sunk | while | flops 1111488512 | bytes 52232288 | solution.py:72
  509.4 86.2 %reduce-scatter.13.cloned.1.call-done = bf16[256,1024]{1,0:T(8,128)(2,1)} async-done(((bf16[2048,1024]{1,0:T(8,128)(2,1)}), bf16[256,1024]{1,0:T(8,128)(2,1)}) %reduce-scatter.13.cloned.1.call-update) | async-done | bytes 524304 | tf_op jit(solution)/shard_map/reduce_scatter | solution.py:273
  601.1 70.6 %all-gather.15.cloned.1.call-done = bf16[2048,1024]{1,0:T(8,128)(2,1)} async-done(((bf16[256,1024]{1,0:T(8,128)(2,1)}), bf16[2048,1024]{1,0:T(8,128)(2,1)}) %all-gather.15.cloned.1.call-update) | async-done | bytes 4194320 | tf_op jit(solution)/shard_map/all_gather | solution.py:287
  671.7 14.9 multiply_convert_fusion.2
  686.6 59.7 %all-gather.17.cloned.1.call-done = bf16[2048,1024]{1,0:T(8,128)(2,1)} async-done(((bf16[256,1024]{1,0:T(8,128)(2,1)}), bf16[2048,1024]{1,0:T(8,128)(2,1)}) %all-gather.17.cloned.1.call-update) | async-done | bytes 4194320 | tf_op jit(solution)/shard_map/all_gather | solution.py:156
  768.5 79.6 %reduce-scatter.17.cloned.1.call-done = bf16[256,1024]{1,0:T(8,128)(2,1)} async-done(((bf16[2048,1024]{1,0:T(8,128)(2,1)}), bf16[256,1024]{1,0:T(8,128)(2,1)}) %reduce-scatter.17.cloned.1.call-update) | async-done | bytes 524304 | tf_op jit(solution)/shard_map/reduce_scatter | solution.py:169
  852.3 87.1 %reduce-scatter.15.cloned.1.call-done = bf16[256,1024]{1,0:T(8,128)(2,1)} async-done(((bf16[2048,1024]{1,0:T(8,128)(2,1)}), bf16[256,1024]{1,0:T(8,128)(2,1)}) %reduce-scatter.15.cloned.1.call-update) | async-done | bytes 524304 | tf_op jit(solution)/shard_map/reduce_scatter | solution.py:294
  945.0 73.2 %all-gather.19.cloned.1.call-done = bf16[2048,1024]{1,0:T(8,128)(2,1)} async-done(((bf16[256,1024]{1,0:T(8,128)(2,1)}), bf16[2048,1024]{1,0:T(8,128)(2,1)}) %all-gather.19.cloned.1.call-update) | async-done | bytes 4194320 | tf_op jit(solution)/shard_map/all_gather | solution.py:184
  1030.3 69.8 %while.56 = (s32[]{:T(128)}, f32[2048,2,64]{0,2,1:T(8,128)S(1)}, f32[2048,2,64]{0,2,1:T(8,128)S(1)}, f32[2,1024,2,64]{1,3,2,0:T(8,128)}, bf16[2,1024,2,64]{1,3,2...) while((s32[]{:T(128)}, f32[2048,2,64]{0,2,1:T(8,128)S(1)}, ...), condition=%wide.region_33.34_spmd.clone, body=%wide.region_31.33_spmd.clone.sunk | while | flops 2736125952 | bytes 179364144 | solution.py:109
  1123.1 86.3 %reduce-scatter.19.cloned.1.call-done = bf16[256,1024]{1,0:T(8,128)(2,1)} async-done(((bf16[2048,1024]{1,0:T(8,128)(2,1)}), bf16[256,1024]{1,0:T(8,128)(2,1)}) %reduce-scatter.19.cloned.1.call-update) | async-done | bytes 524304 | tf_op jit(solution)/shard_map/reduce_scatter | solution.py:216
  1217.2 73.1 %all-gather.21.cloned.1.call-done = bf16[2048,1024]{1,0:T(8,128)(2,1)} async-done(((bf16[256,1024]{1,0:T(8,128)(2,1)}), bf16[2048,1024]{1,0:T(8,128)(2,1)}) %all-gather.21.cloned.1.call-update) | async-done | bytes 4194320 | tf_op jit(solution)/shard_map/all_gather | solution.py:156
  1305.8 86.3 %reduce-scatter.21.cloned.1.call-done = bf16[256,1024]{1,0:T(8,128)(2,1)} async-done(((bf16[2048,1024]{1,0:T(8,128)(2,1)}), bf16[256,1024]{1,0:T(8,128)(2,1)}) %reduce-scatter.21.cloned.1.call-update) | async-done | bytes 524304 | tf_op jit(solution)/shard_map/reduce_scatter | solution.py:169
  1421.8 51.8 %all-gather.23.cloned.1.call-done = bf16[2048,1024]{1,0:T(8,128)(2,1)} async-done(((bf16[256,1024]{1,0:T(8,128)(2,1)}), bf16[2048,1024]{1,0:T(8,128)(2,1)}) %all-gather.23.cloned.1.call-update) | async-done | bytes 4194320 | tf_op jit(solution)/shard_map/all_gather | solution.py:184
  1483.5 52.4 %while.55 = (s32[]{:T(128)}, f32[2,1024,2,64]{1,3,2,0:T(8,128)}, f32[2,1024,2,64]{1,3,2,0:T(8,128)}, bf16[2,1024,2,64]{1,0,3,2:T(2,128)(2,1)}, bf16[2,1024,2,64]...) while((s32[]{:T(128)}, f32[2,1024,2,64]{1,3,2,0:T(8,128)}, ...), condition=%wide.region_46.47_spmd, body=%wide.region_44.46_spmd.sunk | while | flops 1367603200 | bytes 155251056 | solution.py:84
  1590.8 100.9 %all-reduce.8.cloned.1.call-done = (bf16[2,1024,384]{2,1,0:T(8,128)(2,1)}, bf16[2,128,1024]{2,1,0:T(8,128)(2,1)}, bf16[2,1024,512]{2,1,0:T(8,128)(2,1)}, bf16[2,512,1024]{2,1,0:T(8,128)(2,1)}) async-done(((bf16[2,1024,384]{2,1,0:T(8,128)(2,1)}, bf16[2,128,1024]{2,1,0:T(8,128)(2,1)}, bf16[2,1024,512]{2,1,0:T(8,128)(2,1)}, bf16[2,512,1024]{2,1,0:T(8,128)(2,1)}), (bf16[2,1024,384]{2,1,0:T(8,128)(2,1)}, ...) | async-done | bytes 6291472 | tf_op jit(solution)/shard_map/psum | solution.py:344
  1702.3 81.3 %reduce-scatter.23.cloned.1.call-done = bf16[256,1024]{1,0:T(8,128)(2,1)} async-done(((bf16[2048,1024]{1,0:T(8,128)(2,1)}), bf16[256,1024]{1,0:T(8,128)(2,1)}) %reduce-scatter.23.cloned.1.call-update) | async-done | bytes 524304 | tf_op jit(solution)/shard_map/reduce_scatter | solution.py:216
  1790.4 118.7 %all-reduce.6.cloned.1.call-done = (f32[2,4,1024]{2,1,0:T(4,128)}, f32[2,4,1024]{2,1,0:T(4,128)}, f32[2,2,64]{2,1,0:T(2,128)}, f32[2,2,64]{2,1,0:T(2,128)}) async-done(((f32[2,4,1024]{2,1,0:T(4,128)}, f32[2,4,1024]{2,1,0:T(4,128)}, f32[2,2,64]{2,1,0:T(2,128)}, f32[2,2,64]{2,1,0:T(2,128)}), (f32[2,4,1024]{2,1,0:T(4,128)}, f32[2,4,1024]{2,1,0:T(4,128)}, f32[2,2,64]{2,1,0:T(2,128)}, ...) | async-done | bytes 67600 | tf_op jit(solution)/shard_map/psum | solution.py:352
  (703 shorter events, 425.8 us)
Async XLA Ops:
  7.2 84.7 %all-gather.9.cloned.1.call-start = ((), (), s32[]{:S(2)}) async-start(), calls=%async_computation.8 | async-start | bytes 4718592 | tf_op jit(solution)/shard_map/all_gather | solution.py:254
  12.0 200.4 %copy-start.105 = (f32[1,1,1024]{2,1,0:T(1,128)}, f32[1,1,1024]{2,1,0:T(1,128)S(1)}, u32[]{:S(2)}) copy-start(f32[1,1,1024]{2,1,0:T(1,128)S(1)} %get-tuple-element.468) | copy-start | bytes 12292
  12.0 383.1 %copy-start.69 = (f32[1,1,1024]{2,1,0:T(1,128)}, f32[1,1,1024]{2,1,0:T(1,128)S(1)}, u32[]{:S(2)}) copy-start(f32[1,1,1024]{2,1,0:T(1,128)S(1)} %get-tuple-element.471) | copy-start | bytes 12292
  12.0 383.1 %copy-start.112 = (f32[1,1,1024]{2,1,0:T(1,128)}, f32[1,1,1024]{2,1,0:T(1,128)S(1)}, u32[]{:S(2)}) copy-start(f32[1,1,1024]{2,1,0:T(1,128)S(1)} %get-tuple-element.469) | copy-start | bytes 12292
  12.0 384.9 %copy-start.107 = (f32[1,1,1024]{2,1,0:T(1,128)}, f32[1,1,1024]{2,1,0:T(1,128)S(1)}, u32[]{:S(2)}) copy-start(f32[1,1,1024]{2,1,0:T(1,128)S(1)} %get-tuple-element.466) | copy-start | bytes 12292
  13.6 381.5 %copy-start.71 = (f32[1,1,1024]{2,1,0:T(1,128)}, f32[1,1,1024]{2,1,0:T(1,128)S(1)}, u32[]{:S(2)}) copy-start(f32[1,1,1024]{2,1,0:T(1,128)S(1)} %get-tuple-element.478) | copy-start | bytes 12292
  13.6 381.5 %copy-start.119 = (f32[1,1,1024]{2,1,0:T(1,128)}, f32[1,1,1024]{2,1,0:T(1,128)S(1)}, u32[]{:S(2)}) copy-start(f32[1,1,1024]{2,1,0:T(1,128)S(1)} %get-tuple-element.476) | copy-start | bytes 12292
  15.7 193.9 %reduce-scatter.9.cloned.1.call-start = ((), (), s32[]{:S(2)}) async-start(), calls=%async_computation.9 | async-start | bytes 4718592 | tf_op jit(solution)/shard_map/reduce_scatter | solution.py:273
  123.4 164.6 %all-gather.11.cloned.1.call-start = ((), (), s32[]{:S(2)}) async-start(), calls=%async_computation.10 | async-start | bytes 4718592 | tf_op jit(solution)/shard_map/all_gather | solution.py:287
  214.7 180.4 %reduce-scatter.11.cloned.1.call-start = ((), (), s32[]{:S(2)}) async-start(), calls=%async_computation.11 | async-start | bytes 4718592 | tf_op jit(solution)/shard_map/reduce_scatter | solution.py:294
  308.8 163.2 %all-gather.13.cloned.1.call-start = ((), (), s32[]{:S(2)}) async-start(), calls=%async_computation.12 | async-start | bytes 4718592 | tf_op jit(solution)/shard_map/all_gather | solution.py:254
  398.6 197.0 %reduce-scatter.13.cloned.1.call-start = ((), (), s32[]{:S(2)}) async-start(), calls=%async_computation.13 | async-start | bytes 4718592 | tf_op jit(solution)/shard_map/reduce_scatter | solution.py:273
  509.3 162.4 %all-gather.15.cloned.1.call-start = ((), (), s32[]{:S(2)}) async-start(), calls=%async_computation.14 | async-start | bytes 4718592 | tf_op jit(solution)/shard_map/all_gather | solution.py:287
  598.3 148.1 %all-gather.17.cloned.1.call-start = ((), (), s32[]{:S(2)}) async-start(), calls=%async_computation.16 | async-start | bytes 4718592 | tf_op jit(solution)/shard_map/all_gather | solution.py:156
  601.1 247.0 %reduce-scatter.17.cloned.1.call-start = ((), (), s32[]{:S(2)}) async-start(), calls=%async_computation.17 | async-start | bytes 4718592 | tf_op jit(solution)/shard_map/reduce_scatter | solution.py:169
  761.8 177.7 %reduce-scatter.15.cloned.1.call-start = ((), (), s32[]{:S(2)}) async-start(), calls=%async_computation.15 | async-start | bytes 4718592 | tf_op jit(solution)/shard_map/reduce_scatter | solution.py:294
  768.1 250.2 %all-gather.19.cloned.1.call-start = ((), (), s32[]{:S(2)}) async-start(), calls=%async_computation.18 | async-start | bytes 4718592 | tf_op jit(solution)/shard_map/all_gather | solution.py:184
  945.0 264.4 %reduce-scatter.19.cloned.1.call-start = ((), (), s32[]{:S(2)}) async-start(), calls=%async_computation.19 | async-start | bytes 4718592 | tf_op jit(solution)/shard_map/reduce_scatter | solution.py:216
  1123.0 167.2 %all-gather.21.cloned.1.call-start = ((), (), s32[]{:S(2)}) async-start(), calls=%async_computation.20 | async-start | bytes 4718592 | tf_op jit(solution)/shard_map/all_gather | solution.py:156
  1216.9 175.2 %reduce-scatter.21.cloned.1.call-start = ((), (), s32[]{:S(2)}) async-start(), calls=%async_computation.21 | async-start | bytes 4718592 | tf_op jit(solution)/shard_map/reduce_scatter | solution.py:169
  1305.7 167.8 %all-gather.23.cloned.1.call-start = ((), (), s32[]{:S(2)}) async-start(), calls=%async_computation.22 | async-start | bytes 4718592 | tf_op jit(solution)/shard_map/all_gather | solution.py:184
  1400.2 291.4 %all-reduce.8.cloned.1.call-start = ((), (), s32[]{:S(2)}) async-start(), calls=%async_computation.25 | async-start | bytes 12582912 | tf_op jit(solution)/shard_map/psum | solution.py:344
  1572.9 210.7 %reduce-scatter.23.cloned.1.call-start = ((), (), s32[]{:S(2)}) async-start(), calls=%async_computation.23 | async-start | bytes 4718592 | tf_op jit(solution)/shard_map/reduce_scatter | solution.py:216
  1578.9 330.2 %all-reduce.6.cloned.1.call-start = ((), (), s32[]{:S(2)}) async-start(), calls=%async_computation.24 | async-start | bytes 139264 | tf_op jit(solution)/shard_map/psum | solution.py:352
  (199 other events, 5765.5 us)
Sparse Core Ops, SparseCore 0:
  15.8 76.0 all-gather.8
  123.5 86.1 reduce-scatter.8
  214.8 73.1 all-gather.10
  308.9 86.1 reduce-scatter.10
  398.8 73.1 all-gather.12
  509.4 86.1 reduce-scatter.12
  598.5 73.1 all-gather.14
  674.6 71.6 all-gather.16
  761.9 86.1 reduce-scatter.16
  851.6 87.7 reduce-scatter.14
  945.1 73.1 all-gather.18
  1123.1 86.1 reduce-scatter.18
  1217.0 73.1 all-gather.20
  1305.8 86.1 reduce-scatter.20
  1400.4 73.1 all-gather.22
  1573.0 118.5 all-reduce.7
  1695.5 88.0 reduce-scatter.22
  1790.2 118.8 all-reduce.5
where the time goes:
time: 1930 us; the launch traced here: 1920 us
  waiting for transfers between devices  1450 us (75%)
  matrix products  209 us (11%)
  other arithmetic  138 us (7%)
  local copies, waits for them, and re-layouts  99.9 us (5%)
    reduce_scatter x2, waiting for transfers between devices, body(): lax.psum_scatter(jnp.dot(forward_activated, down_weight[block_index], pre...  173 us
    reduce_scatter x2, waiting for transfers between devices, body(): lax.psum_scatter(jnp.dot(forward_mixed_flat, out_weight[block_index], pre...  172 us
    reduce_scatter x2, waiting for transfers between devices, backward_block(): lax.psum_scatter(jnp.einsum('tc,dc->td', projected_grad, qkv_weight[block...  168 us
    reduce_scatter x2, waiting for transfers between devices, backward_block(): lax.psum_scatter(jnp.einsum('tf,df->td', up_grads, up_weight[block_index]...  166 us
    all_gather x2, waiting for transfers between devices, body(): forward_gathered = lax.all_gather(normed, 'tp', axis=0, tiled=True)  147 us
    all_gather x2, waiting for transfers between devices, body(): forward_gathered_two = lax.all_gather(second, 'tp', axis=0, tiled=True)  143 us
    all_gather x2, waiting for transfers between devices, backward_block(): lax.all_gather(grad_branch_two.astype(jnp.bfloat16), 'tp', axis=0, tiled=...  133 us
    all_gather x2, waiting for transfers between devices, backward_block(): lax.all_gather(grad_branch.astype(jnp.bfloat16), 'tp', axis=0, tiled=True)  125 us
  transfers between devices with their start and end apart: 18, of which 18 were waited for; matrix products, arithmetic and copies ran while one was open for 4% of the time, Pallas kernels for 0%

commit v1 on v0

--- a/solution.py
+++ b/solution.py
@@ -1,14 +1,923 @@
+import functools
+
 import jax
 import jax.numpy as jnp
 from jax import lax
+from jax.experimental import pallas as pl
+from jax.experimental.pallas import tpu as pltpu
 from jax.sharding import PartitionSpec as P
 
 HD = 64
 QMAX = 512
 FRAME_TOK = 1024
-
-
 EPSILON = 1e-06
+BF = jnp.bfloat16
+F32 = jnp.float32
+MESH = pl.DeviceIdType.MESH
+VMEM_LIMIT = 60 * 1024 * 1024
+
+AXES = ("sy", "c", "h", "zl", "x")
+
+
+def dot(left, right):
+    return lax.dot_general(left, right, (((1,), (0,)), ((), ())), preferred_element_type=F32)
+
+
+def dot_rt(left, right):
+    return lax.dot_general(left, right, (((1,), (1,)), ((), ())), preferred_element_type=F32)
+
+
+def dot_lt(left, right):
+    return lax.dot_general(left, right, (((0,), (0,)), ((), ())), preferred_element_type=F32)
+
+
+def dot_exact(left, right):
+    return lax.dot_general(
+        left, right, (((1,), (0,)), ((), ())), precision=lax.Precision.HIGHEST, preferred_element_type=F32
+    )
+
+
+def remote(source, target, send, recv, device):
+    return pltpu.make_async_remote_copy(
+        src_ref=source, dst_ref=target, send_sem=send, recv_sem=recv, device_id=device, device_id_type=MESH
+    )
+
+
+class Spot:
+    def __init__(self):
+        self.c = lax.axis_index("c")
+        self.zl = lax.axis_index("zl")
+        self.x = lax.axis_index("x")
+        self.over_x = {"x": 1 - self.x}
+        self.over_z = {"zl": 1 - self.zl}
+        self.core = {"c": 1 - self.c}
+
+    def greet(self):
+        barrier = pltpu.get_barrier_semaphore()
+        for device in (self.over_x, self.over_z, self.core):
+            pl.semaphore_signal(barrier, inc=1, device_id=device, device_id_type=MESH)
+        pl.semaphore_wait(barrier, 3)
+
+    def slot(self, core, step):
+        zl = lax.rem(self.zl + step // 2, 2)
+        x = lax.rem(self.x + step % 2, 2)
+        return core * 4 + zl * 2 + x
+
+
+class Gather:
+    @staticmethod
+    def scratch(rows, width):
+        dma = pltpu.SemaphoreType.DMA
+        return [pltpu.VMEM((8, rows, width), BF), dma((6,)), dma((6,)), dma((4,)), dma((4,))]
+
+    def __init__(self, spot, refs):
+        self.spot = spot
+        self.held, send, recv, self.core_send, self.core_recv = refs
+        half = self.held.shape[1] // 2
+        self.half = half
+
+        def copy(step, part, number, device):
+            ref = self.held.at[spot.slot(spot.c, step), pl.ds(part * half, half)]
+            return remote(ref, ref, send.at[number], recv.at[number], device)
+
+        self.x_first = copy(0, 0, 0, spot.over_x)
+        self.x_later = copy(0, 1, 1, spot.over_x)
+        self.z_later = copy(0, 0, 2, spot.over_z)
+        self.z_first = copy(0, 1, 3, spot.over_z)
+        self.z_relay = copy(1, 0, 4, spot.over_z)
+        self.x_relay = copy(2, 1, 5, spot.over_x)
+
+    def core_copy(self, step):
+        ref = self.held.at[self.spot.slot(self.spot.c, step)]
+        return remote(ref, ref, self.core_send.at[step], self.core_recv.at[step], self.spot.core)
+
+    def put(self, part, values):
+        self.held[self.spot.slot(self.spot.c, 0), pl.ds(part * self.half, self.half)] = values
+        if part == 0:
+            self.x_first.start()
+            self.z_later.start()
+        else:
+            self.z_first.start()
+            self.x_later.start()
+
+    def arrive(self, step):
+        @pl.when(step == 1)
+        def _():
+            self.x_first.wait_recv()
+            self.z_relay.start()
+            self.z_first.wait_recv()
+            self.x_relay.start()
+            self.x_later.wait_recv()
+
+        @pl.when(step == 2)
+        def _():
+            self.z_later.wait_recv()
+
+        @pl.when(step == 3)
+        def _():
+            self.z_relay.wait_recv()
+            self.x_relay.wait_recv()
+
+        self.core_copy(step).start()
+
+    def arrive_core(self, step):
+        self.core_copy(step).wait_recv()
+
+    def finish(self):
+        for copy in (self.x_first, self.x_later, self.z_first, self.z_later, self.z_relay, self.x_relay):
+            copy.wait_send()
+        for step in range(4):
+            self.core_copy(step).wait_send()
+
+
+class Scatter:
+    @staticmethod
+    def local(rows, width):
+        half = rows // 2
+        return [
+            pltpu.VMEM((4, rows, width), BF),
+            pltpu.VMEM((4, rows, width), BF),
+            pltpu.VMEM((4, rows, width), F32),
+            pltpu.VMEM((2, half, width), BF),
+        ]
+
+    @staticmethod
+    def scratch(rows, width):
+        dma = pltpu.SemaphoreType.DMA
+        half = rows // 2
+        return [
+            pltpu.VMEM((4, rows, width), BF),
+            pltpu.VMEM((6, half, width), BF),
+            dma((4,)),
+            dma((4,)),
+            dma((6,)),
+            dma((6,)),
+        ]
+
+    def __init__(self, spot, local, refs):
+        self.spot = spot
+        self.for_core, self.ready, self.sums, self.relayed = local
+        self.from_core, self.landed, self.core_send, self.core_recv, send, recv = refs
+        half = self.for_core.shape[1] // 2
+        self.half = half
+        first, later = pl.ds(0, half), pl.ds(half, half)
+
+        def copy(source, number, device):
+            return remote(source, self.landed.at[number], send.at[number], recv.at[number], device)
+
+        self.x_near = copy(self.ready.at[1, first], 0, spot.over_x)
+        self.x_far = copy(self.ready.at[3, first], 1, spot.over_x)
+        self.z_near = copy(self.ready.at[2, later], 2, spot.over_z)
+        self.z_far = copy(self.ready.at[3, later], 3, spot.over_z)
+        self.z_relay = copy(self.relayed.at[0], 4, spot.over_z)
+        self.x_relay = copy(self.relayed.at[1], 5, spot.over_x)
+
+    def core_copy(self, step):
+        return remote(
+            self.for_core.at[step],
+            self.from_core.at[step],
+            self.core_send.at[step],
+            self.core_recv.at[step],
+            self.spot.core,
+        )
+
+    def put_other(self, step, values):
+        self.for_core[step] = values.astype(BF)
+        self.core_copy(step).start()
+
+    def put_own(self, step, values):
+        self.sums[step] = values
+
+    def flush(self, step):
+        self.core_copy(step).wait_recv()
+        total = self.sums[step] + self.from_core[step].astype(F32)
+        self.sums[step] = total
+        self.ready[step] = total.astype(BF)
+
+        @pl.when(step == 1)
+        def _():
+            self.x_near.start()
+
+        @pl.when(step == 2)
+        def _():
+            self.z_near.start()
+
+        @pl.when(step == 3)
+        def _():
+            self.x_far.start()
+            self.z_far.start()
+
+    def relay(self):
+        half = self.half
+        self.x_far.wait_recv()
+        self.relayed[0] = (self.sums[2, pl.ds(0, half)] + self.landed[1].astype(F32)).astype(BF)
+        self.z_relay.start()
+        self.z_far.wait_recv()
+        self.relayed[1] = (self.sums[1, pl.ds(half, half)] + self.landed[3].astype(F32)).astype(BF)
+        self.x_relay.start()
+
+    def result(self, part):
+        near, last = (self.x_near, self.z_relay) if part == 0 else (self.z_near, self.x_relay)
+        near.wait_recv()
+        last.wait_recv()
+        near_at, last_at = (0, 4) if part == 0 else (2, 5)
+        return (
+            self.sums[0, pl.ds(part * self.half, self.half)]
+            + self.landed[near_at].astype(F32)
+            + self.landed[last_at].astype(F32)
+        )
+
+    def finish(self):
+        for copy in (self.x_near, self.x_far, self.z_near, self.z_far, self.z_relay, self.x_relay):
+            copy.wait_send()
+        for step in range(4):
+            self.core_copy(step).wait_send()
+
+    def produce(self, term):
+        def visit(index, carry):
+            step = 3 - index
+            self.put_other(step, term(self.spot.slot(1 - self.spot.c, step)))
+            self.put_own(step, term(self.spot.slot(self.spot.c, step)))
+            self.flush(step)
+            return carry
+
+        lax.fori_loop(0, 4, visit, 0)
+
+
+def norm_parts(values):
+    average = jnp.mean(values, axis=-1, keepdims=True)
+    centered = values - average
+    scale = lax.rsqrt(jnp.mean(centered * centered, axis=-1, keepdims=True) + EPSILON)
+    return centered * scale, scale
+
+
+def norm_back(grad, gain, normed, scale):
+    scaled = grad * gain
+    back = scale * (
+        scaled
+        - jnp.mean(scaled, axis=-1, keepdims=True)
+        - normed * jnp.mean(scaled * normed, axis=-1, keepdims=True)
+    )
+    return back, jnp.sum(grad * normed, axis=0, keepdims=True), jnp.sum(grad, axis=0, keepdims=True)
+
+
+def gelu_both(values):
+    size = jnp.abs(values) * 0.7071067811865476
+    bell = jnp.exp(-size * size)
+    t = 1.0 / (1.0 + 0.3275911 * size)
+    poly = t * (
+        0.254829592 + t * (-0.284496736 + t * (1.421413741 + t * (-1.453152027 + t * 1.061405429)))
+    )
+    tail = 0.5 * poly * bell
+    below = jnp.where(values < 0, tail, 1.0 - tail)
+    return values * below, below + values * bell * 0.3989422804014327
+
+
+def lanes_of_head(shape, head):
+    lane = lax.broadcasted_iota(jnp.int32, shape, 1)
+    return (lane < HD) if head == 0 else (lane >= HD)
+
+
+def averager(width):
+    row = lax.broadcasted_iota(jnp.int32, (width, width), 0) // HD
+    column = lax.broadcasted_iota(jnp.int32, (width, width), 1) // HD
+    return jnp.where(row == column, 1.0 / HD, 0.0).astype(F32)
+
+
+def project(rows, weight, bias, head_gain, head_offset, raw_ref, qk_ref, v_ref, slot):
+    projected = dot(rows, weight[...]) + bias[...]
+    raw = projected[:, : 4 * HD]
+    raw_ref[slot] = raw
+    average = averager(4 * HD)
+    centered = raw - dot_exact(raw, average)
+    scale = lax.rsqrt(dot_exact(centered * centered, average) + EPSILON)
+    qk_ref[slot] = (centered * scale * head_gain[...] + head_offset[...]).astype(BF)
+    v_ref[slot] = projected[:, 4 * HD :].astype(BF)
+
+
+def first_kernel(
+    frames, gains, offsets, weight, bias, head_gain, head_offset, gathered_out, raw_out, qk_out, v_out, *scratch
+):
+    spot = Spot()
+    spot.greet()
+    gather = Gather(spot, scratch[:5])
+    saved = scratch[5]
+    half = gather.half
+    for part in range(2):
+        rows = frames[pl.ds(part * half, half)].astype(F32)
+        gather.put(part, (norm_parts(rows)[0] * gains[0:1] + offsets[0:1]).astype(BF))
+
+    def use(slot):
+        project(gather.held[slot], weight, bias, head_gain, head_offset, raw_out, qk_out, v_out, slot)
+
+    def visit(step, carry):
+        gather.arrive(step)
+        use(spot.slot(spot.c, step))
+        gather.arrive_core(step)
+        use(spot.slot(1 - spot.c, step))
+        return carry
+
+    lax.fori_loop(0, 4, visit, 0)
+    copy = pltpu.make_async_copy(gather.held, gathered_out, saved)
+    copy.start()
+    gather.finish()
+    copy.wait()
+
+
+def forward_kernel(is_last, *refs):
+    (mixed, hidden, out_weight, up_weight, up_bias, down_weight, gains, offsets) = refs[:8]
+    refs = refs[8:]
+    if not is_last:
+        (next_gains, next_offsets, weight, bias, head_gain, head_offset) = refs[:6]
+        refs = refs[6:]
+    (branch_out, middle_out, second_out, activated_out, slope_out, branch_two_out, state_out) = refs[:7]
+    refs = refs[7:]
+    if not is_last:
+        (gathered_out, raw_out, qk_out, v_out) = refs[:4]
+        refs = refs[4:]
+    local, one, two, held, saved = refs[:4], refs[4:10], refs[10:16], refs[16:21], refs[21]
+    spot = Spot()
+    spot.greet()
+    first, gather, later = Scatter(spot, local, one), Gather(spot, held), Scatter(spot, local, two)
+    half = gather.half
+    first.produce(lambda slot: dot(mixed[slot], out_weight[...]))
+    first.relay()
+    for part in range(2):
+        rows = pl.ds(part * half, half)
+        branch = first.result(part) + offsets[2:3]
+        middle = hidden[rows].astype(F32) + gains[2:3] * branch
+        branch_out[rows] = branch
+        middle_out[rows] = middle
+        gather.put(part, (norm_parts(middle)[0] * gains[1:2] + offsets[1:2]).astype(BF))
+    first.finish()
+
+    def term(slot):
+        activated, slope = gelu_both(dot(gather.held[slot], up_weight[...]) + up_bias[...])
+        activated = activated.astype(BF)
+        activated_out[slot] = activated
+        slope_out[slot] = slope.astype(BF)
+        return dot(activated, down_weight[...])
+
+    def visit(step, carry):
+        gather.arrive(step)
+        later.put_own(step, term(spot.slot(spot.c, step)))
+        gather.arrive_core(step)
+        later.put_other(step, term(spot.slot(1 - spot.c, step)))
+
+        @pl.when(step > 0)
+        def _():
+            later.flush(step - 1)
+
+        return carry
+
+    lax.fori_loop(0, 4, visit, 0)
+    later.flush(3)
+    copy = pltpu.make_async_copy(gather.held, second_out, saved.at[0])
+    copy.start()
+    gather.finish()
+    later.relay()
+    if not is_last:
+        onward = Gather(spot, refs[22:27])
+    for part in range(2):
+        rows = pl.ds(part * half, half)
+        branch_two = later.result(part) + offsets[3:4]
+        state = middle_out[rows] + gains[3:4] * branch_two
+        branch_two_out[rows] = branch_two
+        state_out[rows] = state.astype(state_out.dtype)
+        if not is_last:
+            onward.put(part, (norm_parts(state)[0] * next_gains[0:1] + next_offsets[0:1]).astype(BF))
+    if not is_last:
+
+        def use(slot):
+            project(onward.held[slot], weight, bias, head_gain, head_offset, raw_out, qk_out, v_out, slot)
+
+        def visit_next(step, carry):
+            onward.arrive(step)
+            use(spot.slot(spot.c, step))
+            onward.arrive_core(step)
+            use(spot.slot(1 - spot.c, step))
+            return carry
+
+        lax.fori_loop(0, 4, visit_next, 0)
+        copy_next = pltpu.make_async_copy(onward.held, gathered_out, saved.at[1])
+        copy_next.start()
+        onward.finish()
+        copy_next.wait()
+    later.finish()
+    copy.wait()
+
+
+def backward_kernel(is_first, *refs):
+    if is_first:
+        (grad_ref,) = refs[:1]
+        refs = refs[1:]
+    else:
+        (grad_qkv, above_weight, above_hidden, above_middle_grad, above_gains) = refs[:5]
+        refs = refs[5:]
+    (branch_two, activated, slope, second, middle, branch, mixed) = refs[:7]
+    (down_weight, up_weight, out_weight, gains) = refs[7:11]
+    refs = refs[11:]
+    (middle_grad_out, mixed_grad_out, down_grad, up_grad, out_grad, up_bias_grad, small) = refs[:7]
+    refs = refs[7:]
+    local, one, held, held_two, up_rows, grad_rows, = refs[:4], refs[4:10], refs[10:15], refs[15:20], refs[20], refs[21]
+    spot = Spot()
+    spot.greet()
+    gather, scatter, onward = Gather(spot, held), Scatter(spot, local, one), Gather(spot, held_two)
+    half = gather.half
+    small[...] = jnp.zeros_like(small)
+    if not is_first:
+        above = Scatter(spot, local, refs[22:28])
+        above.produce(lambda slot: dot_rt(grad_qkv[slot], above_weight[...]))
+        above.relay()
+    for part in range(2):
+        rows = pl.ds(part * half, half)
+        if is_first:
+            grad = grad_ref[rows]
+        else:
+            normed, scale = norm_parts(above_hidden[rows].astype(F32))
+            grad, gain_term, offset_term = norm_back(above.result(part), above_gains[0:1], normed, scale)
+            small[6:7] += gain_term
+            small[7:8] += offset_term
+            grad = grad + above_middle_grad[rows]
+        grad_rows[rows] = grad
+        scaled = gains[3:4] * grad
+        gather.put(part, scaled.astype(BF))
+        small[0:1] += jnp.sum(grad * branch_two[rows], axis=0, keepdims=True)
+        small[1:2] += jnp.sum(scaled, axis=0, keepdims=True)
+    if not is_first:
+        above.finish()
+
+    def term(slot):
+        up = (dot_rt(gather.held[slot], down_weight[...]) * slope[slot].astype(F32)).astype(BF)
+        up_rows[slot] = up
+        return dot_rt(up, up_weight[...])
+
+    def visit(step, carry):
+        gather.arrive(step)
+        scatter.put_own(step, term(spot.slot(spot.c, step)))
+        gather.arrive_core(step)
+        scatter.put_other(step, term(spot.slot(1 - spot.c, step)))
+
+        @pl.when(step > 0)
+        def _():
+            scatter.flush(step - 1)
+
+        return carry
+
+    lax.fori_loop(0, 4, visit, 0)
+    scatter.flush(3)
+    gather.finish()
+    wide = lambda ref: ref[...].reshape(ref.shape[0] * ref.shape[1], ref.shape[2])
+    down_grad[...] = dot_lt(wide(activated), wide(gather.held)).astype(BF)
+    scatter.relay()
+    up_grad[...] = dot_lt(wide(second), wide(up_rows)).astype(BF)
+    up_bias_grad[...] = jnp.sum(wide(up_rows).astype(F32), axis=0, keepdims=True)
+    for part in range(2):
+        rows = pl.ds(part * half, half)
+        normed, scale = norm_parts(middle[rows])
+        grad, gain_term, offset_term = norm_back(scatter.result(part), gains[1:2], normed, scale)
+        grad = grad + grad_rows[rows]
+        middle_grad_out[rows] = grad
+        scaled = gains[2:3] * grad
+        onward.put(part, scaled.astype(BF))
+        small[2:3] += gain_term
+        small[3:4] += offset_term
+        small[4:5] += jnp.sum(grad * branch[rows], axis=0, keepdims=True)
+        small[5:6] += jnp.sum(scaled, axis=0, keepdims=True)
+    scatter.finish()
+
+    def use(slot):
+        mixed_grad_out[slot] = dot_rt(onward.held[slot], out_weight[...]).astype(BF)
+
+    def visit_next(step, carry):
+        onward.arrive(step)
+        use(spot.slot(spot.c, step))
+        onward.arrive_core(step)
+        use(spot.slot(1 - spot.c, step))
+        return carry
+
+    lax.fori_loop(0, 4, visit_next, 0)
+    onward.finish()
+    out_grad[...] = dot_lt(wide(mixed), wide(onward.held)).astype(BF)
+
+
+def last_kernel(grad_qkv, weight, hidden, middle_grad, gains, grad_out, small, *refs):
+    spot = Spot()
+    spot.greet()
+    scatter = Scatter(spot, refs[:4], refs[4:10])
+    half = scatter.half
+    scatter.produce(lambda slot: dot_rt(grad_qkv[slot], weight[...]))
+    scatter.relay()
+    small[...] = jnp.zeros_like(small)
+    for part in range(2):
+        rows = pl.ds(part * half, half)
+        normed, scale = norm_parts(hidden[rows].astype(F32))
+        grad, gain_term, offset_term = norm_back(scatter.result(part), gains[0:1], normed, scale)
+        small[0:1] += gain_term
+        small[1:2] += offset_term
+        grad_out[rows] = (grad + middle_grad[rows]).astype(BF)
+    scatter.finish()
+
+
+def in_three(values):
+    high = values.astype(BF)
+    rest = values - high.astype(F32)
+    middle = rest.astype(BF)
+    return high, middle, (rest - middle.astype(F32)).astype(BF)
+
+
+def beside(rows, values, head):
+    lane = lax.broadcasted_iota(jnp.int32, rows.shape, 1)
+    start = HD if head == 0 else 0
+    high, middle, low = (part.astype(F32) for part in in_three(values))
+    other = jnp.where(
+        lane == start, high, jnp.where(lane == start + 1, middle, jnp.where(lane == start + 2, low, 0.0))
+    )
+    return jnp.where(lanes_of_head(rows.shape, head), rows.astype(F32), other).astype(BF)
+
+
+def attention_kernel(keys, block, qk, v, mixed, exact, query_out):
+    def visit(index, carry):
+        base = pl.multiple_of(index * block, block)
+        rows = pl.ds(base, block)
+        span = pl.ds(pl.multiple_of(base // keys * keys, keys), keys)
+        queries = qk[rows, : 2 * HD] * jnp.asarray(HD**-0.5, BF)
+        found = []
+        for head in range(2):
+            mine = jnp.where(lanes_of_head(queries.shape, head), queries, jnp.zeros_like(queries))
+            scores = dot_rt(mine, qk[span, 2 * HD :])
+            largest = jnp.max(scores, axis=-1, keepdims=True)
+            weights = jnp.exp(scores - largest)
+            total = jnp.sum(weights, axis=-1, keepdims=True)
+            found.append(dot(weights.astype(BF), v[span, :]) / total)
+            query_out[head, rows] = beside(mine, largest + jnp.log(total), head)
+        both = jnp.where(lanes_of_head(found[0].shape, 0), found[0], found[1])
+        exact[rows] = both
+        mixed[rows] = both.astype(BF)
+        return carry
+
+    lax.fori_loop(0, mixed.shape[0] // block, visit, 0)
+
+
+def attention_back_kernel(
+    keys, block, raw, qk, v, mixed, query, grad, head_gain, grad_qkv, small, bias_grad, grads, key_in, value_in, grad_in
+):
+    tokens = grad.shape[0]
+    width = 2 * HD
+    grads[...] = jnp.zeros_like(grads)
+    lane_sum = averager(width)
+    row = lax.broadcasted_iota(jnp.int32, (width, width), 0) // HD
+    column = lax.broadcasted_iota(jnp.int32, (width, width), 1) // HD
+    swap_sum = jnp.where(row != column, 1.0, 0.0).astype(F32)
+    del lane_sum
+
+    def prepare(index, carry):
+        rows = pl.ds(pl.multiple_of(index * block, block), block)
+        product = grad[rows].astype(F32) * mixed[rows]
+        delta = dot_exact(product, swap_sum)
+        minus = jnp.full((block, width), -1.0, F32)
+        lane = lax.broadcasted_iota(jnp.int32, (block, width), 1)
+        high, middle, low = (part.astype(F32) for part in in_three(delta))
+        for head in range(2):
+            start = HD if head == 0 else 0
+            own = lanes_of_head((block, width), head)
+            other = jnp.where(
+                lane == start, high, jnp.where(lane == start + 1, middle, jnp.where(lane == start + 2, low, 0.0))
+            )
+            grad_in[head, rows] = jnp.where(own, grad[rows].astype(F32), other).astype(BF)
+            ones = jnp.where(own, 0.0, jnp.where(lane < start + 3, minus, 0.0))
+            key_in[head, rows] = jnp.where(own, qk[rows, width:].astype(F32), ones).astype(BF)
+            value_in[head, rows] = jnp.where(own, v[rows].astype(F32), ones).astype(BF)
+        return carry
+
+    lax.fori_loop(0, tokens // block, prepare, 0)
+    spans = keys // block
+
+    def visit(index, carry):
+        query_at = index // spans
+        key_at = query_at * block // keys * spans + lax.rem(index, spans)
+        query_rows = pl.ds(pl.multiple_of(query_at * block, block), block)
+        key_rows = pl.ds(pl.multiple_of(key_at * block, block), block)
+        for head in range(2):
+            own = lanes_of_head((block, width), head)
+            zeros = jnp.zeros((block, width), BF)
+            query_rows_in = query[head, query_rows]
+            grad_rows_in = grad_in[head, query_rows]
+            key_rows_in = key_in[head, key_rows]
+            probs = jnp.exp(dot_rt(key_rows_in, query_rows_in))
+            back = (probs * dot_rt(value_in[head, key_rows], grad_rows_in)).astype(BF)
+            grads[key_rows, 2 * width :] += dot(probs.astype(BF), jnp.where(own, grad_rows_in, zeros))
+            grads[key_rows, width : 2 * width] += dot(back, jnp.where(own, query_rows_in, zeros))
+            grads[query_rows, :width] += dot_lt(back, jnp.where(own, key_rows_in, zeros))
+        return carry
+
+    lax.fori_loop(0, tokens // block * spans, visit, 0)
+    small[...] = jnp.zeros_like(small)
+    bias_grad[...] = jnp.zeros_like(bias_grad)
+    average = averager(2 * width)
+
+    def leave(index, carry):
+        rows = pl.ds(pl.multiple_of(index * block, block), block)
+        values = raw[rows]
+        centered = values - dot_exact(values, average)
+        scale = lax.rsqrt(dot_exact(centered * centered, average) + EPSILON)
+        normed = centered * scale
+        lane = lax.broadcasted_iota(jnp.int32, normed.shape, 1)
+        found = grads[rows, : 2 * width] * jnp.where(lane < width, HD**-0.5, 1.0)
+        small[0:1] += jnp.sum(found * normed, axis=0, keepdims=True)
+        small[1:2] += jnp.sum(found, axis=0, keepdims=True)
+        scaled = found * head_gain[...]
+        back = scale * (scaled - dot_exact(scaled, average) - normed * dot_exact(scaled * normed, average))
+        back = back.astype(BF)
+        values_back = grads[rows, 2 * width :].astype(BF)
+        grad_qkv[rows, : 2 * width] = back
+        grad_qkv[rows, 2 * width :] = values_back
+        bias_grad[:, : 2 * width] += jnp.sum(back.astype(F32), axis=0, keepdims=True)
+        bias_grad[:, 2 * width :] += jnp.sum(values_back.astype(F32), axis=0, keepdims=True)
+        return carry
+
+    lax.fori_loop(0, tokens // block, leave, 0)
+
+
+def over_square(kernel, name, outs, operands, scratch, number, outside=()):
+    return pl.pallas_call(
+        kernel,
+        name=name,
+        out_shape=outs,
+        in_specs=[pl.BlockSpec(memory_space=pltpu.VMEM)] * len(operands),
+        out_specs=[
+            pl.BlockSpec(memory_space=pl.ANY if place in outside else pltpu.VMEM) for place in range(len(outs))
+        ],
+        scratch_shapes=scratch,
+        compiler_params=pltpu.CompilerParams(
+            collective_id=number, has_side_effects=True, vmem_limit_bytes=VMEM_LIMIT
+        ),
+    )(*operands)
+
+
+def alone(kernel, name, outs, operands, scratch=()):
+    return pl.pallas_call(
+        kernel,
+        name=name,
+        out_shape=outs,
+        in_specs=[pl.BlockSpec(memory_space=pltpu.VMEM)] * len(operands),
+        out_specs=[pl.BlockSpec(memory_space=pltpu.VMEM)] * len(outs),
+        scratch_shapes=list(scratch),
+        compiler_params=pltpu.CompilerParams(vmem_limit_bytes=VMEM_LIMIT),
+    )(*operands)
+
+
+def shape(*sizes):
+    return jax.ShapeDtypeStruct(sizes[:-1], sizes[-1])
+
+
+def exchange(values):
+    return lax.ppermute(values, ("c", "h"), [(0, 0), (1, 2), (2, 1), (3, 3)])
+
+
+def by_kind(values):
+    split = values.reshape(values.shape[:-1] + (2, 3, HD))
+    return jnp.swapaxes(split, -3, -2).reshape(values.shape)
+
+
+def by_head(values):
+    split = values.reshape(values.shape[:-1] + (3, 2, HD))
+    return jnp.swapaxes(split, -3, -2).reshape(values.shape)
+
+
+def over_scenes(grad):
+    sy, c, h = (lax.axis_index(name) for name in ("sy", "c", "h"))
+    halves = grad.reshape(2, grad.shape[0] // 2, grad.shape[1])
+    keep = lax.dynamic_index_in_dim(halves, sy, 0, keepdims=False)
+    give = lax.dynamic_index_in_dim(halves, 1 - sy, 0, keepdims=False)
+    got = lax.ppermute(give, "sy", [(0, 1), (1, 0)])
+    share = (keep.astype(F32) + got.astype(F32)).astype(BF)
+    got = lax.ppermute(share, ("c", "h"), [(1, 0), (2, 3)])
+    share = (share.astype(F32) + got.astype(F32)).astype(BF)
+    other = lax.ppermute(share, ("sy", "c", "h"), [(0, 4), (4, 0), (3, 7), (7, 3)])
+    home = c == h
+    core = [(0, 2), (3, 1)]
+    share = jnp.where(home, share, lax.ppermute(share, ("c", "h"), core))
+    other = jnp.where(home, other, lax.ppermute(other, ("c", "h"), core))
+    first, later = jnp.where(sy == 0, share, other), jnp.where(sy == 0, other, share)
+    return jnp.concatenate([first, later], axis=0)
+
+
+def square_body(
+    frames_in,
+    qkv_weight,
+    qkv_bias,
+    out_weight,
+    up_weight,
+    up_bias,
+    down_weight,
+    norm_gain,
+    norm_offset,
+    head_gain,
+    head_offset,
+    cotangent,
+    visible,
+    query_count,
+):
+    rows, width = frames_in.shape[1:]
+    tokens = 8 * rows
+    inner = mid = 2 * HD
+    hidden_units = up_weight.shape[2]
+    frames = exchange(frames_in[0])
+    qkv_weights, out_weights, up_weights, down_weights, qkv_biases, up_biases = (
+        [exchange(stacked[block]) for block in range(2)]
+        for stacked in (by_kind(qkv_weight), out_weight, up_weight, down_weight, by_kind(qkv_bias), up_bias)
+    )
+    qkv_biases = [bias.astype(F32)[None] for bias in qkv_biases]
+    up_biases = [bias.astype(F32)[None] for bias in up_biases]
+    weighting = visible[0].astype(F32) * (query_count[0].astype(F32) / QMAX)
+    grad = exchange(cotangent[0]).astype(F32) * exchange(weighting)[:, None]
+    head_gains, head_offsets = (
+        [jnp.concatenate([pair[block, 0]] * 2 + [pair[block, 1]] * 2)[None] for block in range(2)]
+        for pair in (head_gain, head_offset)
+    )
+    gather = Gather.scratch(rows, width)
+    local, scatter = Scatter.local(rows, width), Scatter.scratch(rows, width)
+    dma = pltpu.SemaphoreType.DMA
+    qkv_outs = [
+        shape(8, rows, width, BF),
+        shape(8, rows, 2 * inner, F32),
+        shape(8, rows, 2 * inner, BF),
+        shape(8, rows, inner, BF),
+    ]
+
+    def attend(block, raw, qk, v):
+        keys = FRAME_TOK if block == 0 else tokens
+        flat = [part.reshape(tokens, part.shape[2]) for part in (qk, v)]
+        return alone(
+            functools.partial(attention_kernel, keys, 256),
+            f"attention_{block}",
+            [shape(tokens, inner, BF), shape(tokens, inner, F32), shape(2, tokens, inner, BF)],
+            flat,
+        )
+
+    def attend_back(block, saved, grad_mixed):
+        keys = FRAME_TOK if block == 0 else tokens
+        flat = [part.reshape(tokens, part.shape[2]) for part in (saved["raw"], saved["qk"], saved["v"])]
+        return alone(
+            functools.partial(attention_back_kernel, keys, 512),
+            f"attention_back_{block}",
+            [shape(tokens, 3 * inner, BF), shape(2, 2 * inner, F32), shape(1, 3 * inner, F32)],
+            flat + [saved["exact"], saved["query"], grad_mixed.reshape(tokens, inner), head_gains[block]],
+            [pltpu.VMEM((tokens, 3 * inner), F32)] + [pltpu.VMEM((2, tokens, inner), BF)] * 3,
+        )
+
+    saved = [{}, {}]
+    gathered, raw, qk, v = over_square(
+        first_kernel,
+        "gather_project",
+        qkv_outs,
+        [frames, norm_gain[0], norm_offset[0], qkv_weights[0], qkv_biases[0], head_gains[0], head_offsets[0]],
+        gather + [dma],
+        0,
+        (0,),
+    )
+    hidden = frames
+    for block in range(2):
+        is_last = block == 1
+        mixed, exact, query = attend(block, raw, qk, v)
+        saved[block].update(hidden=hidden, gathered=gathered, raw=raw, qk=qk, v=v, mixed=mixed, exact=exact, query=query)
+        operands = [
+            mixed.reshape(8, rows, inner),
+            hidden,
+            out_weights[block],
+            up_weights[block],
+            up_biases[block],
+            down_weights[block],
+            norm_gain[block],
+            norm_offset[block],
+        ]
+        outs = [
+            shape(rows, width, F32),
+            shape(rows, width, F32),
+            shape(8, rows, width, BF),
+            shape(8, rows, hidden_units, BF),
+            shape(8, rows, hidden_units, BF),
+            shape(rows, width, F32),
+            shape(rows, width, BF if is_last else F32),
+        ]
+        scratch = local + scatter + scatter + gather + [dma((2,))]
+        if not is_last:
+            operands += [
+                norm_gain[1], norm_offset[1], qkv_weights[1], qkv_biases[1], head_gains[1], head_offsets[1],
+            ]
+            outs += qkv_outs
+            scratch += gather
+        found = over_square(
+            functools.partial(forward_kernel, is_last),
+            f"feed_forward_{block}",
+            outs,
+            operands,
+            scratch,
+            1 + block,
+            (2,) if is_last else (2, 7),
+        )
+        names = ("branch", "middle", "second", "activated", "slope", "branch_two")
+        saved[block].update(zip(names, found))
+        hidden = found[6]
+        if not is_last:
+            gathered, raw, qk, v = found[7:]
+    layer_out = exchange(hidden)[None]
+
+    large = [None, None]
+    gain_rows, offset_rows = [[None] * 4, [None] * 4], [[None] * 4, [None] * 4]
+    up_bias_grads, qkv_bias_grads, head_grads = [None, None], [None, None], [None, None]
+    back = None
+    for block in (1, 0):
+        is_first = block == 1
+        kept = saved[block]
+        if is_first:
+            operands = [grad]
+        else:
+            above = saved[1]
+            operands = [
+                back.reshape(8, rows, 3 * inner), qkv_weights[1], above["hidden"], middle_grad, norm_gain[1],
+            ]
+        operands += [kept[name] for name in ("branch_two", "activated", "slope", "second", "middle", "branch")]
+        operands += [kept["mixed"].reshape(8, rows, inner)]
+        operands += [down_weights[block], up_weights[block], out_weights[block], norm_gain[block]]
+        middle_grad, mixed_grad, down_grad, up_grad, out_grad, up_bias_grads[block], small = over_square(
+            functools.partial(backward_kernel, is_first),
+            f"feed_back_{block}",
+            [
+                shape(rows, width, F32),
+                shape(8, rows, inner, BF),
+                shape(hidden_units, width, BF),
+                shape(width, hidden_units, BF),
+                shape(inner, width, BF),
+                shape(1, hidden_units, F32),
+                shape(8, width, F32),
+            ],
+            operands,
+            local
+            + scatter
+            + gather
+            + gather
+            + [pltpu.VMEM((8, rows, hidden_units), BF), pltpu.VMEM((rows, width), F32)]
+            + ([] if is_first else scatter),
+            3 + block,
+        )
+        gain_rows[block][3], offset_rows[block][3] = small[0], small[1]
+        gain_rows[block][1], offset_rows[block][1] = small[2], small[3]
+        gain_rows[block][2], offset_rows[block][2] = small[4], small[5]
+        if not is_first:
+            gain_rows[1][0], offset_rows[1][0] = small[6], small[7]
+        back, head_grads[block], qkv_bias_grads[block] = attend_back(block, kept, mixed_grad)
+        qkv_grad = jnp.einsum(
+            "td,tc->dc", kept["gathered"].reshape(tokens, width), back, preferred_element_type=F32
+        ).astype(BF)
+        large[block] = [over_scenes(part) for part in (qkv_grad, out_grad, up_grad, down_grad)]
+    grad_in, small = over_square(
+        last_kernel,
+        "project_back",
+        [shape(rows, width, BF), shape(8, width, F32)],
+        [back.reshape(8, rows, 3 * inner), qkv_weights[0], saved[0]["hidden"], middle_grad, norm_gain[0]],
+        local + scatter,
+        5,
+    )
+    gain_rows[0][0], offset_rows[0][0] = small[0], small[1]
+    input_grad = exchange(grad_in)[None]
+
+    c, h, zl, x = (lax.axis_index(name) for name in ("c", "h", "zl", "x"))
+    place = zl * 2 + x
+    biases = jnp.stack(
+        [jnp.concatenate([by_head(qkv_bias_grads[block][0]), up_bias_grads[block][0]]) for block in range(2)]
+    )
+    biases = jnp.where(jnp.arange(8)[:, None, None] == c * 4 + place, biases[None], 0.0)
+    heads = jnp.stack(head_grads).reshape(2, 2, 2, 2, HD).sum(axis=3)
+    small = (
+        jnp.stack([jnp.stack(part) for part in gain_rows]),
+        jnp.stack([jnp.stack(part) for part in offset_rows]),
+        heads,
+        biases,
+    )
+    gain_grad, offset_grad, heads, biases = lax.psum(small, AXES)
+    biases = lax.dynamic_index_in_dim(biases, h * 4 + place, 0, keepdims=False)
+    qkv_grad, out_grad, up_grad, down_grad = (
+        jnp.stack([first, later]).astype(F32) for first, later in zip(large[0], large[1])
+    )
+    return (
+        layer_out,
+        input_grad,
+        by_head(qkv_grad),
+        biases[:, : 3 * inner],
+        out_grad,
+        up_grad,
+        biases[:, 3 * inner :],
+        down_grad,
+        gain_grad,
+        offset_grad,
+        heads[:, 0],
+        heads[:, 1],
+    )
+
+
+TP = ("c", "r")
 
 
 def layer_norm(values, norm_scale, norm_bias):
@@ -112,7 +1021,7 @@
     return (grad_query.reshape(queries.shape), grad_key, grad_value)
 
 
-def body(
+def any_body(
     frames_in,
     qkv_weight,
     qkv_bias,
@@ -129,6 +1038,14 @@
     query_count,
 ):
     score_scale = HD ** (-0.5)
+    frames = exchange(frames_in[0])
+    qkv_weight, out_weight, up_weight, down_weight, qkv_bias, up_bias = (
+        [exchange(stacked[block_index]) for block_index in range(2)]
+        for stacked in (qkv_weight, out_weight, up_weight, down_weight, qkv_bias, up_bias)
+    )
+    weighting = visible[0].astype(jnp.float32) * (query_count[0].astype(jnp.float32) / QMAX)
+    weighting = exchange(weighting)
+    cotangent = exchange(cotangent[0])
 
     def backward_block(grad_out, block_index, frame_only, saved):
         (
@@ -153,7 +1070,7 @@
         grad_branch_two = gains[3] * grad_out
         offset_grad_three = jnp.sum(grad_branch_two, axis=0)
         gain_grad_three = jnp.sum(grad_out * branch_two, axis=0)
-        shard_rows = lax.all_gather(grad_branch_two.astype(jnp.bfloat16), "tp", axis=0, tiled=True)
+        shard_rows = lax.all_gather(grad_branch_two.astype(jnp.bfloat16), TP, axis=0, tiled=True)
         down_grad = jnp.einsum(
             "tf,td->fd", activated, shard_rows, preferred_element_type=jnp.float32
         )
@@ -170,7 +1087,7 @@
             jnp.einsum(
                 "tf,df->td", up_grads, up_weight[block_index], preferred_element_type=jnp.float32
             ).astype(jnp.bfloat16),
-            "tp",
+            TP,
             scatter_dimension=0,
             tiled=True,
         ).astype(jnp.float32)
@@ -181,7 +1098,7 @@
         grad_branch = gains[2] * middle_grad
         offset_grad_two = jnp.sum(grad_branch, axis=0)
         gain_grad_two = jnp.sum(middle_grad * branch, axis=0)
-        shard_rows = lax.all_gather(grad_branch.astype(jnp.bfloat16), "tp", axis=0, tiled=True)
+        shard_rows = lax.all_gather(grad_branch.astype(jnp.bfloat16), TP, axis=0, tiled=True)
         out_grad = jnp.einsum(
             "tc,td->cd", mixed_flat, shard_rows, preferred_element_type=jnp.float32
         )
@@ -220,7 +1137,7 @@
                 qkv_weight[block_index],
                 preferred_element_type=jnp.float32,
             ).astype(jnp.bfloat16),
-            "tp",
+            TP,
             scatter_dimension=0,
             tiled=True,
         ).astype(jnp.float32)
@@ -244,14 +1161,14 @@
         )
         return (hidden_grad, large_grads, small_grads)
 
-    hidden = frames_in[0].astype(jnp.float32)
+    hidden = frames.astype(jnp.float32)
     kept_states = []
     for block_index in range(2):
         forward_frame_only = block_index == 0
         forward_gains = norm_gain[block_index]
         forward_offsets = norm_offset[block_index]
         normed = layer_norm(hidden, forward_gains[0], forward_offsets[0]).astype(jnp.bfloat16)
-        forward_gathered = lax.all_gather(normed, "tp", axis=0, tiled=True)
+        forward_gathered = lax.all_gather(normed, TP, axis=0, tiled=True)
         projected = jnp.dot(
             forward_gathered, qkv_weight[block_index], preferred_element_type=jnp.float32
         )
@@ -274,7 +1191,7 @@
                 jnp.dot(
                     forward_mixed_flat, out_weight[block_index], preferred_element_type=jnp.float32
                 ).astype(jnp.bfloat16),
-                "tp",
+                TP,
                 scatter_dimension=0,
                 tiled=True,
             ).astype(jnp.float32)
@@ -284,7 +1201,7 @@
         second = layer_norm(forward_middle, forward_gains[1], forward_offsets[1]).astype(
             jnp.bfloat16
         )
-        forward_gathered_two = lax.all_gather(second, "tp", axis=0, tiled=True)
+        forward_gathered_two = lax.all_gather(second, TP, axis=0, tiled=True)
         forward_hidden_up = jnp.dot(
             forward_gathered_two, up_weight[block_index], preferred_element_type=jnp.float32
         )
@@ -295,7 +1212,7 @@
                 jnp.dot(
                     forward_activated, down_weight[block_index], preferred_element_type=jnp.float32
                 ).astype(jnp.bfloat16),
-                "tp",
+                TP,
                 scatter_dimension=0,
                 tiled=True,
             ).astype(jnp.float32)
@@ -321,36 +1238,33 @@
         hidden = result
         saved = forward_saved
         kept_states.append(saved)
-    layer_out = hidden.astype(jnp.bfloat16)[None]
-    grad_hidden = (
-        cotangent[0].astype(jnp.float32)
-        * visible[0].astype(jnp.float32)[:, None]
-        * (query_count[0].astype(jnp.float32) / QMAX)
-    )
+    layer_out = exchange(hidden.astype(jnp.bfloat16))[None]
+    grad_hidden = cotangent.astype(jnp.float32) * weighting[:, None]
     grad_hidden, large_one, small_one = backward_block(grad_hidden, 1, False, kept_states[1])
     grad_hidden, large_zero, small_zero = backward_block(grad_hidden, 0, True, kept_states[0])
-    input_grad = grad_hidden.astype(jnp.bfloat16)[None]
-
-    def stack_pair(first, later):
-        return jnp.stack([first, later])
-
-    qkv_w_part, qkv_b_part, out_w_part, up_w_part, up_b_part, down_w_part = jax.tree.map(
-        stack_pair, large_zero, large_one
-    )
-    gain_part, offset_part, head_gain_part, head_offset_part = jax.tree.map(
-        stack_pair, small_zero, small_one
-    )
-    summed = (
-        lax.psum(qkv_w_part.astype(jnp.bfloat16), "scene").astype(jnp.float32),
-        lax.psum(qkv_b_part.astype(jnp.bfloat16), "scene").astype(jnp.float32),
-        lax.psum(out_w_part.astype(jnp.bfloat16), "scene").astype(jnp.float32),
-        lax.psum(up_w_part.astype(jnp.bfloat16), "scene").astype(jnp.float32),
-        lax.psum(up_b_part.astype(jnp.bfloat16), "scene").astype(jnp.float32),
-        lax.psum(down_w_part.astype(jnp.bfloat16), "scene").astype(jnp.float32),
-    )
-    summed = tuple(summed) + tuple(
-        lax.psum((gain_part, offset_part, head_gain_part, head_offset_part), ("scene", "tp"))
-    )
+    input_grad = exchange(grad_hidden.astype(jnp.bfloat16))[None]
+
+    def over_scenes(grads):
+        shapes = [grad.shape for grad in grads]
+        parts = lax.axis_size("sy")
+        flat = [grad.astype(jnp.bfloat16).reshape(parts, -1) for grad in grads]
+        sizes = [part.shape[1] for part in flat]
+        joined = jnp.concatenate(flat, axis=1)
+        share = lax.psum_scatter(joined, "sy", scatter_dimension=0, tiled=True)
+        share = lax.psum(share, "h")
+        whole = exchange(lax.all_gather(share, "sy", axis=0, tiled=True))
+        found = []
+        start = 0
+        for shape, size in zip(shapes, sizes):
+            found.append(whole[:, start : start + size].reshape(shape).astype(jnp.float32))
+            start += size
+        return found
+
+    summed_one = over_scenes(large_one)
+    summed_zero = over_scenes(large_zero)
+    summed = [jnp.stack(pair) for pair in zip(summed_zero, summed_one)]
+    small = jax.tree.map(lambda first, later: jnp.stack([first, later]), small_zero, small_one)
+    summed = tuple(summed) + tuple(lax.psum(small, ("sy", "c", "h", "r")))
     return (
         layer_out,
         input_grad,
@@ -368,34 +1282,40 @@
 
 
 def solution(mesh):
+    scenes, shards = mesh.shape["scene"], mesh.shape["tp"]
+    if (scenes, shards) == (4, 8):
+        body, sizes, axes, tp = square_body, (2, 2, 2, 2, 2), AXES, ("h", "zl", "x")
+    else:
+        body, sizes, axes, tp = any_body, (scenes // 2, 2, 2, shards // 2), ("sy", "c", "h", "r"), ("h", "r")
+    scene = ("sy", "c")
     return jax.shard_map(
         body,
-        mesh=mesh,
+        mesh=jax.sharding.Mesh(mesh.devices.reshape(sizes), axes),
         in_specs=(
-            P("scene", "tp", None),
-            P(None, None, "tp"),
-            P(None, "tp"),
-            P(None, "tp", None),
-            P(None, None, "tp"),
-            P(None, "tp"),
-            P(None, "tp", None),
+            P(scene, tp, None),
+            P(None, None, tp),
+            P(None, tp),
+            P(None, tp, None),
+            P(None, None, tp),
+            P(None, tp),
+            P(None, tp, None),
             P(),
             P(),
             P(),
             P(),
-            P("scene", "tp", None),
-            P("scene", "tp"),
-            P("scene"),
+            P(scene, tp, None),
+            P(scene, tp),
+            P(scene),
         ),
         out_specs=(
-            P("scene", "tp", None),
-            P("scene", "tp", None),
-            P(None, None, "tp"),
-            P(None, "tp"),
-            P(None, "tp", None),
-            P(None, None, "tp"),
-            P(None, "tp"),
-            P(None, "tp", None),
+            P(scene, tp, None),
+            P(scene, tp, None),
+            P(None, None, tp),
+            P(None, tp),
+            P(None, tp, None),
+            P(None, None, tp),
+            P(None, tp),
+            P(None, tp, None),
             P(),
             P(),
             P(),

time: 1930 us -> 1040 us (0.54)
  waiting for transfers between devices: 1450 us -> 192 us
  Pallas kernels: 0 us -> 624 us
  matrix products: 209 us -> 9.09 us
  starting transfers between devices: 2.02 us -> 119 us
  other arithmetic: 138 us -> 28.2 us
  local copies, waits for them, and re-layouts: 99.9 us -> 44.5 us
    reduce_scatter x8 -> x0, waiting for transfers between devices: 679 us -> none  [the longest x2 173 us: body(): lax.psum_scatter(jnp.dot(forward_activated, down_weight[block_index], pre...]
    pallas_call x0 -> x10, Pallas kernels: none -> 624 us  [the longest x6 522 us: over_square(): pl.pallas_call(kernel, name=name, out_shape=outs, in_specs=[pl.BlockSpec(...]
    all_gather x8 -> x0, waiting for transfers between devices: 548 us -> none  [the longest x2 147 us: body(): forward_gathered = lax.all_gather(normed, 'tp', axis=0, tiled=True)]
    dot_general x52 -> x2, matrix products: 209 us -> 9.09 us  [square_body(): jnp.einsum('td,tc->dc', kept['gathered'].reshape(tokens, width), back, pr...]
    ppermute x0 -> x57, starting transfers between devices: none -> 119 us  [the longest x17 50.6 us: exchange(): return lax.ppermute(values, ('c', 'h'), [(0, 0), (1, 2), (2, 1), (3, 3)])]
    psum x2 -> x1, waiting for transfers between devices: 220 us -> 120 us  [square_body(): gain_grad, offset_grad, heads, biases = lax.psum(small, AXES)]
    ppermute x0 -> x57, waiting for transfers between devices: none -> 72.6 us  [the longest x8 34.9 us: over_scenes(): got = lax.ppermute(share, ('c', 'h'), [(1, 0), (2, 3)])]
    reduce_sum x43 -> x1, other arithmetic: 68.2 us -> 0.62 us  [square_body(): heads = jnp.stack(head_grads).reshape(2, 2, 2, 2, HD).sum(axis=3)]
  transfers between devices with their start and end apart: 18 -> 58, of which waited for: 18 -> 14; matrix products, arithmetic and copies ran while one was open for 4% -> 7% of each run, Pallas kernels for 0% -> 53%
where the time goes in v1:
time: 1040 us; the launch traced here: 1030 us
  Pallas kernels  624 us (60%)
  waiting for transfers between devices  192 us (18%)
  starting transfers between devices  119 us (11%)
  local copies, waits for them, and re-layouts  44.5 us (4%)
  other arithmetic  28.2 us (3%)
  between operations  16.3 us (2%)
    pallas_call x6, Pallas kernels, over_square(): pl.pallas_call(kernel, name=name, out_shape=outs, in_specs=[pl.BlockSpec(...  522 us
    psum x1, waiting for transfers between devices, square_body(): gain_grad, offset_grad, heads, biases = lax.psum(small, AXES)  120 us
    pallas_call x4, Pallas kernels, alone(): pl.pallas_call(kernel, name=name, out_shape=outs, in_specs=[pl.BlockSpec(...  102 us
    ppermute x17, starting transfers between devices, exchange(): return lax.ppermute(values, ('c', 'h'), [(0, 0), (1, 2), (2, 1), (3, 3)])  50.6 us
    ppermute x8, waiting for transfers between devices, over_scenes(): got = lax.ppermute(share, ('c', 'h'), [(1, 0), (2, 3)])  34.9 us
    ppermute x8, waiting for transfers between devices, over_scenes(): got = lax.ppermute(give, 'sy', [(0, 1), (1, 0)])  33.3 us
    ppermute x8, starting transfers between devices, over_scenes(): lax.ppermute(share, ('sy', 'c', 'h'), [(0, 4), (4, 0), (3, 7), (7, 3)])  27.1 us
  transfers between devices with their start and end apart: 58, of which 14 were waited for; matrix products, arithmetic and copies ran while one was open for 7% of the time, Pallas kernels for 53%

profile of v1, /device:TPU:0, one launch (start us, length us, event | category | flops | bytes accessed | tf_op | source)
XLA Modules:
  0.0 1033.6 jit_solution(5175748947966327912)
XLA Ops:
  17.1 5.4 collective-permute-start.14
  35.1 9.5 collective-permute-start.6
  44.6 7.4 collective-permute-start.7
  67.7 152.7 %gather_project.1 = (bf16[8,256,1024]{2,1,0:T(8,128)(2,1)}, f32[8,256,256]{2,1,0:T(8,128)}, bf16[8,256,256]{2,1,0:T(8,128)(2,1)}, bf16[8,256,128]{2,1,0:T(8,128)(2,1)}) custom-call(bf16[256,1024]{1,0:T(8,128)(2,1)} %copy-done, f32[4,1024]{1,0:T(4,128)} %get-tuple-element.189.gains.refs_6_.refs_15_, f32[4,1024]{1,0:T(4,128)} %get-tuple-element.187.offsets.refs_7_, ...), custom_call_target="tpu_custom_call" | custom-call | tf_op jit(solution)/shard_map/gather_project/pallas_call | solution.py:643
  220.4 12.3 %attention_0.1 = (bf16[2048,128]{1,0:T(8,128)(2,1)}, f32[2048,128]{1,0:T(8,128)}, bf16[2,2048,128]{2,1,0:T(8,128)(2,1)}) custom-call(bf16[2048,256]{1,0:T(8,128)(2,1)} %bitcast.159, bf16[2048,128]{1,0:T(8,128)(2,1)} %bitcast.173), custom_call_target="tpu_custom_call" | custom-call | tf_op jit(solution)/shard_map/attention_0/pallas_call | solution.py:659
  233.7 96.9 %feed_forward_0.1 = (f32[256,1024]{1,0:T(8,128)}, f32[256,1024]{1,0:T(8,128)}, bf16[8,256,1024]{2,1,0:T(8,128)(2,1)}, bf16[8,256,512]{2,1,0:T(8,128)(2,1)}, bf16...) custom-call(bf16[8,256,128]{2,1,0:T(8,128)(2,1)} %bitcast.167, ...), custom_call_target="tpu_custom_call" | custom-call | tf_op jit(solution)/shard_map/feed_forward_0/pallas_call | solution.py:643
  330.6 18.2 %attention_1.1 = (bf16[2048,128]{1,0:T(8,128)(2,1)}, f32[2048,128]{1,0:T(8,128)}, bf16[2,2048,128]{2,1,0:T(8,128)(2,1)}) custom-call(bf16[2048,256]{1,0:T(8,128)(2,1)} %bitcast.161, bf16[2048,128]{1,0:T(8,128)(2,1)} %bitcast.175), custom_call_target="tpu_custom_call" | custom-call | tf_op jit(solution)/shard_map/attention_1/pallas_call | solution.py:659
  350.1 73.3 %feed_forward_1.1 = (f32[256,1024]{1,0:T(8,128)}, f32[256,1024]{1,0:T(8,128)}, bf16[8,256,1024]{2,1,0:T(8,128)(2,1)}, bf16[8,256,512]{2,1,0:T(8,128)(2,1)}, bf16...) custom-call(bf16[8,256,128]{2,1,0:T(8,128)(2,1)} %bitcast.169, ...), custom_call_target="tpu_custom_call" | custom-call | tf_op jit(solution)/shard_map/feed_forward_1/pallas_call | solution.py:643
  423.3 5.4 collective-permute-start.13
  428.7 77.1 %feed_back_1.1 = (f32[256,1024]{1,0:T(8,128)}, bf16[8,256,128]{2,1,0:T(8,128)(2,1)}, bf16[512,1024]{1,0:T(8,128)(2,1)}, bf16[1024,512]{1,0:T(8,128)(2,1)}, bf16[...) custom-call(f32[256,1024]{1,0:T(8,128)} %convert_multiply_fusion.refs_0_, ...), custom_call_target="tpu_custom_call" | custom-call | tf_op jit(solution)/shard_map/feed_back_1/pallas_call | solution.py:643
  505.8 41.7 %attention_back_1.1 = (bf16[2048,384]{1,0:T(8,128)(2,1)}, f32[2,256]{1,0:T(2,128)}, f32[1,384]{1,0:T(1,128)}) custom-call(f32[2048,256]{1,0:T(8,128)} %bitcast.172, bf16[2048,256]{1,0:T(8,128)(2,1)} %bitcast.162, bf16[2048,128]{1,0:T(8,128)(2,1)} %bitcast.176, f32[2048,128]{1,0:T(8,128)} %get-tuple-element.74.mixed, ...), custom_call_target="tpu_custom_call" | custom-call | tf_op jit(solution)/shard_map/attention_back_1/pallas_call | solution.py:659
  547.5 95.9 %feed_back_0.1 = (f32[256,1024]{1,0:T(8,128)}, bf16[8,256,128]{2,1,0:T(8,128)(2,1)}, bf16[512,1024]{1,0:T(8,128)(2,1)}, bf16[1024,512]{1,0:T(8,128)(2,1)}, bf16[...) custom-call(bf16[8,256,384]{2,1,0:T(8,128)(2,1)} %bitcast.177, ...), custom_call_target="tpu_custom_call" | custom-call | tf_op jit(solution)/shard_map/feed_back_0/pallas_call | solution.py:643
  643.4 29.6 %attention_back_0.1 = (bf16[2048,384]{1,0:T(8,128)(2,1)}, f32[2,256]{1,0:T(2,128)}, f32[1,384]{1,0:T(1,128)}) custom-call(f32[2048,256]{1,0:T(8,128)} %bitcast.171, bf16[2048,256]{1,0:T(8,128)(2,1)} %bitcast.160, bf16[2048,128]{1,0:T(8,128)(2,1)} %bitcast.174, f32[2048,128]{1,0:T(8,128)} %get-tuple-element.71.mixed, ...), custom_call_target="tpu_custom_call" | custom-call | tf_op jit(solution)/shard_map/attention_back_0/pallas_call | solution.py:659
  673.0 26.3 %project_back.1 = (bf16[256,1024]{1,0:T(8,128)(2,1)}, f32[8,1024]{1,0:T(8,128)}) custom-call(bf16[8,256,384]{2,1,0:T(8,128)(2,1)} %bitcast.178, bf16[1024,384]{1,0:T(8,128)(2,1)} %copy-done.4, bf16[256,1024]{1,0:T(8,128)(2,1)} %copy-done, f32[256,1024]{1,0:T(8,128)} %get-tuple-element.93.middle_grad, f32[4,1024]{1,0:T(4,128)} %get-tuple-element.189.gains.refs_6_.refs_15_), custom_call_target="tpu_custom_call" | custom-call | tf_op jit(solution)/shard_map/project_back/pallas_call | solution.py:643
  699.3 5.4 collective-permute-start.16
  737.9 119.6 %all-reduce.3.cloned.1.call-done = (f32[8,2,896]{2,1,0:T(2,128)}, f32[2,4,1024]{2,1,0:T(4,128)}, f32[2,4,1024]{2,1,0:T(4,128)}, f32[2,2,2,64]{3,2,1,0:T(2,128)}) async-done(((f32[8,2,896]{2,1,0:T(2,128)}, f32[2,4,1024]{2,1,0:T(4,128)}, f32[2,4,1024]{2,1,0:T(4,128)}, f32[2,2,2,64]{3,2,1,0:T(2,128)}), (f32[8,2,896]{2,1,0:T(2,128)}, f32[2,4,1024]{2,1,0:T(4,128)}, f32[2,4,1024]{2,1,0:T(4,128)}, ...) | async-done | bytes 124944 | tf_op jit(solution)/shard_map/psum | solution.py:899
  868.2 6.4 collective-permute-done.28
  875.9 6.4 collective-permute-done.33
  905.0 5.2 collective-permute-done.37
  913.0 8.5 collective-permute-done.42
  922.9 9.8 collective-permute-done.47
  934.2 6.7 collective-permute-done.52
  943.8 5.0 collective-permute-start.25
  948.9 12.8 %collective-permute-done.38 = bf16[512,512]{1,0:T(8,128)(2,1)S(1)} collective-permute-done((bf16[512,512]{1,0:T(8,128)(2,1)S(1)}, bf16[512,512]{1,0:T(8,128)(2,1)S(1)}, u32[]{:S(2)}, u32[]{:S(2)}) %collective-permute-start.38) | collective-permute-done | bytes 524320 | tf_op jit(solution)/shard_map/ppermute | solution.py:695
  (322 shorter events, 179.9 us)
Async XLA Ops:
  7.2 850.3 %all-reduce.3.cloned.1.call-start = ((), (), s32[]{:S(2)}) async-start(), calls=%async_computation | async-start | bytes 253952 | tf_op jit(solution)/shard_map/psum | solution.py:899
  7.2 37.4 %collective-permute-start = (bf16[256,1024]{1,0:T(8,128)(2,1)}, bf16[256,1024]{1,0:T(8,128)(2,1)S(1)}, u32[]{:S(2)}, u32[]{:S(2)}) collective-permute-start(bf16[256,1024]{1,0:T(8,128)(2,1)} %bitcast.211), channel_id=1, source_target_pairs={{0,0},{4,8},{8,4},{12,12},{1,1},{5,9},{9,5},{13,13},{2,2},{6,10},{... | collective-permute-start | bytes 1572872 | tf_op jit(solution)/shard_map/ppermute | solution.py:675
  12.0 41.9 %collective-permute-start.1 = (bf16[1024,384]{1,0:T(8,128)(2,1)}, bf16[1024,384]{1,0:T(8,128)(2,1)S(1)}, u32[]{:S(2)}, u32[]{:S(2)}) collective-permute-start(bf16[1024,384]{1,0:T(8,128)(2,1)} %copy.46), channel_id=1, source_target_pairs={{0,0},{4,8},{8,4},{12,12},{1,1},{5,9},{9,5},{13,13},{2,2},{6,10},{... | collective-permute-start | bytes 2359304 | tf_op jit(solution)/shard_map/ppermute | solution.py:675
  17.1 34.9 %collective-permute-start.14 = (bf16[256,1024]{1,0:T(8,128)(2,1)}, bf16[256,1024]{1,0:T(8,128)(2,1)}, u32[]{:S(2)}, u32[]{:S(2)}) collective-permute-start(bf16[256,1024]{1,0:T(8,128)(2,1)} %bitcast.212), channel_id=1, source_target_pairs={{0,0},{4,8},{8,4},{12,12},{1,1},{5,9},{9,5},{13,13},{2,2},{6,10},{... | collective-permute-start | bytes 1572872 | tf_op jit(solution)/shard_map/ppermute | solution.py:675
  33.2 199.6 %collective-permute-start.4 = (bf16[1024,512]{1,0:T(8,128)(2,1)}, bf16[1024,512]{1,0:T(8,128)(2,1)S(1)}, u32[]{:S(2)}, u32[]{:S(2)}) collective-permute-start(bf16[1024,512]{1,0:T(8,128)(2,1)} %get-tuple-element.153), channel_id=1, source_target_pairs={{0,0},{4,8},{8,4},{12,12},{1,1},{5,9},{9,5},{13,13},{2,2},{6,10},{... | collective-permute-start | bytes 3145736 | tf_op jit(solution)/shard_map/ppermute | solution.py:675
  35.1 197.7 %collective-permute-start.6 = (bf16[512,1024]{1,0:T(8,128)(2,1)}, bf16[512,1024]{1,0:T(8,128)(2,1)}, u32[]{:S(2)}, u32[]{:S(2)}) collective-permute-start(bf16[512,1024]{1,0:T(8,128)(2,1)} %get-tuple-element.151), channel_id=1, source_target_pairs={{0,0},{4,8},{8,4},{12,12},{1,1},{5,9},{9,5},{13,13},{2,2},{6,10},{... | collective-permute-start | bytes 3145736 | tf_op jit(solution)/shard_map/ppermute | solution.py:675
  52.0 296.7 %collective-permute-start.10 = (bf16[1024,512]{1,0:T(8,128)(2,1)}, bf16[1024,512]{1,0:T(8,128)(2,1)S(1)}, u32[]{:S(2)}, u32[]{:S(2)}) collective-permute-start(bf16[1024,512]{1,0:T(8,128)(2,1)} %get-tuple-element.152), channel_id=1, source_target_pairs={{0,0},{4,8},{8,4},{12,12},{1,1},{5,9},{9,5},{13,13},{2,2},{6,10},{... | collective-permute-start | bytes 3145736 | tf_op jit(solution)/shard_map/ppermute | solution.py:675
  54.8 293.9 %collective-permute-start.12 = (bf16[512,1024]{1,0:T(8,128)(2,1)}, bf16[512,1024]{1,0:T(8,128)(2,1)S(1)}, u32[]{:S(2)}, u32[]{:S(2)}) collective-permute-start(bf16[512,1024]{1,0:T(8,128)(2,1)} %get-tuple-element.150), channel_id=1, source_target_pairs={{0,0},{4,8},{8,4},{12,12},{1,1},{5,9},{9,5},{13,13},{2,2},{6,10},{... | collective-permute-start | bytes 3145736 | tf_op jit(solution)/shard_map/ppermute | solution.py:675
  62.0 286.8 %collective-permute-start.9 = (bf16[128,1024]{1,0:T(8,128)(2,1)}, bf16[128,1024]{1,0:T(8,128)(2,1)}, u32[]{:S(2)}, u32[]{:S(2)}) collective-permute-start(bf16[128,1024]{1,0:T(8,128)(2,1)} %get-tuple-element.168), channel_id=1, source_target_pairs={{0,0},{4,8},{8,4},{12,12},{1,1},{5,9},{9,5},{13,13},{2,2},{6,10},{... | collective-permute-start | bytes 786440 | tf_op jit(solution)/shard_map/ppermute | solution.py:675
  423.3 487.1 %collective-permute-start.13 = (bf16[256,1024]{1,0:T(8,128)(2,1)}, bf16[256,1024]{1,0:T(8,128)(2,1)}, u32[]{:S(2)}, u32[]{:S(2)}) collective-permute-start(bf16[256,1024]{1,0:T(8,128)(2,1)} %get-tuple-element.69), channel_id=1, source_target_pairs={{0,0},{4,8},{8,4},{12,12},{1,1},{5,9},{9,5},{13,13},{2,2},{6,10},{... | collective-permute-start | bytes 1572872 | tf_op jit(solution)/shard_map/ppermute | solution.py:675
  699.3 212.4 %collective-permute-start.16 = (bf16[256,1024]{1,0:T(8,128)(2,1)}, bf16[256,1024]{1,0:T(8,128)(2,1)}, u32[]{:S(2)}, u32[]{:S(2)}) collective-permute-start(bf16[256,1024]{1,0:T(8,128)(2,1)} %get-tuple-element.94), channel_id=1, source_target_pairs={{0,0},{4,8},{8,4},{12,12},{1,1},{5,9},{9,5},{13,13},{2,2},{6,10},{... | collective-permute-start | bytes 1572872 | tf_op jit(solution)/shard_map/ppermute | solution.py:675
  710.3 173.4 %collective-permute-start.22 = (bf16[512,384]{0,1:T(8,128)(2,1)}, bf16[512,384]{0,1:T(8,128)(2,1)}, u32[]{:S(2)}, u32[]{:S(2)}) collective-permute-start(bf16[512,384]{0,1:T(8,128)(2,1)} %bitcast.56), channel_id=1, source_target_pairs={{0,16},{16,0},{1,17},{17,1},{2,18},{18,2},{3,19},{19,3},{4,20},{20... | collective-permute-start | bytes 1179656 | tf_op jit(solution)/shard_map/ppermute | solution.py:693
  717.7 177.6 %collective-permute-start.17 = (bf16[512,384]{0,1:T(8,128)(2,1)}, bf16[512,384]{0,1:T(8,128)(2,1)}, u32[]{:S(2)}, u32[]{:S(2)}) collective-permute-start(bf16[512,384]{0,1:T(8,128)(2,1)} %bitcast.51), channel_id=1, source_target_pairs={{0,16},{16,0},{1,17},{17,1},{2,18},{18,2},{3,19},{19,3},{4,20},{20... | collective-permute-start | bytes 1179656 | tf_op jit(solution)/shard_map/ppermute | solution.py:693
  728.4 132.3 %collective-permute-start.27 = (bf16[64,1024]{1,0:T(8,128)(2,1)}, bf16[64,1024]{1,0:T(8,128)(2,1)S(1)}, u32[]{:S(2)}, u32[]{:S(2)}) collective-permute-start(bf16[64,1024]{1,0:T(8,128)(2,1)} %dynamic-slice_bitcast_fusion.5), channel_id=1, source_target_pairs={{0,16},{16,0},{1,17},{17,1},{2,18},{18,2},{3,19},{19,3},{4,20},{20... | collective-permute-start | bytes 393224 | tf_op jit(solution)/shard_map/ppermute | solution.py:693
  903.2 29.5 %collective-permute-start.47 = (bf16[256,1024]{1,0:T(8,128)(2,1)S(1)}, bf16[256,1024]{1,0:T(8,128)(2,1)S(1)}, u32[]{:S(2)}, u32[]{:S(2)}) collective-permute-start(bf16[256,1024]{1,0:T(8,128)(2,1)S(1)} %copy-done.17), channel_id=1, source_target_pairs={{0,16},{16,0},{1,17},{17,1},{2,18},{18,2},{3,19},{19,3},{4,20},{20... | collective-permute-start | bytes 1572872 | tf_op jit(solution)/shard_map/ppermute | solution.py:693
  910.3 30.6 %collective-permute-start.52 = (bf16[256,1024]{1,0:T(8,128)(2,1)S(1)}, bf16[256,1024]{1,0:T(8,128)(2,1)S(1)}, u32[]{:S(2)}, u32[]{:S(2)}) collective-permute-start(bf16[256,1024]{1,0:T(8,128)(2,1)S(1)} %copy-done.16), channel_id=1, source_target_pairs={{0,16},{16,0},{1,17},{17,1},{2,18},{18,2},{3,19},{19,3},{4,20},{20... | collective-permute-start | bytes 1572872 | tf_op jit(solution)/shard_map/ppermute | solution.py:693
  910.4 32.0 %collective-permute-start.23 = (bf16[512,384]{0,1:T(8,128)(2,1)S(1)}, bf16[512,384]{0,1:T(8,128)(2,1)S(1)}, u32[]{:S(2)}, u32[]{:S(2)}) collective-permute-start(bf16[512,384]{0,1:T(8,128)(2,1)S(1)} %fusion.4), channel_id=1, source_target_pairs={{4,0},{8,12},{5,1},{9,13},{6,2},{10,14},{7,3},{11,15},{20,16},{24,... | collective-permute-start | bytes 1179656 | tf_op jit(solution)/shard_map/ppermute | solution.py:695
  911.7 32.1 %collective-permute-start.18 = (bf16[512,384]{0,1:T(8,128)(2,1)S(1)}, bf16[512,384]{0,1:T(8,128)(2,1)S(1)}, u32[]{:S(2)}, u32[]{:S(2)}) collective-permute-start(bf16[512,384]{0,1:T(8,128)(2,1)S(1)} %fusion.5), channel_id=1, source_target_pairs={{4,0},{8,12},{5,1},{9,13},{6,2},{10,14},{7,3},{11,15},{20,16},{24,... | collective-permute-start | bytes 1179656 | tf_op jit(solution)/shard_map/ppermute | solution.py:695
  921.5 40.2 %collective-permute-start.38 = (bf16[512,512]{1,0:T(8,128)(2,1)S(1)}, bf16[512,512]{1,0:T(8,128)(2,1)S(1)}, u32[]{:S(2)}, u32[]{:S(2)}) collective-permute-start(bf16[512,512]{1,0:T(8,128)(2,1)S(1)} %fusion.3), channel_id=1, source_target_pairs={{4,0},{8,12},{5,1},{9,13},{6,2},{10,14},{7,3},{11,15},{20,16},{24,... | collective-permute-start | bytes 1572872 | tf_op jit(solution)/shard_map/ppermute | solution.py:695
  932.7 34.6 %collective-permute-start.43 = (bf16[512,512]{1,0:T(8,128)(2,1)S(1)}, bf16[512,512]{1,0:T(8,128)(2,1)S(1)}, u32[]{:S(2)}, u32[]{:S(2)}) collective-permute-start(bf16[512,512]{1,0:T(8,128)(2,1)S(1)} %fusion.2), channel_id=1, source_target_pairs={{4,0},{8,12},{5,1},{9,13},{6,2},{10,14},{7,3},{11,15},{20,16},{24,... | collective-permute-start | bytes 1572872 | tf_op jit(solution)/shard_map/ppermute | solution.py:695
  940.9 32.1 %collective-permute-start.48 = (bf16[256,1024]{1,0:T(8,128)(2,1)S(1)}, bf16[256,1024]{1,0:T(8,128)(2,1)S(1)}, u32[]{:S(2)}, u32[]{:S(2)}) collective-permute-start(bf16[256,1024]{1,0:T(8,128)(2,1)S(1)} %fusion.1), channel_id=1, source_target_pairs={{4,0},{8,12},{5,1},{9,13},{6,2},{10,14},{7,3},{11,15},{20,16},{24,... | collective-permute-start | bytes 1572872 | tf_op jit(solution)/shard_map/ppermute | solution.py:695
  942.4 36.2 %collective-permute-start.53 = (bf16[256,1024]{1,0:T(8,128)(2,1)S(1)}, bf16[256,1024]{1,0:T(8,128)(2,1)S(1)}, u32[]{:S(2)}, u32[]{:S(2)}) collective-permute-start(bf16[256,1024]{1,0:T(8,128)(2,1)S(1)} %fusion), channel_id=1, source_target_pairs={{4,0},{8,12},{5,1},{9,13},{6,2},{10,14},{7,3},{11,15},{20,16},{24,... | collective-permute-start | bytes 1572872 | tf_op jit(solution)/shard_map/ppermute | solution.py:695
  943.8 38.7 %collective-permute-start.25 = (bf16[512,384]{0,1:T(8,128)(2,1)S(1)}, bf16[512,384]{0,1:T(8,128)(2,1)S(1)}, u32[]{:S(2)}, u32[]{:S(2)}) collective-permute-start(bf16[512,384]{0,1:T(8,128)(2,1)S(1)} %add_convert_fusion.4), channel_id=1, source_target_pairs={{0,16},{16,0},{12,28},{28,12},{1,17},{17,1},{13,29},{29,13},{2,18}... | collective-permute-start | bytes 1179656 | tf_op jit(solution)/shard_map/ppermute | solution.py:697
  961.7 22.1 %collective-permute-start.20 = (bf16[512,384]{0,1:T(8,128)(2,1)S(1)}, bf16[512,384]{0,1:T(8,128)(2,1)S(1)}, u32[]{:S(2)}, u32[]{:S(2)}) collective-permute-start(bf16[512,384]{0,1:T(8,128)(2,1)S(1)} %add_convert_fusion.5), channel_id=1, source_target_pairs={{0,16},{16,0},{12,28},{28,12},{1,17},{17,1},{13,29},{29,13},{2,18}... | collective-permute-start | bytes 1179656 | tf_op jit(solution)/shard_map/ppermute | solution.py:697
  (88 other events, 1161.8 us)
Sparse Core Ops, SparseCore 0:
  737.3 120.1 all-reduce.2

commit v2 on v0

--- a/solution.py
+++ b/solution.py
@@ -1,14 +1,1647 @@
+import functools
+import types
+
 import jax
 import jax.numpy as jnp
 from jax import lax
+from jax.experimental import pallas as pl
+from jax.experimental.pallas import tpu as pltpu
 from jax.sharding import PartitionSpec as P
 
 HD = 64
 QMAX = 512
 FRAME_TOK = 1024
-
-
 EPSILON = 1e-06
+BF = jnp.bfloat16
+F32 = jnp.float32
+MESH = pl.DeviceIdType.MESH
+DMA = pltpu.SemaphoreType.DMA
+VMEM_LIMIT = 63 * 1024 * 1024
+
+AXES = ("sy", "c", "h", "zl", "x")
+
+
+def dot(left, right):
+    return lax.dot_general(left, right, (((1,), (0,)), ((), ())), preferred_element_type=F32)
+
+
+def dot_rt(left, right):
+    return lax.dot_general(left, right, (((1,), (1,)), ((), ())), preferred_element_type=F32)
+
+
+def dot_lt(left, right):
+    return lax.dot_general(left, right, (((0,), (0,)), ((), ())), preferred_element_type=F32)
+
+
+def dot_fine(left, right):
+    high = left.astype(BF)
+    return dot(high, right) + dot((left - high.astype(F32)).astype(BF), right)
+
+
+def remote(source, target, send, recv, device):
+    return pltpu.make_async_remote_copy(
+        src_ref=source, dst_ref=target, send_sem=send, recv_sem=recv, device_id=device, device_id_type=MESH
+    )
+
+
+class Spot:
+    def __init__(self):
+        self.sy, self.c, self.h, self.zl, self.x = (lax.axis_index(name) for name in AXES)
+        self.over_x = dict(x=1 - self.x)
+        self.over_z = dict(zl=1 - self.zl)
+        self.core = dict(c=1 - self.c)
+        self.over_y = dict(sy=1 - self.sy)
+        self.over_h = dict(h=1 - self.h)
+        self.partner = dict(c=1 - self.c, h=1 - self.h)
+        self.home = self.c == self.h
+        self.away = self.c != self.h
+
+    def greet(self, *devices):
+        barrier = pltpu.get_barrier_semaphore()
+        for device in devices:
+            pl.semaphore_signal(barrier, inc=1, device_id=device, device_id_type=MESH)
+        pl.semaphore_wait(barrier, len(devices))
+
+    def slot(self, core, step):
+        zl = lax.rem(self.zl + step // 2, 2)
+        x = lax.rem(self.x + step % 2, 2)
+        return core * 4 + zl * 2 + x
+
+    def part(self, size, own=True, piece=0, pieces=1):
+        half = size // 2
+        rows = half // pieces
+        return pl.ds(pl.multiple_of((self.sy if own else 1 - self.sy) * half + piece * rows, rows), rows)
+
+
+class Gather:
+    @staticmethod
+    def scratch(rows, width):
+        return [pltpu.VMEM((8, rows, width), BF), DMA((2, 6)), DMA((2, 6)), DMA((2, 4)), DMA((2, 4))]
+
+    def __init__(self, spot, refs):
+        self.spot = spot
+        self.held, self.send, self.recv, self.core_send, self.core_recv = refs
+        self.rows = self.held.shape[1] // 2
+
+    def link(self, stream, step, part, number, device):
+        half = self.rows // 2
+        start = pl.multiple_of(stream * self.rows + part * half, half)
+        ref = self.held.at[self.spot.slot(self.spot.c, step), pl.ds(start, half)]
+        return remote(ref, ref, self.send.at[stream, number], self.recv.at[stream, number], device)
+
+    def x_first(self, stream):
+        return self.link(stream, 0, 0, 0, self.spot.over_x)
+
+    def x_later(self, stream):
+        return self.link(stream, 0, 1, 1, self.spot.over_x)
+
+    def z_later(self, stream):
+        return self.link(stream, 0, 0, 2, self.spot.over_z)
+
+    def z_first(self, stream):
+        return self.link(stream, 0, 1, 3, self.spot.over_z)
+
+    def z_relay(self, stream):
+        return self.link(stream, 1, 0, 4, self.spot.over_z)
+
+    def x_relay(self, stream):
+        return self.link(stream, 2, 1, 5, self.spot.over_x)
+
+    def core_copy(self, stream, step):
+        ref = self.held.at[self.spot.slot(self.spot.c, step), self.span(stream)]
+        return remote(
+            ref, ref, self.core_send.at[stream, step], self.core_recv.at[stream, step], self.spot.core
+        )
+
+    def span(self, stream):
+        return pl.ds(pl.multiple_of(stream * self.rows, self.rows), self.rows)
+
+    def part(self, slot, stream):
+        return self.held[slot, self.span(stream)]
+
+    def put(self, stream, values):
+        self.held[self.spot.slot(self.spot.c, 0), self.span(stream)] = values
+        self.x_first(stream).start()
+        self.z_first(stream).start()
+        self.core_copy(stream, 0).start()
+        self.z_later(stream).start()
+        self.x_later(stream).start()
+
+    def pass_on(self, stream):
+        self.x_first(stream).wait_recv()
+        self.z_relay(stream).start()
+        self.z_first(stream).wait_recv()
+        self.x_relay(stream).start()
+
+    def arrive(self, stream, step):
+        pl.when(step == 1)(lambda: self.x_later(stream).wait_recv())
+        pl.when(step == 2)(lambda: self.z_later(stream).wait_recv())
+
+        @pl.when(step == 3)
+        def _():
+            self.z_relay(stream).wait_recv()
+            self.x_relay(stream).wait_recv()
+
+        pl.when(step > 0)(lambda: self.core_copy(stream, step).start())
+
+    def arrive_core(self, stream, step):
+        self.core_copy(stream, step).wait_recv()
+
+    def finish(self):
+        for stream in range(2):
+            for copy in (self.x_first, self.x_later, self.z_first, self.z_later, self.z_relay, self.x_relay):
+                copy(stream).wait_send()
+            for step in range(4):
+                self.core_copy(stream, step).wait_send()
+
+    def consume(self, use, passed=0, before=None):
+        def visit(index, carry):
+            stream, step = index // 4, lax.rem(index, 4)
+            if before is not None:
+                before(index)
+            self.arrive(stream, step)
+            use(self.spot.slot(self.spot.c, step), stream)
+            pl.when((index >= passed) & (index < 2))(lambda: self.pass_on(index))
+            self.arrive_core(stream, step)
+            use(self.spot.slot(1 - self.spot.c, step), stream)
+            return carry
+
+        lax.fori_loop(0, 8, visit, 0)
+
+
+class Scatter:
+    @staticmethod
+    def local(rows, width):
+        return [
+            pltpu.VMEM((4, rows, width), BF),
+            pltpu.VMEM((4, rows, width), BF),
+            pltpu.VMEM((2, 2, rows // 4, width), BF),
+        ]
+
+    @staticmethod
+    def scratch(rows, width):
+        return [
+            pltpu.VMEM((4, rows, width), BF),
+            pltpu.VMEM((2, 6, rows // 4, width), BF),
+            DMA((2, 4)),
+            DMA((2, 4)),
+            DMA((2, 6)),
+            DMA((2, 6)),
+        ]
+
+    def __init__(self, spot, local, refs):
+        self.spot = spot
+        self.for_core, self.ready, self.relayed = local
+        self.from_core, self.landed, self.core_send, self.core_recv, self.send, self.recv = refs
+        self.rows = self.for_core.shape[1] // 2
+
+    def span(self, stream):
+        return pl.ds(pl.multiple_of(stream * self.rows, self.rows), self.rows)
+
+    def half(self, stream, part):
+        half = self.rows // 2
+        return pl.ds(pl.multiple_of(stream * self.rows + part * half, half), half)
+
+    def link(self, source, stream, number, device):
+        return remote(
+            source, self.landed.at[stream, number], self.send.at[stream, number], self.recv.at[stream, number], device
+        )
+
+    def x_near(self, stream):
+        return self.link(self.ready.at[1, self.half(stream, 0)], stream, 0, self.spot.over_x)
+
+    def x_far(self, stream):
+        return self.link(self.ready.at[3, self.half(stream, 0)], stream, 1, self.spot.over_x)
+
+    def z_near(self, stream):
+        return self.link(self.ready.at[2, self.half(stream, 1)], stream, 2, self.spot.over_z)
+
+    def z_far(self, stream):
+        return self.link(self.ready.at[3, self.half(stream, 1)], stream, 3, self.spot.over_z)
+
+    def z_relay(self, stream):
+        return self.link(self.relayed.at[stream, 0], stream, 4, self.spot.over_z)
+
+    def x_relay(self, stream):
+        return self.link(self.relayed.at[stream, 1], stream, 5, self.spot.over_x)
+
+    def core_copy(self, stream, step):
+        span = self.span(stream)
+        return remote(
+            self.for_core.at[step, span],
+            self.from_core.at[step, span],
+            self.core_send.at[stream, step],
+            self.core_recv.at[stream, step],
+            self.spot.core,
+        )
+
+    def put_other(self, stream, step, values):
+        self.for_core[step, self.span(stream)] = values.astype(BF)
+        self.core_copy(stream, step).start()
+
+    def put_own(self, stream, step, values):
+        self.ready[step, self.span(stream)] = values.astype(BF)
+
+    def flush(self, stream, step):
+        self.core_copy(stream, step).wait_recv()
+        span = self.span(stream)
+        total = self.ready[step, span].astype(F32) + self.from_core[step, span].astype(F32)
+        self.ready[step, span] = total.astype(BF)
+
+        pl.when(step == 1)(lambda: self.x_near(stream).start())
+        pl.when(step == 2)(lambda: self.z_near(stream).start())
+
+        @pl.when(step == 3)
+        def _():
+            self.x_far(stream).start()
+            self.z_far(stream).start()
+
+    def relay(self, stream):
+        self.x_far(stream).wait_recv()
+        mine = self.ready[2, self.half(stream, 0)].astype(F32)
+        self.relayed[stream, 0] = (mine + self.landed[stream, 1].astype(F32)).astype(BF)
+        self.z_relay(stream).start()
+        self.z_far(stream).wait_recv()
+        mine = self.ready[1, self.half(stream, 1)].astype(F32)
+        self.relayed[stream, 1] = (mine + self.landed[stream, 3].astype(F32)).astype(BF)
+        self.x_relay(stream).start()
+
+    def result(self, stream):
+        self.x_near(stream).wait_recv()
+        self.z_near(stream).wait_recv()
+        self.z_relay(stream).wait_recv()
+        self.x_relay(stream).wait_recv()
+        landed = lambda number: self.landed[stream, number].astype(F32)
+        return self.ready[0, self.span(stream)].astype(F32) + jnp.concatenate(
+            [landed(0) + landed(4), landed(2) + landed(5)], axis=0
+        )
+
+    def finish(self):
+        for stream in range(2):
+            for copy in (self.x_near, self.x_far, self.z_near, self.z_far, self.z_relay, self.x_relay):
+                copy(stream).wait_send()
+            for step in range(4):
+                self.core_copy(stream, step).wait_send()
+
+    def produce(self, term, before=None):
+        spot = self.spot
+
+        def visit(index, carry):
+            stream, step = index // 4, 3 - lax.rem(index, 4)
+            if before is not None:
+                before(index)
+            self.put_other(stream, step, term(spot.slot(1 - spot.c, step), stream))
+
+            @pl.when(index > 0)
+            def _():
+                pl.when(index == 5)(lambda: self.relay(0))
+                self.flush((index - 1) // 4, 3 - lax.rem(index - 1, 4))
+
+            self.put_own(stream, step, term(spot.slot(spot.c, step), stream))
+            return carry
+
+        lax.fori_loop(0, 8, visit, 0)
+        self.flush(1, 0)
+
+    def produce_from(self, gather, term, passed=1):
+        spot = self.spot
+
+        def visit(index, carry):
+            stream, step = index // 4, lax.rem(index, 4)
+            gather.arrive(stream, step)
+            self.put_own(stream, step, term(spot.slot(spot.c, step), stream))
+            pl.when((index >= passed) & (index < 2))(lambda: gather.pass_on(index))
+            gather.arrive_core(stream, step)
+            self.put_other(stream, step, term(spot.slot(1 - spot.c, step), stream))
+
+            @pl.when(index > 0)
+            def _():
+                pl.when(index == 6)(lambda: self.relay(0))
+                self.flush((index - 1) // 4, lax.rem(index - 1, 4))
+
+            return carry
+
+        lax.fori_loop(0, 8, visit, 0)
+        self.flush(1, 3)
+
+
+class Swap:
+    scratch = [DMA((2,))]
+
+    def __init__(self, spot, source, target, refs):
+        (sems,) = refs
+        self.spot = spot
+        self.local = pltpu.make_async_copy(source, target, sems.at[0])
+        self.copy = remote(source, target, sems.at[0], sems.at[1], spot.partner)
+
+    def start(self):
+        pl.when(self.spot.home)(self.local.start)
+        pl.when(self.spot.away)(self.copy.start)
+
+    def arrive(self):
+        pl.when(self.spot.home)(self.local.wait)
+        pl.when(self.spot.away)(self.copy.wait_recv)
+
+    def finish(self):
+        pl.when(self.spot.away)(self.copy.wait_send)
+
+
+class Move:
+    scratch = [DMA((2, 4))]
+
+    def __init__(self, spot, own, got, refs):
+        (sems,) = refs
+        self.spot, self.own, self.got = spot, own, got
+        self.over, self.along = [], []
+        for piece in range(2):
+            rows = spot.part(got.shape[0], True, piece, 2)
+            at = sems.at[piece]
+            self.over.append(remote(own.at[rows], got.at[rows], at.at[0], at.at[1], spot.over_h))
+            self.along.append(remote(got.at[rows], got.at[rows], at.at[2], at.at[3], spot.over_y))
+
+    def start(self):
+        @pl.when(self.spot.home)
+        def _():
+            for copy in self.over:
+                copy.start()
+
+    def relay(self, piece):
+        @pl.when(self.spot.away)
+        def _():
+            self.over[piece].wait_recv()
+            self.along[piece].start()
+
+    def finish(self):
+        @pl.when(self.spot.away)
+        def _():
+            for copy in self.along:
+                copy.wait_recv()
+                copy.wait_send()
+
+        @pl.when(self.spot.home)
+        def _():
+            for copy in self.over:
+                copy.wait_send()
+
+    def pick(self, target, sem):
+        copy = pltpu.make_async_copy(self.got, target, sem)
+        pl.when(self.spot.home)(pltpu.make_async_copy(self.own, target, sem).start)
+        pl.when(self.spot.away)(copy.start)
+        return copy
+
+
+class Total:
+    @staticmethod
+    def scratch(rows, width):
+        half = pltpu.VMEM((rows // 2, width), BF)
+        return [half, half, half, DMA((11,))]
+
+    def __init__(self, spot, grad, whole, refs):
+        self.landed, self.share, self.later_landed, sems = refs
+        self.grad, self.spot = grad, spot
+        size = grad.shape[0]
+        mine, other = whole.at[spot.part(size)], whole.at[spot.part(size, False)]
+        share = self.share
+        self.first = remote(grad.at[spot.part(size, False)], self.landed, sems.at[0], sems.at[1], spot.over_y)
+        self.over = remote(share, self.later_landed, sems.at[2], sems.at[3], spot.over_h)
+        self.along = remote(share, mine, sems.at[4], sems.at[5], spot.over_y)
+        self.near = remote(share, mine, sems.at[6], sems.at[7], spot.core)
+        self.later = remote(other, other, sems.at[8], sems.at[9], spot.core)
+        self.local = pltpu.make_async_copy(share, mine, sems.at[10])
+
+    def start(self):
+        self.first.start()
+
+    def add(self):
+        self.first.wait_recv()
+        mine = self.grad[self.spot.part(self.grad.shape[0])]
+        self.share[...] = (mine.astype(F32) + self.landed[...].astype(F32)).astype(BF)
+        pl.when(self.spot.away)(self.over.start)
+
+    def add_over(self):
+        @pl.when(self.spot.home)
+        def _():
+            self.over.wait_recv()
+            self.share[...] = (self.share[...].astype(F32) + self.later_landed[...].astype(F32)).astype(BF)
+            self.along.start()
+            self.near.start()
+            self.local.start()
+
+    def relay(self):
+        @pl.when(self.spot.home)
+        def _():
+            self.along.wait_recv()
+            self.later.start()
+
+    def finish(self):
+        self.first.wait_send()
+
+        @pl.when(self.spot.home)
+        def _():
+            self.along.wait_send()
+            self.near.wait_send()
+            self.later.wait_send()
+            self.local.wait()
+
+        @pl.when(self.spot.away)
+        def _():
+            self.over.wait_send()
+            self.near.wait_recv()
+            self.later.wait_recv()
+
+
+class SmallSum:
+    @staticmethod
+    def scratch(rows, width):
+        return [pltpu.VMEM((5, rows, width), F32), DMA((5,)), DMA((5,))]
+
+    def __init__(self, spot, total, refs):
+        landed, send, recv = refs
+        self.total, self.landed = total, landed
+        self.copies = [
+            remote(total, landed.at[number], send.at[number], recv.at[number], device)
+            for number, device in enumerate((spot.core, spot.over_x, spot.over_z, spot.over_h, spot.over_y))
+        ]
+
+    def step(self, number):
+        if number > 0:
+            self.copies[number - 1].wait()
+            self.total[...] += self.landed[number - 1]
+        if number < 5:
+            self.copies[number].start()
+
+
+class QuickSum:
+    @staticmethod
+    def scratch(rows, width):
+        return [pltpu.VMEM((8, rows, width), F32), pltpu.VMEM((4, rows, width), F32), DMA((10,)), DMA((10,))]
+
+    def __init__(self, spot, total, refs):
+        self.total = total
+        self.near, self.far, send, recv = refs
+        self.near_place = spot.c * 4 + spot.zl * 2 + spot.x
+        self.far_place = spot.sy * 2 + spot.h
+        self.near_copies, self.far_copies = [], []
+        for number in range(1, 8):
+            device = dict(c=spot.c, zl=spot.zl, x=spot.x)
+            for bit, name in ((4, "c"), (2, "zl"), (1, "x")):
+                if number & bit:
+                    device[name] = 1 - device[name]
+            target = self.near.at[self.near_place]
+            self.near_copies.append(remote(total, target, send.at[number - 1], recv.at[number - 1], device))
+        for number in range(1, 4):
+            device = dict(sy=spot.sy, h=spot.h)
+            for bit, name in ((2, "sy"), (1, "h")):
+                if number & bit:
+                    device[name] = 1 - device[name]
+            target = self.far.at[self.far_place]
+            self.far_copies.append(remote(total, target, send.at[number + 6], recv.at[number + 6], device))
+
+    @staticmethod
+    def partners(spot):
+        flip = lambda **names: {name: 1 - getattr(spot, name) for name in names}
+        return [
+            flip(c=0, x=0), flip(c=0, zl=0), flip(zl=0, x=0), flip(c=0, zl=0, x=0), flip(sy=0, h=0),
+        ]
+
+    def start(self):
+        self.near[self.near_place] = self.total[...]
+        for copy in self.near_copies:
+            copy.start()
+
+    def step(self):
+        for copy in self.near_copies:
+            copy.wait()
+        total = self.near[0]
+        for place in range(1, 8):
+            total += self.near[place]
+        self.total[...] = total
+        self.far[self.far_place] = total
+        for copy in self.far_copies:
+            copy.start()
+
+    def end(self):
+        for copy in self.far_copies:
+            copy.wait()
+        total = self.far[0]
+        for place in range(1, 4):
+            total += self.far[place]
+        self.total[...] = total
+
+
+def norm_parts(values):
+    average = jnp.mean(values, axis=-1, keepdims=True)
+    centered = values - average
+    scale = lax.rsqrt(jnp.mean(centered * centered, axis=-1, keepdims=True) + EPSILON)
+    return centered * scale, scale
+
+
+def norm_back(grad, gain, normed, scale):
+    scaled = grad * gain
+    back = scale * (
+        scaled
+        - jnp.mean(scaled, axis=-1, keepdims=True)
+        - normed * jnp.mean(scaled * normed, axis=-1, keepdims=True)
+    )
+    return back, jnp.sum(grad * normed, axis=0, keepdims=True), jnp.sum(grad, axis=0, keepdims=True)
+
+
+def gelu_both(values):
+    size = jnp.abs(values) * 0.7071067811865476
+    bell = jnp.exp(-size * size)
+    t = 1.0 / (1.0 + 0.3275911 * size)
+    poly = t * (
+        0.254829592 + t * (-0.284496736 + t * (1.421413741 + t * (-1.453152027 + t * 1.061405429)))
+    )
+    tail = 0.5 * poly * bell
+    below = jnp.where(values < 0, tail, 1.0 - tail)
+    return values * below, below + values * bell * 0.3989422804014327
+
+
+def lanes_of_head(shape, head):
+    lane = lax.broadcasted_iota(jnp.int32, shape, 1)
+    return (lane < HD) if head == 0 else (lane >= HD)
+
+
+def pack_queries_keys(projected):
+    one, two, three = (projected[:, part * 2 * HD : (part + 1) * 2 * HD] for part in range(3))
+    low = lanes_of_head(one.shape, 0)
+    keys = pltpu.roll(jnp.where(low, three, one), HD, 1)
+    return jnp.concatenate([jnp.where(low, one, two), keys], axis=1), jnp.where(low, two, three)
+
+
+def unpack_queries_keys(queries, keys, values):
+    low = lanes_of_head(queries.shape, 0)
+    keys = pltpu.roll(keys, HD, 1)
+    return jnp.where(low, queries, keys), jnp.where(low, values, queries), jnp.where(low, keys, values)
+
+
+def averager(width):
+    row = lax.broadcasted_iota(jnp.int32, (width, width), 0) // HD
+    column = lax.broadcasted_iota(jnp.int32, (width, width), 1) // HD
+    return jnp.where(row == column, 1.0 / HD, 0.0).astype(BF)
+
+
+def project(k, block, gather, slot, stream):
+    span = gather.span(stream)
+    projected = dot(gather.part(slot, stream), k.qkv_weight[...]) + k.biases[block : block + 1, : 6 * HD]
+    raw, values = pack_queries_keys(projected)
+    k.raw[slot, span] = raw
+    average = averager(4 * HD)
+    centered = raw - dot_fine(raw, average)
+    scale = lax.rsqrt(dot_fine(centered * centered, average) + EPSILON)
+    gain, offset = k.head_gains[block : block + 1], k.head_offsets[block : block + 1]
+    k.qk[slot, span] = (centered * scale * gain + offset).astype(BF)
+    k.v[slot, span] = values.astype(BF)
+
+
+def in_three(values):
+    high = values.astype(BF)
+    rest = values - high.astype(F32)
+    middle = rest.astype(BF)
+    return high.astype(F32), middle.astype(F32), (rest - middle.astype(F32)).astype(BF).astype(F32)
+
+
+def beside(rows, values, head):
+    lane = lax.broadcasted_iota(jnp.int32, rows.shape, 1)
+    start = HD if head == 0 else 0
+    high, middle, low = in_three(values)
+    other = jnp.where(
+        lane == start, high, jnp.where(lane == start + 1, middle, jnp.where(lane == start + 2, low, 0.0))
+    )
+    return jnp.where(lanes_of_head(rows.shape, head), rows.astype(F32), other).astype(BF)
+
+
+def slice_attend(k, keys, start, size):
+    rows = pl.ds(pl.multiple_of(start, size), size)
+    span = pl.ds(pl.multiple_of(start // keys * keys, keys), keys)
+    queries = k.qk_in[rows, : 2 * HD] * jnp.asarray(HD**-0.5, BF)
+    low = lanes_of_head(queries.shape, 0)
+    zeros = jnp.zeros_like(queries)
+    mine = [jnp.where(low, queries, zeros), jnp.where(low, zeros, queries)]
+    scores = dot_rt(jnp.concatenate(mine, axis=0), k.qk_in[span, 2 * HD :])
+    largest = jnp.max(scores, axis=-1, keepdims=True)
+    weights = jnp.exp(scores - largest)
+    total = jnp.sum(weights, axis=-1, keepdims=True)
+    found = dot(weights.astype(BF), k.v_in[span, :]) / total
+    logs = largest + jnp.log(total)
+    for head in range(2):
+        k.query[head, rows] = beside(mine[head], logs[head * size : (head + 1) * size], head)
+    both = jnp.where(low, found[:size], found[size:])
+    k.exact[rows] = both
+    k.mixed[rows] = both.astype(BF)
+
+
+def first_kernel(k):
+    spot = k.spot
+    spot.greet(spot.over_x, spot.over_z, spot.core, spot.over_y, spot.over_h, spot.partner)
+    gather = Gather(spot, k.gather)
+    swaps = [
+        Swap(spot, k.frames.at[0, gather.span(stream)], k.hidden.at[gather.span(stream)], k.swaps[stream])
+        for stream in range(2)
+    ]
+    swaps.append(Swap(spot, k.own_biases, k.biases, k.swaps[2]))
+    swaps[0].start()
+    swaps[2].start()
+    swaps[0].finish()
+    swaps[1].start()
+    for stream in range(2):
+        swaps[stream].arrive()
+        rows = k.hidden[gather.span(stream)].astype(F32)
+        values = (norm_parts(rows)[0] * k.gains[0, 0:1] + k.offsets[0, 0:1]).astype(BF)
+        if stream == 1:
+            gather.pass_on(0)
+        gather.put(stream, values)
+    qkv, out, up = (
+        Move(spot, own.at[0], got, refs)
+        for own, got, refs in zip((k.qkv_own, k.out_own, k.up_own), (k.qkv_got, k.out_got, k.up_got), k.moves)
+    )
+    for move in (qkv, out, up):
+        move.start()
+    k.saves.hidden()
+    gather.pass_on(1)
+    qkv.relay(0)
+    qkv.relay(1)
+    gather.arrive(0, 1)
+    qkv.finish()
+    swaps[2].arrive()
+    qkv.pick(k.qkv_weight, k.pick).wait()
+
+    def visit(index, carry):
+        stream, step = index // 4, lax.rem(index, 4)
+        pl.when(index > 1)(lambda: gather.arrive(stream, step))
+        project(k, 0, gather, spot.slot(spot.c, step), stream)
+        gather.arrive_core(stream, step)
+        project(k, 0, gather, spot.slot(1 - spot.c, step), stream)
+
+        @pl.when(index == 6)
+        def _():
+            out.relay(0)
+            out.relay(1)
+            up.relay(0)
+
+        return carry
+
+    lax.fori_loop(0, 8, visit, 0)
+    k.saves.gathered(gather.held)
+    k.saves.raw()
+    k.saves.qk()
+    k.saves.v()
+    up.relay(1)
+    for swap in swaps[1:]:
+        swap.finish()
+    gather.finish()
+    out.finish()
+    up.finish()
+
+
+def forward_kernel(is_last, k):
+    spot = k.spot
+    block = 1 if is_last else 0
+    spot.greet(spot.over_x, spot.over_z, spot.core, spot.over_y, spot.over_h, spot.partner)
+    down = Move(spot, k.down_own.at[block], k.down_got, k.moves[0])
+    if is_last:
+        up = Move(spot, k.up_own.at[1], k.up_got, k.moves[1])
+        up.start()
+        others = []
+    else:
+        down.start()
+        others = [Move(spot, k.qkv_own.at[1], k.qkv_got, k.moves[1]), Move(spot, k.out_own.at[1], k.out_got, k.moves[2])]
+    first, gather, later = Scatter(spot, k.local, k.one), Gather(spot, k.gather), Scatter(spot, k.local, k.two)
+    rows_of = gather.span
+    size = gather.held.shape[1]
+    keys = k.mixed.shape[0] if is_last else FRAME_TOK
+    k.loads.qk_in.wait()
+    k.loads.v_in.wait()
+    k.loads.out_weight.wait()
+
+    def term_attention(slot, stream):
+        start = pl.multiple_of(slot * size + stream * (size // 2), size // 2)
+        slice_attend(k, keys, start, size // 2)
+        return dot(k.mixed[pl.ds(start, size // 2)], k.out_weight[...])
+
+    def before(index):
+        if is_last:
+
+            @pl.when(index == 6)
+            def _():
+                up.relay(0)
+                up.relay(1)
+                down.start()
+
+        else:
+            pl.when(index == 6)(lambda: down.relay(0))
+
+    first.produce(term_attention, before)
+    k.saves.exact()
+    k.saves.query()
+    k.loads.hidden.wait()
+    for stream in range(2):
+        rows = rows_of(stream)
+        branch = first.result(stream) + k.offsets[block, 2:3]
+        middle = k.hidden[rows].astype(F32) + k.gains[block, 2:3] * branch
+        k.branch[rows] = branch
+        k.middle[rows] = middle
+        gather.put(stream, (norm_parts(middle)[0] * k.gains[block, 1:2] + k.offsets[block, 1:2]).astype(BF))
+        if stream == 0:
+            first.relay(1)
+            if is_last:
+                down.relay(0)
+            else:
+                down.relay(1)
+            gather.pass_on(0)
+    if is_last:
+        down.relay(1)
+        up.finish()
+        up_pick = up.pick(k.up_weight, k.pick.at[0])
+    if is_last:
+        cotangent = Swap(spot, k.cotangent.at[0], k.cotangent_here, k.swaps[0])
+        weighting = Swap(spot, k.weighting, k.weighting_here, k.swaps[1])
+        cotangent.start()
+        weighting.start()
+    for move in others:
+        move.start()
+    k.saves.branch()
+    k.saves.middle()
+    first.finish()
+    gather.pass_on(1)
+    down.finish()
+    down_pick = down.pick(k.down_weight, k.pick.at[1])
+    if is_last:
+        up_pick.wait()
+    else:
+        k.loads.up_weight.wait()
+    down_pick.wait()
+
+    def term(slot, stream):
+        bias = k.biases[block : block + 1, 6 * HD :]
+        activated, slope = gelu_both(dot(gather.part(slot, stream), k.up_weight[...]) + bias)
+        activated = activated.astype(BF)
+        k.activated[slot, rows_of(stream)] = activated
+        k.slope[slot, rows_of(stream)] = slope.astype(BF)
+        return dot(activated, k.down_weight[...])
+
+    later.produce_from(gather, term, 2)
+    k.saves.second(gather.held)
+    k.saves.activated()
+    k.saves.slope()
+    if not is_last:
+        onward = Gather(spot, k.gather_next)
+    for stream in range(2):
+        rows = rows_of(stream)
+        branch = later.result(stream) + k.offsets[block, 3:4]
+        state = k.middle[rows] + k.gains[block, 3:4] * branch
+        k.branch_two[rows] = branch
+        k.state[rows] = state.astype(k.state.dtype)
+        if not is_last:
+            onward.put(stream, (norm_parts(state)[0] * k.gains[1, 0:1] + k.offsets[1, 0:1]).astype(BF))
+        if stream == 0:
+            later.relay(1)
+            if not is_last:
+                onward.pass_on(0)
+            for move in others:
+                move.relay(0)
+                move.relay(1)
+    k.saves.branch_two()
+    k.saves.state()
+    gather.finish()
+    later.finish()
+    if is_last:
+        for swap in (cotangent, weighting):
+            swap.arrive()
+            swap.finish()
+        return
+    for move in others:
+        move.finish()
+    others[0].pick(k.qkv_weight, k.pick.at[0]).wait()
+    onward.consume(functools.partial(project, k, 1, onward), 1)
+    k.saves.gathered(onward.held)
+    k.saves.raw()
+    k.saves.qk()
+    k.saves.v()
+    onward.finish()
+
+
+def wide(ref):
+    return ref[...].reshape(ref.shape[0] * ref.shape[1], ref.shape[2])
+
+
+def with_bias_row(grad_ref, weight_grad, bias_grad):
+    size = weight_grad.shape[0]
+    row = lax.broadcasted_iota(jnp.int32, (grad_ref.shape[0] - size, grad_ref.shape[1]), 0)
+    grad_ref[:size] = weight_grad.astype(BF)
+    grad_ref[size:] = jnp.where(row == 0, bias_grad, 0.0).astype(BF)
+
+
+def pieces_of(ref):
+    cut = ref.shape[0] // 64 * 32
+    return pl.ds(0, cut), pl.ds(cut, ref.shape[0] - cut)
+
+
+def qkv_weight_grad(k, gathered):
+    rows = wide(k.above_qkv)
+    with_bias_row(k.qkv_grad, dot_lt(wide(gathered), rows), jnp.sum(rows.astype(F32), axis=0, keepdims=True))
+
+
+def prepare_keys(k, rows):
+    shape = (rows.size, 2 * HD)
+    lane = lax.broadcasted_iota(jnp.int32, shape, 1)
+    for head in range(2):
+        own = lanes_of_head(shape, head)
+        ones = jnp.where(lane < (HD if head == 0 else 0) + 3, -1.0, 0.0)
+        k.key_in[head, rows] = jnp.where(own, k.qk_in[rows, 2 * HD :].astype(F32), ones).astype(BF)
+        k.value_in[head, rows] = jnp.where(own, k.v_in[rows].astype(F32), ones).astype(BF)
+
+
+def slice_back(k, keys, block_keys, start, size, grad):
+    width = 2 * HD
+    rows = pl.ds(pl.multiple_of(start, size), size)
+    row = lax.broadcasted_iota(jnp.int32, (width, width), 0) // HD
+    column = lax.broadcasted_iota(jnp.int32, (width, width), 1) // HD
+    swap_sum = jnp.where(row != column, 1.0, 0.0).astype(BF)
+    delta = dot_fine(grad * k.exact[rows], swap_sum)
+    lane = lax.broadcasted_iota(jnp.int32, (size, width), 1)
+    high, middle, low = in_three(delta)
+    for head in range(2):
+        lead = HD if head == 0 else 0
+        other = jnp.where(
+            lane == lead, high, jnp.where(lane == lead + 1, middle, jnp.where(lane == lead + 2, low, 0.0))
+        )
+        k.grad_in[head] = jnp.where(lanes_of_head((size, width), head), grad, other).astype(BF)
+    k.query_grad[...] = jnp.zeros_like(k.query_grad)
+    first = start // keys * keys
+
+    def visit(index, carry):
+        key_rows = pl.ds(pl.multiple_of(first + index * block_keys, block_keys), block_keys)
+        for head in range(2):
+            own = lanes_of_head((size, width), head)
+            own_keys = lanes_of_head((block_keys, width), head)
+            query = k.query[head, rows]
+            grad_rows = k.grad_in[head]
+            key = k.key_in[head, key_rows]
+            probs = jnp.exp(dot_rt(key, query))
+            back = (probs * dot_rt(k.value_in[head, key_rows], grad_rows)).astype(BF)
+            zeros = jnp.zeros((size, width), BF)
+            k.grads[key_rows, 2 * width :] += dot(probs.astype(BF), jnp.where(own, grad_rows, zeros))
+            k.grads[key_rows, width : 2 * width] += dot(back, jnp.where(own, query, zeros))
+            k.query_grad[...] += dot_lt(back, jnp.where(own_keys, key, jnp.zeros((block_keys, width), BF)))
+        return carry
+
+    lax.fori_loop(0, keys // block_keys, visit, 0)
+    k.grads[rows, :width] = k.query_grad[...]
+
+
+def leave_heads(k, level, rows, target):
+    width = 2 * HD
+    average = averager(2 * width)
+    values = k.raw_in[rows]
+    centered = values - dot_fine(values, average)
+    scale = lax.rsqrt(dot_fine(centered * centered, average) + EPSILON)
+    normed = centered * scale
+    lane = lax.broadcasted_iota(jnp.int32, normed.shape, 1)
+    found = k.grads[rows, : 2 * width] * jnp.where(lane < width, HD**-0.5, 1.0)
+    k.head_small[0:1] += jnp.sum(found * normed, axis=0, keepdims=True)
+    k.head_small[1:2] += jnp.sum(found, axis=0, keepdims=True)
+    scaled = found * k.head_gains[level : level + 1]
+    back = scale * (scaled - dot_fine(scaled, average) - normed * dot_fine(scaled * normed, average))
+    parts = unpack_queries_keys(back[:, :width], back[:, width:], k.grads[rows, 2 * width :])
+    for number, part in enumerate(parts):
+        target[:, number * width : (number + 1) * width] = part.astype(BF)
+
+
+def backward_kernel(is_first, k):
+    spot = k.spot
+    block = 1 if is_first else 0
+    spot.greet(spot.over_x, spot.over_z, spot.core, spot.over_y, spot.over_h, *((spot.partner,) if is_first else ()))
+    gather, scatter, onward = Gather(spot, k.gather), Scatter(spot, k.local, k.one), Gather(spot, k.gather_next)
+    rows_of = gather.span
+    size = gather.held.shape[1]
+    tokens = 8 * size
+    keys = tokens if is_first else FRAME_TOK
+    sums = [
+        Total(spot, grad.at[rows], whole.at[rows], refs)
+        for (grad, whole), pieces in (
+            ((k.down_grad, k.down_whole), zip(pieces_of(k.down_grad), k.down_total)),
+            ((k.up_grad, k.up_whole), zip(pieces_of(k.up_grad), k.up_total)),
+        )
+        for rows, refs in pieces
+    ]
+    k.small[...] = jnp.zeros_like(k.small)
+    if is_first:
+        layer = Swap(spot, k.state, k.layer_out, k.swap)
+        k.loads.cotangent.wait()
+    else:
+        above = Scatter(spot, k.local, k.two)
+        qkv = Total(spot, k.qkv_grad, k.qkv_whole, k.qkv_total)
+        out = Total(spot, k.out_grad_in, k.out_whole, k.out_total)
+        out.start()
+        k.loads.above_qkv.wait()
+        k.loads.qkv_weight.wait()
+        above.produce(lambda slot, stream: dot_rt(k.above_qkv[slot, rows_of(stream)], k.qkv_weight[...]))
+        gathered = pltpu.make_async_copy(k.gathered, k.shared, k.pick.at[0])
+        gathered.start()
+        out.add()
+        gathered.wait()
+        qkv_weight_grad(k, k.shared)
+        qkv.start()
+        k.loads.above_hidden.wait()
+        k.loads.above_middle_grad.wait()
+    k.loads.branch_two.wait()
+    for stream in range(2):
+        rows = rows_of(stream)
+        if is_first:
+            grad = k.cotangent[rows].astype(F32) * k.weighting[rows, 0:1]
+        else:
+            normed, scale = norm_parts(k.above_hidden[rows])
+            grad, gain_term, offset_term = norm_back(above.result(stream), k.gains[1, 0:1], normed, scale)
+            k.small[6:7] += gain_term
+            k.small[7:8] += offset_term
+            grad = grad + k.above_middle_grad[rows]
+        k.grad_rows[rows] = grad
+        scaled = k.gains[block, 3:4] * grad
+        gather.put(stream, scaled.astype(BF))
+        k.small[0:1] += jnp.sum(grad * k.branch_two[rows], axis=0, keepdims=True)
+        k.small[1:2] += jnp.sum(scaled, axis=0, keepdims=True)
+        if stream == 0:
+            if not is_first:
+                above.relay(1)
+            gather.pass_on(0)
+    second = pltpu.make_async_copy(k.second, k.shared, k.pick.at[1])
+    second.start()
+    if is_first:
+        middle_rows, branch_rows, fetched = k.middle, k.branch, [k.loads.middle, k.loads.branch]
+    else:
+        middle_rows, branch_rows = k.above_hidden, k.above_middle_grad
+        fetched = [
+            pltpu.make_async_copy(k.middle, middle_rows, k.pick.at[2]),
+            pltpu.make_async_copy(k.branch, branch_rows, k.pick.at[3]),
+        ]
+        for copy in fetched:
+            copy.start()
+    if is_first:
+        layer.start()
+    else:
+        above.finish()
+        qkv.add()
+        out.add_over()
+    k.loads.down_weight.wait()
+    k.loads.up_weight.wait()
+    k.loads.slope.wait()
+
+    def term(slot, stream):
+        slope = k.slope[slot, rows_of(stream)].astype(F32)
+        up_rows = (dot_rt(gather.part(slot, stream), k.down_weight[...]) * slope).astype(BF)
+        k.up_rows[slot, rows_of(stream)] = up_rows
+        return dot_rt(up_rows, k.up_weight[...])
+
+    scatter.produce_from(gather, term)
+    gather.finish()
+    for copy in fetched:
+        copy.wait()
+    k.loads.activated.wait()
+
+    def down_piece(piece):
+        cut = k.down_grad.shape[0] // 2
+        lanes = slice(piece * cut, (piece + 1) * cut)
+        rows = k.activated[:, :, lanes].reshape(tokens, cut)
+        k.down_grad[lanes] = dot_lt(rows, wide(gather.held)).astype(BF)
+        sums[piece].start()
+
+    def up_piece(piece):
+        cut = k.shared.shape[2] // 2
+        lanes = slice(piece * cut, (piece + 1) * cut)
+        rows = k.shared[:, :, lanes].reshape(tokens, cut)
+        k.up_grad[lanes] = dot_lt(rows, wide(k.up_rows)).astype(BF)
+        if piece == 1:
+            total = jnp.sum(wide(k.up_rows).astype(F32), axis=0, keepdims=True)
+            row = lax.broadcasted_iota(jnp.int32, (k.up_grad.shape[0] - 2 * cut, k.up_grad.shape[1]), 0)
+            k.up_grad[2 * cut :] = jnp.where(row == 0, total, 0.0).astype(BF)
+        sums[2 + piece].start()
+
+    def leave_rows(stream):
+        rows = rows_of(stream)
+        normed, scale = norm_parts(middle_rows[rows])
+        grad, gain_term, offset_term = norm_back(scatter.result(stream), k.gains[block, 1:2], normed, scale)
+        grad = grad + k.grad_rows[rows]
+        k.middle_grad[rows] = grad
+        scaled = k.gains[block, 2:3] * grad
+        onward.put(stream, scaled.astype(BF))
+        k.small[2:3] += gain_term
+        k.small[3:4] += offset_term
+        k.small[4:5] += jnp.sum(grad * branch_rows[rows], axis=0, keepdims=True)
+        k.small[5:6] += jnp.sum(scaled, axis=0, keepdims=True)
+
+    down_piece(0)
+    scatter.relay(1)
+    leave_rows(0)
+    down_piece(1)
+    second.wait()
+    up_piece(0)
+    up_piece(1)
+    onward.pass_on(0)
+    leave_rows(1)
+    if not is_first:
+        qkv.add_over()
+        out.relay()
+    k.saves.middle_grad()
+    if not is_first:
+        early = SmallSum(spot, k.early, k.early_sum)
+        lanes = 4 * HD
+        k.early[0:8] = k.small_first[...]
+        k.early[8:16] = k.small[...]
+        k.early[16:24] = jnp.zeros_like(k.early[16:24])
+        k.early[16:17, :lanes] = k.head_first[0:1]
+        k.early[16:17, lanes : 2 * lanes] = k.head_first[1:2]
+        early.step(0)
+    scatter.finish()
+    k.loads.out_weight.wait()
+    k.loads.qk_in.wait()
+    k.loads.v_in.wait()
+    k.loads.query.wait()
+    k.loads.exact.wait()
+    k.grads[...] = jnp.zeros_like(k.grads)
+
+    def prepare(index, carry):
+        prepare_keys(k, pl.ds(pl.multiple_of(index * size, size), size))
+        return carry
+
+    lax.fori_loop(0, 8, prepare, 0)
+
+    def use(slot):
+        grad = dot_rt(onward.held[slot], k.out_weight[...]).astype(BF).astype(F32)
+        slice_back(k, keys, 512, slot * size, size, grad)
+
+    def visit(step, carry):
+        for stream in range(2):
+            onward.arrive(stream, step)
+        use(spot.slot(spot.c, step))
+
+        @pl.when(step == 0)
+        def _():
+            onward.pass_on(1)
+            sums[0].add()
+            sums[1].add()
+
+        for stream in range(2):
+            onward.arrive_core(stream, step)
+        use(spot.slot(1 - spot.c, step))
+
+        @pl.when(step == 0)
+        def _():
+            sums[2].add()
+            if not is_first:
+                qkv.relay()
+                early.step(1)
+
+        @pl.when(step == 1)
+        def _():
+            sums[3].add()
+            sums[0].add_over()
+            if not is_first:
+                early.step(2)
+
+        @pl.when(step == 2)
+        def _():
+            sums[1].add_over()
+            if not is_first:
+                early.step(3)
+
+        @pl.when(step == 3)
+        def _():
+            sums[2].add_over()
+            sums[0].relay()
+            sums[1].relay()
+            if not is_first:
+                early.step(4)
+
+        return carry
+
+    lax.fori_loop(0, 4, visit, 0)
+    k.out_grad[...] = dot_lt(k.exact[...].astype(BF), wide(onward.held)).astype(BF)
+    k.saves.out_grad()
+    k.loads.raw_in.wait()
+    k.head_small[...] = jnp.zeros_like(k.head_small)
+    qkv_rows = k.qkv_rows if is_first else k.above_qkv
+
+    def leave(index, carry):
+        leave_heads(k, block, pl.ds(pl.multiple_of(index * size, size), size), qkv_rows.at[index])
+        return carry
+
+    lax.fori_loop(0, 8, leave, 0)
+    k.saves.grad_qkv(qkv_rows)
+    onward.finish()
+    if not is_first:
+        early.step(5)
+    sums[3].add_over()
+    sums[2].relay()
+    sums[3].relay()
+    if is_first:
+        layer.arrive()
+        layer.finish()
+    else:
+        sums += [qkv, out]
+    for total in sums:
+        total.finish()
+
+
+def last_kernel(k):
+    spot = k.spot
+    spot.greet(
+        spot.over_x, spot.over_z, spot.core, spot.over_y, spot.over_h, spot.partner, *QuickSum.partners(spot)
+    )
+    scatter = Scatter(spot, k.local, k.one)
+    out = Total(spot, k.out_grad_in, k.out_whole, k.out_total)
+    pieces = pieces_of(k.qkv_grad)
+    sums = [
+        Total(spot, k.qkv_grad.at[rows], k.qkv_whole.at[rows], refs) for rows, refs in zip(pieces, k.qkv_total)
+    ]
+    out.start()
+    k.loads.qkv_weight.wait()
+    k.loads.above_qkv.wait()
+    scatter.produce(lambda slot, stream: dot_rt(k.above_qkv[slot, scatter.span(stream)], k.qkv_weight[...]))
+    late = QuickSum(spot, k.late, k.late_sum)
+    k.loads.gathered.wait()
+    rows = wide(k.above_qkv)
+    cut = k.gathered.shape[2] // 2
+    k.qkv_grad[:cut] = dot_lt(k.gathered[:, :, :cut].reshape(rows.shape[0], cut), rows).astype(BF)
+    sums[0].start()
+    scatter.relay(1)
+    out.add()
+    k.qkv_grad[cut : 2 * cut] = dot_lt(k.gathered[:, :, cut:].reshape(rows.shape[0], cut), rows).astype(BF)
+    total = jnp.sum(rows.astype(F32), axis=0, keepdims=True)
+    row = lax.broadcasted_iota(jnp.int32, (k.qkv_grad.shape[0] - 2 * cut, k.qkv_grad.shape[1]), 0)
+    k.qkv_grad[2 * cut :] = jnp.where(row == 0, total, 0.0).astype(BF)
+    sums[1].start()
+    lanes = 4 * HD
+    k.late[...] = jnp.zeros_like(k.late)
+    k.late[2:3, :lanes] = k.head_later[0:1]
+    k.late[2:3, lanes : 2 * lanes] = k.head_later[1:2]
+    k.loads.hidden.wait()
+    k.loads.middle_grad.wait()
+    swaps = []
+    for stream in range(2):
+        span = scatter.span(stream)
+        normed, scale = norm_parts(k.hidden[span].astype(F32))
+        grad, gain_term, offset_term = norm_back(scatter.result(stream), k.gains[0, 0:1], normed, scale)
+        k.late[0:1] += gain_term
+        k.late[1:2] += offset_term
+        k.grad_in[span] = (grad + k.middle_grad[span]).astype(BF)
+        swap = Swap(spot, k.grad_in.at[span], k.input_grad.at[span], k.swaps[stream])
+        swap.start()
+        swaps.append(swap)
+        if stream == 0:
+            sums[0].add()
+    late.start()
+    sums[1].add()
+    out.add_over()
+    late.step()
+    sums[0].add_over()
+    out.relay()
+    late.end()
+    sums[1].add_over()
+    sums[0].relay()
+    sums[1].relay()
+    for swap in swaps:
+        swap.arrive()
+        swap.finish()
+    for part in sums:
+        part.finish()
+    out.finish()
+    scatter.finish()
+
+
+class Own:
+    def __init__(self, own, level, got):
+        self.own, self.level, self.got = own, level, got
+
+
+class Load:
+    def __init__(self, values):
+        self.values = values
+
+
+class Outside(Load):
+    pass
+
+
+INSIDE, APART, SAVED, TARGET = range(4)
+
+
+def run(kernel, number, inputs, outputs, scratch):
+    operands, in_specs = [], []
+    vmem, outside = pl.BlockSpec(memory_space=pltpu.VMEM), pl.BlockSpec(memory_space=pl.ANY)
+    loaded, places = {}, {}
+
+    def give(values, spec):
+        operands.append(values)
+        in_specs.append(spec)
+        return len(operands) - 1
+
+    for key, value in inputs.items():
+        if isinstance(value, Own):
+            places[key] = (give(value.own, outside), give(value.got, outside))
+            loaded[key] = value.own.shape[1:], value.own.dtype
+        elif isinstance(value, Load):
+            places[key] = give(value.values, outside)
+            if not isinstance(value, Outside):
+                loaded[key] = value.values.shape, value.values.dtype
+        else:
+            places[key] = give(value, vmem)
+    out_keys = list(outputs)
+    kinds = [outputs[key][1] for key in out_keys]
+    saved = [key for key, kind in zip(out_keys, kinds) if kind in (SAVED, TARGET)]
+    shapes = []
+
+    def hold(item):
+        if isinstance(item, list):
+            return [hold(part) for part in item]
+        shapes.append(item)
+        return len(shapes) - 1
+
+    layout = {key: hold(item) for key, item in scratch.items()}
+    load_layout = {key: hold(pltpu.VMEM(size, kind)) for key, (size, kind) in loaded.items()}
+    for key, kind in zip(out_keys, kinds):
+        if kind == SAVED:
+            layout[key] = hold(pltpu.VMEM(outputs[key][0].shape, outputs[key][0].dtype))
+    load_at, save_at = hold(DMA((max(len(loaded), 1),))), hold(DMA((max(len(saved), 1),)))
+
+    def whole(*refs):
+        ins, rest = refs[: len(operands)], refs[len(operands) :]
+        outs, held = rest[: len(out_keys)], rest[len(out_keys) :]
+
+        def find(item):
+            return [find(part) for part in item] if isinstance(item, list) else held[item]
+
+        k = types.SimpleNamespace(**{key: find(item) for key, item in layout.items()})
+        k.spot = Spot()
+        saving = []
+        loads, saves = {}, {}
+
+        def saver(ref, target, sem):
+            def save(source=ref):
+                copy = pltpu.make_async_copy(source, target, sem)
+                copy.start()
+                saving.append(copy)
+
+            return save
+
+        for key, kind, out in zip(out_keys, kinds, outs):
+            if kind in (INSIDE, APART):
+                setattr(k, key, out)
+            else:
+                saves[key] = saver(getattr(k, key, None), out, held[save_at].at[saved.index(key)])
+        for place, key in enumerate(loaded):
+            target, sem = held[load_layout[key]], held[load_at].at[place]
+            setattr(k, key, target)
+            if isinstance(inputs[key], Own):
+                own, got = (ins[at] for at in places[key])
+                copy = pltpu.make_async_copy(got, target, sem)
+                pl.when(k.spot.home)(pltpu.make_async_copy(own.at[inputs[key].level], target, sem).start)
+                pl.when(k.spot.away)(copy.start)
+            else:
+                copy = pltpu.make_async_copy(ins[places[key]], target, sem)
+                copy.start()
+            loads[key] = copy
+        for key in inputs:
+            if key not in loaded:
+                setattr(k, key, ins[places[key]])
+        k.loads, k.saves = types.SimpleNamespace(**loads), types.SimpleNamespace(**saves)
+        kernel(k)
+        for copy in saving:
+            copy.wait()
+
+    found = pl.pallas_call(
+        whole,
+        name=getattr(kernel, "func", kernel).__name__,
+        out_shape=[outputs[key][0] for key in out_keys],
+        in_specs=in_specs,
+        out_specs=[vmem if kind == INSIDE else outside for kind in kinds],
+        scratch_shapes=shapes,
+        compiler_params=pltpu.CompilerParams(
+            collective_id=number, has_side_effects=True, vmem_limit_bytes=VMEM_LIMIT
+        ),
+    )(*operands)
+    return types.SimpleNamespace(**dict(zip(out_keys, found)))
+
+
+def shape(*sizes):
+    return jax.ShapeDtypeStruct(sizes[:-1], sizes[-1])
+
+
+def square_body(
+    frames_in,
+    qkv_weight,
+    qkv_bias,
+    out_weight,
+    up_weight,
+    up_bias,
+    down_weight,
+    norm_gain,
+    norm_offset,
+    head_gain,
+    head_offset,
+    cotangent,
+    visible,
+    query_count,
+):
+    rows, width = frames_in.shape[1:]
+    tokens = 8 * rows
+    inner = 2 * HD
+    units = up_weight.shape[2]
+    gather = Gather.scratch(rows, width)
+    local, scatter = Scatter.local(rows, width), Scatter.scratch(rows, width)
+    pad = 32
+
+    def moved(weight):
+        return shape(*weight.shape[1:], BF), APART
+
+    def flat(values):
+        return values.reshape(tokens, values.shape[2])
+
+    biases = jnp.concatenate([qkv_bias, up_bias], axis=1).astype(F32)
+    biases = jnp.pad(biases, ((0, 6), (0, 0)))
+    weighting = visible[0].astype(F32) * (query_count[0].astype(F32) / QMAX)
+    weighting = jnp.broadcast_to(weighting[:, None], (rows, 128))
+    head_gains, head_offsets = (
+        jnp.concatenate([pair[:, 0], pair[:, 0], pair[:, 1], pair[:, 1]], axis=1) for pair in (head_gain, head_offset)
+    )
+    norms = dict(gains=norm_gain, offsets=norm_offset)
+    heads = dict(head_gains=head_gains, head_offsets=head_offsets)
+    qkv_outs = dict(
+        gathered=(shape(8, rows, width, BF), TARGET),
+        raw=(shape(8, rows, 2 * inner, F32), SAVED),
+        qk=(shape(8, rows, 2 * inner, BF), SAVED),
+        v=(shape(8, rows, inner, BF), SAVED),
+    )
+    entry = run(
+        first_kernel,
+        0,
+        dict(
+            frames=Outside(frames_in),
+            own_biases=biases,
+            qkv_own=Outside(qkv_weight),
+            out_own=Outside(out_weight),
+            up_own=Outside(up_weight),
+            **norms,
+            **heads,
+        ),
+        dict(
+            hidden=(shape(rows, width, BF), SAVED),
+            biases=(shape(*biases.shape, F32), INSIDE),
+            qkv_got=moved(qkv_weight),
+            out_got=moved(out_weight),
+            up_got=moved(up_weight),
+            **qkv_outs,
+        ),
+        dict(
+            gather=gather,
+            swaps=[Swap.scratch] * 3,
+            moves=[Move.scratch] * 3,
+            qkv_weight=pltpu.VMEM(qkv_weight.shape[1:], BF),
+            pick=DMA,
+        ),
+    )
+    biases = entry.biases
+    down_buffer = pltpu.VMEM(down_weight.shape[1:], BF)
+
+    def forward(is_last, came, **extra):
+        inputs, outputs, scratch = extra.pop("inputs"), extra.pop("outputs"), extra.pop("scratch")
+        block = 1 if is_last else 0
+        return run(
+            functools.partial(forward_kernel, is_last),
+            1 + block,
+            dict(
+                qk_in=Load(flat(came.qk)),
+                v_in=Load(flat(came.v)),
+                hidden=Load(came.hidden),
+                down_own=Outside(down_weight),
+                biases=biases,
+                **norms,
+                **inputs,
+            ),
+            dict(
+                exact=(shape(tokens, inner, F32), SAVED),
+                query=(shape(2, tokens, inner, BF), SAVED),
+                branch=(shape(rows, width, F32), SAVED),
+                middle=(shape(rows, width, F32), SAVED),
+                second=(shape(8, rows, width, BF), TARGET),
+                activated=(shape(8, rows, units, BF), SAVED),
+                slope=(shape(8, rows, units, BF), SAVED),
+                branch_two=(shape(rows, width, F32), SAVED),
+                state=(shape(rows, width, BF if is_last else F32), SAVED),
+                down_got=moved(down_weight),
+                **outputs,
+            ),
+            dict(
+                local=local,
+                one=scatter,
+                two=scatter,
+                gather=gather,
+                pick=DMA((2,)),
+                mixed=pltpu.VMEM((tokens, inner), BF),
+                down_weight=down_buffer,
+                **scratch,
+            ),
+        )
+
+    lower = forward(
+        False,
+        entry,
+        inputs=dict(
+            out_weight=Own(out_weight, 0, entry.out_got),
+            up_weight=Own(up_weight, 0, entry.up_got),
+            qkv_own=Outside(qkv_weight),
+            out_own=Outside(out_weight),
+            **heads,
+        ),
+        outputs=dict(qkv_got=moved(qkv_weight), out_got=moved(out_weight), **qkv_outs),
+        scratch=dict(gather_next=gather, qkv_weight=pltpu.VMEM(qkv_weight.shape[1:], BF), moves=[Move.scratch] * 3),
+    )
+    between = types.SimpleNamespace(hidden=lower.state, **{key: getattr(lower, key) for key in qkv_outs})
+    upper = forward(
+        True,
+        between,
+        inputs=dict(
+            out_weight=Own(out_weight, 1, lower.out_got),
+            up_own=Outside(up_weight),
+            cotangent=Outside(cotangent),
+            weighting=weighting,
+        ),
+        outputs=dict(
+            up_got=moved(up_weight),
+            cotangent_here=(shape(rows, width, BF), APART),
+            weighting_here=(shape(rows, 128, F32), APART),
+        ),
+        scratch=dict(
+            swaps=[Swap.scratch] * 2, up_weight=pltpu.VMEM(up_weight.shape[1:], BF), moves=[Move.scratch] * 2
+        ),
+    )
+
+    qkv_grad = pltpu.VMEM((width + pad, 3 * inner), BF)
+
+    def in_pieces(size, lanes):
+        cut = size // 64 * 32
+        return [Total.scratch(cut, lanes), Total.scratch(size - cut, lanes)]
+
+    qkv_whole = dict(qkv_whole=(shape(width + pad, 3 * inner, BF), APART))
+    out_whole = dict(out_whole=(shape(inner, width, BF), APART))
+    out_total = dict(out_total=Total.scratch(inner, width))
+
+    def backward(is_first, came, kept, up_got, out_got, inputs, outputs, scratch):
+        block = 1 if is_first else 0
+        return run(
+            functools.partial(backward_kernel, is_first),
+            3 + block,
+            dict(
+                **inputs,
+                branch_two=Load(kept.branch_two),
+                down_weight=Own(down_weight, block, kept.down_got),
+                up_weight=Own(up_weight, block, up_got),
+                slope=Load(kept.slope),
+                activated=Load(kept.activated),
+                second=Outside(kept.second),
+                out_weight=Own(out_weight, block, out_got),
+                qk_in=Load(flat(came.qk)),
+                v_in=Load(flat(came.v)),
+                query=Load(kept.query),
+                exact=Load(kept.exact),
+                raw_in=Load(flat(came.raw)),
+                gains=norm_gain,
+                head_gains=head_gains,
+            ),
+            dict(
+                middle_grad=(shape(rows, width, F32), SAVED),
+                grad_qkv=(shape(8, rows, 3 * inner, BF), TARGET),
+                out_grad=(shape(inner, width, BF), SAVED),
+                down_whole=(shape(units, width, BF), APART),
+                up_whole=(shape(width + pad, units, BF), APART),
+                small=(shape(8, width, F32), INSIDE),
+                head_small=(shape(2, 2 * inner, F32), INSIDE),
+                **outputs,
+            ),
+            dict(
+                local=local,
+                one=scatter,
+                gather=gather,
+                gather_next=gather,
+                up_rows=pltpu.VMEM((8, rows, units), BF),
+                grad_rows=pltpu.VMEM((rows, width), F32),
+                shared=pltpu.VMEM((8, rows, width), BF),
+                pick=DMA((4,)),
+                down_grad=pltpu.VMEM((units, width), BF),
+                up_grad=pltpu.VMEM((width + pad, units), BF),
+                down_total=in_pieces(units, width),
+                up_total=in_pieces(width + pad, units),
+                key_in=pltpu.VMEM((2, tokens, inner), BF),
+                value_in=pltpu.VMEM((2, tokens, inner), BF),
+                grad_in=pltpu.VMEM((2, rows, inner), BF),
+                query_grad=pltpu.VMEM((rows, inner), F32),
+                grads=pltpu.VMEM((tokens, 3 * inner), F32),
+                **scratch,
+            ),
+        )
+
+    upper_back = backward(
+        True,
+        between,
+        upper,
+        upper.up_got,
+        lower.out_got,
+        dict(
+            cotangent=Load(upper.cotangent_here),
+            weighting=upper.weighting_here,
+            state=Outside(upper.state),
+            middle=Load(upper.middle),
+            branch=Load(upper.branch),
+        ),
+        dict(layer_out=(shape(rows, width, BF), APART)),
+        dict(swap=Swap.scratch, qkv_rows=pltpu.VMEM((8, rows, 3 * inner), BF)),
+    )
+    lower_back = backward(
+        False,
+        entry,
+        lower,
+        entry.up_got,
+        entry.out_got,
+        dict(
+            above_qkv=Load(upper_back.grad_qkv),
+            qkv_weight=Own(qkv_weight, 1, lower.qkv_got),
+            gathered=Outside(between.gathered),
+            above_hidden=Load(between.hidden),
+            above_middle_grad=Load(upper_back.middle_grad),
+            out_grad_in=upper_back.out_grad,
+            middle=Outside(lower.middle),
+            branch=Outside(lower.branch),
+            small_first=upper_back.small,
+            head_first=upper_back.head_small,
+        ),
+        dict(early=(shape(24, width, F32), INSIDE), **qkv_whole, **out_whole),
+        dict(
+            early_sum=SmallSum.scratch(24, width),
+            two=scatter,
+            qkv_grad=qkv_grad, qkv_total=Total.scratch(width + pad, 3 * inner), **out_total),
+    )
+    last = run(
+        last_kernel,
+        5,
+        dict(
+            above_qkv=Load(lower_back.grad_qkv),
+            qkv_weight=Own(qkv_weight, 0, entry.qkv_got),
+            gathered=Load(entry.gathered),
+            hidden=Load(entry.hidden),
+            middle_grad=Load(lower_back.middle_grad),
+            out_grad_in=lower_back.out_grad,
+            gains=norm_gain,
+            head_later=lower_back.head_small,
+        ),
+        dict(
+            input_grad=(shape(rows, width, BF), APART),
+            late=(shape(8, width, F32), INSIDE),
+            **qkv_whole,
+            **out_whole,
+        ),
+        dict(
+            local=local,
+            one=scatter,
+            grad_in=pltpu.VMEM((rows, width), BF),
+            swaps=[Swap.scratch] * 2,
+            late_sum=QuickSum.scratch(8, width),
+            qkv_grad=qkv_grad,
+            qkv_total=in_pieces(width + pad, 3 * inner),
+            **out_total,
+        ),
+    )
+    early, late = lower_back.early, last.late
+    gains = [late[0], early[10], early[12], early[8], early[14], early[2], early[4], early[0]]
+    offsets = [late[1], early[11], early[13], early[9], early[15], early[3], early[5], early[1]]
+    head_sums = jnp.stack([late[2, : 8 * HD], early[16, : 8 * HD]]).reshape(2, 2, 2, 2, HD).sum(axis=3)
+
+    def joined(first, later, part):
+        return jnp.stack([first[part], later[part]]).astype(F32)
+
+    qkv_sums, up_sums = (last.qkv_whole, lower_back.qkv_whole), (lower_back.up_whole, upper_back.up_whole)
+    inside = slice(width)
+    return (
+        upper_back.layer_out[None],
+        last.input_grad[None],
+        joined(*qkv_sums, inside),
+        joined(*qkv_sums, width),
+        joined(last.out_whole, lower_back.out_whole, inside),
+        joined(*up_sums, inside),
+        joined(*up_sums, width),
+        joined(lower_back.down_whole, upper_back.down_whole, inside),
+        jnp.stack(gains).reshape(2, 4, width),
+        jnp.stack(offsets).reshape(2, 4, width),
+        head_sums[:, 0],
+        head_sums[:, 1],
+    )
+
+
+TP = ("c", "r")
+
+
+def exchange(values):
+    return lax.ppermute(values, ("c", "h"), [(0, 0), (1, 2), (2, 1), (3, 3)])
 
 
 def layer_norm(values, norm_scale, norm_bias):
@@ -112,7 +1745,7 @@
     return (grad_query.reshape(queries.shape), grad_key, grad_value)
 
 
-def body(
+def any_body(
     frames_in,
     qkv_weight,
     qkv_bias,
@@ -129,6 +1762,14 @@
     query_count,
 ):
     score_scale = HD ** (-0.5)
+    frames = exchange(frames_in[0])
+    qkv_weight, out_weight, up_weight, down_weight, qkv_bias, up_bias = (
+        [exchange(stacked[block_index]) for block_index in range(2)]
+        for stacked in (qkv_weight, out_weight, up_weight, down_weight, qkv_bias, up_bias)
+    )
+    weighting = visible[0].astype(jnp.float32) * (query_count[0].astype(jnp.float32) / QMAX)
+    weighting = exchange(weighting)
+    cotangent = exchange(cotangent[0])
 
     def backward_block(grad_out, block_index, frame_only, saved):
         (
@@ -153,7 +1794,7 @@
         grad_branch_two = gains[3] * grad_out
         offset_grad_three = jnp.sum(grad_branch_two, axis=0)
         gain_grad_three = jnp.sum(grad_out * branch_two, axis=0)
-        shard_rows = lax.all_gather(grad_branch_two.astype(jnp.bfloat16), "tp", axis=0, tiled=True)
+        shard_rows = lax.all_gather(grad_branch_two.astype(jnp.bfloat16), TP, axis=0, tiled=True)
         down_grad = jnp.einsum(
             "tf,td->fd", activated, shard_rows, preferred_element_type=jnp.float32
         )
@@ -170,7 +1811,7 @@
             jnp.einsum(
                 "tf,df->td", up_grads, up_weight[block_index], preferred_element_type=jnp.float32
             ).astype(jnp.bfloat16),
-            "tp",
+            TP,
             scatter_dimension=0,
             tiled=True,
         ).astype(jnp.float32)
@@ -181,7 +1822,7 @@
         grad_branch = gains[2] * middle_grad
         offset_grad_two = jnp.sum(grad_branch, axis=0)
         gain_grad_two = jnp.sum(middle_grad * branch, axis=0)
-        shard_rows = lax.all_gather(grad_branch.astype(jnp.bfloat16), "tp", axis=0, tiled=True)
+        shard_rows = lax.all_gather(grad_branch.astype(jnp.bfloat16), TP, axis=0, tiled=True)
         out_grad = jnp.einsum(
             "tc,td->cd", mixed_flat, shard_rows, preferred_element_type=jnp.float32
         )
@@ -220,7 +1861,7 @@
                 qkv_weight[block_index],
                 preferred_element_type=jnp.float32,
             ).astype(jnp.bfloat16),
-            "tp",
+            TP,
             scatter_dimension=0,
             tiled=True,
         ).astype(jnp.float32)
@@ -244,14 +1885,14 @@
         )
         return (hidden_grad, large_grads, small_grads)
 
-    hidden = frames_in[0].astype(jnp.float32)
+    hidden = frames.astype(jnp.float32)
     kept_states = []
     for block_index in range(2):
         forward_frame_only = block_index == 0
         forward_gains = norm_gain[block_index]
         forward_offsets = norm_offset[block_index]
         normed = layer_norm(hidden, forward_gains[0], forward_offsets[0]).astype(jnp.bfloat16)
-        forward_gathered = lax.all_gather(normed, "tp", axis=0, tiled=True)
+        forward_gathered = lax.all_gather(normed, TP, axis=0, tiled=True)
         projected = jnp.dot(
             forward_gathered, qkv_weight[block_index], preferred_element_type=jnp.float32
         )
@@ -274,7 +1915,7 @@
                 jnp.dot(
                     forward_mixed_flat, out_weight[block_index], preferred_element_type=jnp.float32
                 ).astype(jnp.bfloat16),
-                "tp",
+                TP,
                 scatter_dimension=0,
                 tiled=True,
             ).astype(jnp.float32)
@@ -284,7 +1925,7 @@
         second = layer_norm(forward_middle, forward_gains[1], forward_offsets[1]).astype(
             jnp.bfloat16
         )
-        forward_gathered_two = lax.all_gather(second, "tp", axis=0, tiled=True)
+        forward_gathered_two = lax.all_gather(second, TP, axis=0, tiled=True)
         forward_hidden_up = jnp.dot(
             forward_gathered_two, up_weight[block_index], preferred_element_type=jnp.float32
         )
@@ -295,7 +1936,7 @@
                 jnp.dot(
                     forward_activated, down_weight[block_index], preferred_element_type=jnp.float32
                 ).astype(jnp.bfloat16),
-                "tp",
+                TP,
                 scatter_dimension=0,
                 tiled=True,
             ).astype(jnp.float32)
@@ -321,36 +1962,33 @@
         hidden = result
         saved = forward_saved
         kept_states.append(saved)
-    layer_out = hidden.astype(jnp.bfloat16)[None]
-    grad_hidden = (
-        cotangent[0].astype(jnp.float32)
-        * visible[0].astype(jnp.float32)[:, None]
-        * (query_count[0].astype(jnp.float32) / QMAX)
-    )
+    layer_out = exchange(hidden.astype(jnp.bfloat16))[None]
+    grad_hidden = cotangent.astype(jnp.float32) * weighting[:, None]
     grad_hidden, large_one, small_one = backward_block(grad_hidden, 1, False, kept_states[1])
     grad_hidden, large_zero, small_zero = backward_block(grad_hidden, 0, True, kept_states[0])
-    input_grad = grad_hidden.astype(jnp.bfloat16)[None]
-
-    def stack_pair(first, later):
-        return jnp.stack([first, later])
-
-    qkv_w_part, qkv_b_part, out_w_part, up_w_part, up_b_part, down_w_part = jax.tree.map(
-        stack_pair, large_zero, large_one
-    )
-    gain_part, offset_part, head_gain_part, head_offset_part = jax.tree.map(
-        stack_pair, small_zero, small_one
-    )
-    summed = (
-        lax.psum(qkv_w_part.astype(jnp.bfloat16), "scene").astype(jnp.float32),
-        lax.psum(qkv_b_part.astype(jnp.bfloat16), "scene").astype(jnp.float32),
-        lax.psum(out_w_part.astype(jnp.bfloat16), "scene").astype(jnp.float32),
-        lax.psum(up_w_part.astype(jnp.bfloat16), "scene").astype(jnp.float32),
-        lax.psum(up_b_part.astype(jnp.bfloat16), "scene").astype(jnp.float32),
-        lax.psum(down_w_part.astype(jnp.bfloat16), "scene").astype(jnp.float32),
-    )
-    summed = tuple(summed) + tuple(
-        lax.psum((gain_part, offset_part, head_gain_part, head_offset_part), ("scene", "tp"))
-    )
+    input_grad = exchange(grad_hidden.astype(jnp.bfloat16))[None]
+
+    def over_scenes(grads):
+        shapes = [grad.shape for grad in grads]
+        parts = lax.axis_size("sy")
+        flat = [grad.astype(jnp.bfloat16).reshape(parts, -1) for grad in grads]
+        sizes = [part.shape[1] for part in flat]
+        joined = jnp.concatenate(flat, axis=1)
+        share = lax.psum_scatter(joined, "sy", scatter_dimension=0, tiled=True)
+        share = lax.psum(share, "h")
+        whole = exchange(lax.all_gather(share, "sy", axis=0, tiled=True))
+        found = []
+        start = 0
+        for shape, size in zip(shapes, sizes):
+            found.append(whole[:, start : start + size].reshape(shape).astype(jnp.float32))
+            start += size
+        return found
+
+    summed_one = over_scenes(large_one)
+    summed_zero = over_scenes(large_zero)
+    summed = [jnp.stack(pair) for pair in zip(summed_zero, summed_one)]
+    small = jax.tree.map(lambda first, later: jnp.stack([first, later]), small_zero, small_one)
+    summed = tuple(summed) + tuple(lax.psum(small, ("sy", "c", "h", "r")))
     return (
         layer_out,
         input_grad,
@@ -368,34 +2006,40 @@
 
 
 def solution(mesh):
+    scenes, shards = mesh.shape["scene"], mesh.shape["tp"]
+    if (scenes, shards) == (4, 8):
+        body, sizes, axes, tp = square_body, (2, 2, 2, 2, 2), AXES, ("h", "zl", "x")
+    else:
+        body, sizes, axes, tp = any_body, (scenes // 2, 2, 2, shards // 2), ("sy", "c", "h", "r"), ("h", "r")
+    scene = ("sy", "c")
     return jax.shard_map(
         body,
-        mesh=mesh,
+        mesh=jax.sharding.Mesh(mesh.devices.reshape(sizes), axes),
         in_specs=(
-            P("scene", "tp", None),
-            P(None, None, "tp"),
-            P(None, "tp"),
-            P(None, "tp", None),
-            P(None, None, "tp"),
-            P(None, "tp"),
-            P(None, "tp", None),
+            P(scene, tp, None),
+            P(None, None, tp),
+            P(None, tp),
+            P(None, tp, None),
+            P(None, None, tp),
+            P(None, tp),
+            P(None, tp, None),
             P(),
             P(),
             P(),
             P(),
-            P("scene", "tp", None),
-            P("scene", "tp"),
-            P("scene"),
+            P(scene, tp, None),
+            P(scene, tp),
+            P(scene),
         ),
         out_specs=(
-            P("scene", "tp", None),
-            P("scene", "tp", None),
-            P(None, None, "tp"),
-            P(None, "tp"),
-            P(None, "tp", None),
-            P(None, None, "tp"),
-            P(None, "tp"),
-            P(None, "tp", None),
+            P(scene, tp, None),
+            P(scene, tp, None),
+            P(None, None, tp),
+            P(None, tp),
+            P(None, tp, None),
+            P(None, None, tp),
+            P(None, tp),
+            P(None, tp, None),
             P(),
             P(),
             P(),

time: 1930 us -> 594 us (0.31)
  waiting for transfers between devices: 1450 us -> 0 us
  Pallas kernels: 0 us -> 559 us
  matrix products: 209 us -> 0 us
  other arithmetic: 138 us -> 11.4 us
  local copies, waits for them, and re-layouts: 99.9 us -> 13.2 us
    reduce_scatter x8 -> x0, waiting for transfers between devices: 679 us -> none  [the longest x2 173 us: body(): lax.psum_scatter(jnp.dot(forward_activated, down_weight[block_index], pre...]
    pallas_call x0 -> x6, Pallas kernels: none -> 559 us  [run(): pl.pallas_call(whole, name=getattr(kernel, 'func', kernel).__name__, out_...]
    all_gather x8 -> x0, waiting for transfers between devices: 548 us -> none  [the longest x2 147 us: body(): forward_gathered = lax.all_gather(normed, 'tp', axis=0, tiled=True)]
    psum x2 -> x0, waiting for transfers between devices: 220 us -> none  [the longest x1 119 us: body(): lax.psum((gain_part, offset_part, head_gain_part, head_offset_part), ('sc...]
    dot_general x52 -> x0, matrix products: 209 us -> none  [the longest x2 30 us: body(): jnp.dot(forward_gathered_two, up_weight[block_index], preferred_element_t...]
    reduce_sum x43 -> x1, other arithmetic: 68.2 us -> 0.02 us  [square_body(): jnp.stack([late[2, :8 * HD], early[16, :8 * HD]]).reshape(2, 2, 2, 2, HD)]
    convert_element_type x23 -> x6, other arithmetic: 49.4 us -> 8.67 us  [joined(): return jnp.stack([first[part], later[part]]).astype(F32)]
    unnamed x358 -> x22, local copies, waits for them, and re-layouts: 27.1 us -> 2.19 us
  transfers between devices with their start and end apart: 18 -> 0, of which waited for: 18 -> 0; matrix products, arithmetic and copies ran while one was open for 4% -> 0% of each run, Pallas kernels for 0% -> 0%
where the time goes in v2:
time: 594 us; the launch traced here: 585 us
  Pallas kernels  559 us (94%)
  local copies, waits for them, and re-layouts  13.2 us (2%)
  other arithmetic  11.4 us (2%)
    pallas_call x6, Pallas kernels, run(): pl.pallas_call(whole, name=getattr(kernel, 'func', kernel).__name__, out_...  559 us

profile of v2, /device:TPU:0, one launch (start us, length us, event | category | flops | bytes accessed | tf_op | source)
XLA Modules:
  0.0 585.5 jit_solution(1832747140059526058)
XLA Ops:
  1.3 0.7 convert_multiply_fusion
  2.0 0.8 fusion.7
  2.7 0.8 fusion.6
  4.2 1.3 fusion.3.refs_1_
  5.5 0.8 broadcast_in_dim.12.refs_11_
  6.2 64.6 %first_kernel.1 = (bf16[256,1024]{1,0:T(8,128)(2,1)}, f32[8,896]{1,0:T(8,128)}, bf16[1024,384]{1,0:T(8,128)(2,1)}, bf16[128,1024]{1,0:T(8,128)(2,1)}, bf16[1024,...) custom-call(bf16[1,256,1024]{2,1,0:T(8,128)(2,1)} %refs_0_.1, ...), custom_call_target="tpu_custom_call" | custom-call | tf_op jit(solution)/shard_map/first_kernel/pallas_call | solution.py:1313
  70.9 108.9 %forward_kernel.2 = (f32[2048,128]{1,0:T(8,128)}, bf16[2,2048,128]{2,1,0:T(8,128)(2,1)}, f32[256,1024]{1,0:T(8,128)}, f32[256,1024]{1,0:T(8,128)}, bf16[8,256,10...) custom-call(bf16[2048,256]{1,0:T(8,128)(2,1)} %bitcast.30, ...), custom_call_target="tpu_custom_call" | custom-call | tf_op jit(solution)/shard_map/forward_kernel/pallas_call | solution.py:1313
  179.7 91.2 %forward_kernel.3 = (f32[2048,128]{1,0:T(8,128)}, bf16[2,2048,128]{2,1,0:T(8,128)(2,1)}, f32[256,1024]{1,0:T(8,128)}, f32[256,1024]{1,0:T(8,128)}, bf16[8,256,10...) custom-call(bf16[2048,256]{1,0:T(8,128)(2,1)} %bitcast.32, ...), custom_call_target="tpu_custom_call" | custom-call | tf_op jit(solution)/shard_map/forward_kernel/pallas_call | solution.py:1313
  270.9 111.3 %backward_kernel.2 = (f32[256,1024]{1,0:T(8,128)}, bf16[8,256,384]{2,1,0:T(8,128)(2,1)}, bf16[128,1024]{1,0:T(8,128)(2,1)}, bf16[512,1024]{1,0:T(8,128)(2,1)}, b...) custom-call(bf16[256,1024]{1,0:T(8,128)(2,1)} %get-tuple-element.81.refs_0_, ...), custom_call_target="tpu_custom_call" | custom-call | tf_op jit(solution)/shard_map/backward_kernel/pallas_call | solution.py:1313
  382.2 127.4 %backward_kernel.3 = (f32[256,1024]{1,0:T(8,128)}, bf16[8,256,384]{2,1,0:T(8,128)(2,1)}, bf16[128,1024]{1,0:T(8,128)(2,1)}, bf16[512,1024]{1,0:T(8,128)(2,1)}, b...) custom-call(bf16[8,256,384]{2,1,0:T(8,128)(2,1)} %get-tuple-element., ...), custom_call_target="tpu_custom_call" | custom-call | tf_op jit(solution)/shard_map/backward_kernel/pallas_call | solution.py:1313
  509.6 55.7 %last_kernel.1 = (bf16[256,1024]{1,0:T(8,128)(2,1)}, f32[8,1024]{1,0:T(8,128)}, bf16[1056,384]{1,0:T(8,128)(2,1)}, bf16[128,1024]{1,0:T(8,128)(2,1)}) custom-call(bf16[8,256,384]{2,1,0:T(8,128)(2,1)} %get-tuple-element.113.refs_0_, bf16[2,1024,384]{2,1,0:T(8,128)(2,1)} %refs_1_.3, bf16[1024,384]{1,0:T(8,128)(2,1)} %get-tuple-element.114.refs_2_, ...), custom_call_target="tpu_custom_call" | custom-call | tf_op jit(solution)/shard_map/last_kernel/pallas_call | solution.py:1313
  565.3 0.8 slice.106
  566.1 1.2 slice_bitcast_fusion.3
  567.4 1.0 slice_bitcast_fusion.2
  568.9 0.7 slice.128
  569.6 0.8 fusion.5
  571.4 0.7 slice.111
  572.1 1.3 slice_bitcast_fusion
  575.4 1.0 maximum_convert_fusion.3
  576.9 1.9 maximum_convert_fusion.2
  578.8 2.3 maximum_convert_fusion
  581.1 2.3 maximum_convert_fusion.1
  583.4 0.8 copy.29
  584.2 0.8 copy.30
  (36 shorter events, 4.7 us)
Async XLA Ops:
  509.6 57.7 %copy-start.4 = (bf16[1056,384]{1,0:T(8,128)(2,1)S(1)}, bf16[1056,384]{1,0:T(8,128)(2,1)}, u32[]{:S(2)}) copy-start(bf16[1056,384]{1,0:T(8,128)(2,1)} %get-tuple-element.121) | copy-start | bytes 2433028
  565.3 5.1 copy-start.3
  567.4 3.2 copy-start.9
  570.5 4.9 copy-start.7
  570.5 4.9 copy-start.8
  575.4 1.5 copy-start
  578.8 2.3 copy-start.1
  578.8 2.4 copy-start.2
  581.1 2.3 copy-start.5
  581.1 3.1 copy-start.6

commit v3 on v2

--- a/solution.py
+++ b/solution.py
@@ -399,15 +399,19 @@
     def __init__(self, spot, grad, whole, refs):
         self.landed, self.share, self.later_landed, sems = refs
         self.grad, self.spot = grad, spot
-        size = grad.shape[0]
-        mine, other = whole.at[spot.part(size)], whole.at[spot.part(size, False)]
         share = self.share
-        self.first = remote(grad.at[spot.part(size, False)], self.landed, sems.at[0], sems.at[1], spot.over_y)
-        self.over = remote(share, self.later_landed, sems.at[2], sems.at[3], spot.over_h)
-        self.along = remote(share, mine, sems.at[4], sems.at[5], spot.over_y)
-        self.near = remote(share, mine, sems.at[6], sems.at[7], spot.core)
-        self.later = remote(other, other, sems.at[8], sems.at[9], spot.core)
-        self.local = pltpu.make_async_copy(share, mine, sems.at[10])
+        if grad is not None:
+            other = grad.at[spot.part(grad.shape[0], False)]
+            self.first = remote(other, self.landed, sems.at[0], sems.at[1], spot.over_y)
+        if self.later_landed is not None:
+            self.over = remote(share, self.later_landed, sems.at[2], sems.at[3], spot.over_h)
+        if whole is not None:
+            size = whole.shape[0]
+            mine, other = whole.at[spot.part(size)], whole.at[spot.part(size, False)]
+            self.along = remote(share, mine, sems.at[4], sems.at[5], spot.over_y)
+            self.near = remote(share, mine, sems.at[6], sems.at[7], spot.core)
+            self.later = remote(other, other, sems.at[8], sems.at[9], spot.core)
+            self.local = pltpu.make_async_copy(share, mine, sems.at[10])
 
     def start(self):
         self.first.start()
@@ -416,6 +420,8 @@
         self.first.wait_recv()
         mine = self.grad[self.spot.part(self.grad.shape[0])]
         self.share[...] = (mine.astype(F32) + self.landed[...].astype(F32)).astype(BF)
+
+    def send_over(self):
         pl.when(self.spot.away)(self.over.start)
 
     def add_over(self):
@@ -423,6 +429,10 @@
         def _():
             self.over.wait_recv()
             self.share[...] = (self.share[...].astype(F32) + self.later_landed[...].astype(F32)).astype(BF)
+
+    def spread(self):
+        @pl.when(self.spot.home)
+        def _():
             self.along.start()
             self.near.start()
             self.local.start()
@@ -433,9 +443,13 @@
             self.along.wait_recv()
             self.later.start()
 
-    def finish(self):
+    def finish_first(self):
         self.first.wait_send()
 
+    def finish_over(self):
+        pl.when(self.spot.away)(self.over.wait_send)
+
+    def finish_spread(self):
         @pl.when(self.spot.home)
         def _():
             self.along.wait_send()
@@ -445,9 +459,13 @@
 
         @pl.when(self.spot.away)
         def _():
-            self.over.wait_send()
             self.near.wait_recv()
             self.later.wait_recv()
+
+    def finish(self):
+        self.finish_first()
+        self.finish_over()
+        self.finish_spread()
 
 
 class SmallSum:
@@ -582,17 +600,17 @@
     return jnp.where(row == column, 1.0 / HD, 0.0).astype(BF)
 
 
-def project(k, block, gather, slot, stream):
-    span = gather.span(stream)
+def project(k, block, gather, raw_ref, qk_ref, v_ref, slot, stream):
+    rows = pl.ds(pl.multiple_of((slot * 2 + stream) * gather.rows, gather.rows), gather.rows)
     projected = dot(gather.part(slot, stream), k.qkv_weight[...]) + k.biases[block : block + 1, : 6 * HD]
     raw, values = pack_queries_keys(projected)
-    k.raw[slot, span] = raw
+    raw_ref[rows] = raw
     average = averager(4 * HD)
     centered = raw - dot_fine(raw, average)
     scale = lax.rsqrt(dot_fine(centered * centered, average) + EPSILON)
     gain, offset = k.head_gains[block : block + 1], k.head_offsets[block : block + 1]
-    k.qk[slot, span] = (centered * scale * gain + offset).astype(BF)
-    k.v[slot, span] = values.astype(BF)
+    qk_ref[rows] = (centered * scale * gain + offset).astype(BF)
+    v_ref[rows] = values.astype(BF)
 
 
 def in_three(values):
@@ -632,19 +650,18 @@
     k.mixed[rows] = both.astype(BF)
 
 
-def first_kernel(k):
+def enter(k):
     spot = k.spot
-    spot.greet(spot.over_x, spot.over_z, spot.core, spot.over_y, spot.over_h, spot.partner)
-    gather = Gather(spot, k.gather)
+    gather = Gather(spot, k.gather_first)
     swaps = [
         Swap(spot, k.frames.at[0, gather.span(stream)], k.hidden.at[gather.span(stream)], k.swaps[stream])
         for stream in range(2)
     ]
     swaps.append(Swap(spot, k.own_biases, k.biases, k.swaps[2]))
-    swaps[0].start()
-    swaps[2].start()
-    swaps[0].finish()
-    swaps[1].start()
+    cotangent = Swap(spot, k.cotangent.at[0], k.cotangent_here, k.swaps[3])
+    weighting = Swap(spot, k.weighting, k.weighting_here, k.swaps[4])
+    for swap in swaps:
+        swap.start()
     for stream in range(2):
         swaps[stream].arrive()
         rows = k.hidden[gather.span(stream)].astype(F32)
@@ -652,68 +669,74 @@
         if stream == 1:
             gather.pass_on(0)
         gather.put(stream, values)
-    qkv, out, up = (
-        Move(spot, own.at[0], got, refs)
-        for own, got, refs in zip((k.qkv_own, k.out_own, k.up_own), (k.qkv_got, k.out_got, k.up_got), k.moves)
-    )
-    for move in (qkv, out, up):
-        move.start()
+    owns = (k.qkv_own, k.out_own, k.up_own, k.down_own)
+    gots = (k.qkv_got, k.out_got, k.up_got, k.down_got)
+    qkv, out, up, down = (Move(spot, own.at[0], got, refs) for own, got, refs in zip(owns, gots, k.moves))
     k.saves.hidden()
     gather.pass_on(1)
+    for stream in range(2):
+        gather.arrive_core(stream, 0)
+    for move in (qkv, out, up, down):
+        move.start()
     qkv.relay(0)
     qkv.relay(1)
     gather.arrive(0, 1)
     qkv.finish()
     swaps[2].arrive()
-    qkv.pick(k.qkv_weight, k.pick).wait()
+    qkv.pick(k.qkv_weight, k.pick.at[0]).wait()
 
     def visit(index, carry):
         stream, step = index // 4, lax.rem(index, 4)
         pl.when(index > 1)(lambda: gather.arrive(stream, step))
-        project(k, 0, gather, spot.slot(spot.c, step), stream)
-        gather.arrive_core(stream, step)
-        project(k, 0, gather, spot.slot(1 - spot.c, step), stream)
-
-        @pl.when(index == 6)
+        project(k, 0, gather, k.raw_first, k.qk_in, k.v_in, spot.slot(spot.c, step), stream)
+        pl.when(step > 0)(lambda: gather.arrive_core(stream, step))
+        project(k, 0, gather, k.raw_first, k.qk_in, k.v_in, spot.slot(1 - spot.c, step), stream)
+
+        @pl.when(index == 3)
         def _():
             out.relay(0)
             out.relay(1)
-            up.relay(0)
-
+            cotangent.start()
+            weighting.start()
+
+        pl.when(index == 6)(lambda: up.relay(0))
         return carry
 
     lax.fori_loop(0, 8, visit, 0)
-    k.saves.gathered(gather.held)
-    k.saves.raw()
-    k.saves.qk()
-    k.saves.v()
-    up.relay(1)
-    for swap in swaps[1:]:
+    out.finish()
+    out_pick = out.pick(k.out_weight, k.pick.at[1])
+    k.saves.gathered_first(gather.held)
+    k.saves.raw_first()
+    k.saves.qk_in()
+    k.saves.v_in()
+    for swap in swaps:
         swap.finish()
     gather.finish()
-    out.finish()
-    up.finish()
+    out_pick.wait()
+    return up, down, (cotangent, weighting)
 
 
 def forward_kernel(is_last, k):
     spot = k.spot
     block = 1 if is_last else 0
     spot.greet(spot.over_x, spot.over_z, spot.core, spot.over_y, spot.over_h, spot.partner)
-    down = Move(spot, k.down_own.at[block], k.down_got, k.moves[0])
     if is_last:
+        down = Move(spot, k.down_own.at[1], k.down_got, k.moves[0])
         up = Move(spot, k.up_own.at[1], k.up_got, k.moves[1])
         up.start()
         others = []
+        k.loads.qk_in.wait()
+        k.loads.v_in.wait()
+        k.loads.out_weight.wait()
+        k.loads.hidden.wait()
     else:
-        down.start()
-        others = [Move(spot, k.qkv_own.at[1], k.qkv_got, k.moves[1]), Move(spot, k.out_own.at[1], k.out_got, k.moves[2])]
+        up, down, swaps = enter(k)
+        owns, gots = (k.qkv_own, k.out_own), (k.qkv_got_later, k.out_got_later)
+        others = [Move(spot, own.at[1], got, refs) for own, got, refs in zip(owns, gots, k.moves[4:])]
     first, gather, later = Scatter(spot, k.local, k.one), Gather(spot, k.gather), Scatter(spot, k.local, k.two)
     rows_of = gather.span
     size = gather.held.shape[1]
     keys = k.mixed.shape[0] if is_last else FRAME_TOK
-    k.loads.qk_in.wait()
-    k.loads.v_in.wait()
-    k.loads.out_weight.wait()
 
     def term_attention(slot, stream):
         start = pl.multiple_of(slot * size + stream * (size // 2), size // 2)
@@ -730,12 +753,12 @@
                 down.start()
 
         else:
+            pl.when(index == 1)(lambda: up.relay(1))
             pl.when(index == 6)(lambda: down.relay(0))
 
     first.produce(term_attention, before)
     k.saves.exact()
     k.saves.query()
-    k.loads.hidden.wait()
     for stream in range(2):
         rows = rows_of(stream)
         branch = first.result(stream) + k.offsets[block, 2:3]
@@ -745,20 +768,12 @@
         gather.put(stream, (norm_parts(middle)[0] * k.gains[block, 1:2] + k.offsets[block, 1:2]).astype(BF))
         if stream == 0:
             first.relay(1)
-            if is_last:
-                down.relay(0)
-            else:
-                down.relay(1)
+            down.relay(0 if is_last else 1)
             gather.pass_on(0)
     if is_last:
         down.relay(1)
-        up.finish()
-        up_pick = up.pick(k.up_weight, k.pick.at[0])
-    if is_last:
-        cotangent = Swap(spot, k.cotangent.at[0], k.cotangent_here, k.swaps[0])
-        weighting = Swap(spot, k.weighting, k.weighting_here, k.swaps[1])
-        cotangent.start()
-        weighting.start()
+    up.finish()
+    up_pick = up.pick(k.up_weight, k.pick.at[0])
     for move in others:
         move.start()
     k.saves.branch()
@@ -767,10 +782,7 @@
     gather.pass_on(1)
     down.finish()
     down_pick = down.pick(k.down_weight, k.pick.at[1])
-    if is_last:
-        up_pick.wait()
-    else:
-        k.loads.up_weight.wait()
+    up_pick.wait()
     down_pick.wait()
 
     def term(slot, stream):
@@ -807,14 +819,14 @@
     gather.finish()
     later.finish()
     if is_last:
-        for swap in (cotangent, weighting):
-            swap.arrive()
-            swap.finish()
         return
+    for swap in swaps:
+        swap.arrive()
+        swap.finish()
     for move in others:
         move.finish()
     others[0].pick(k.qkv_weight, k.pick.at[0]).wait()
-    onward.consume(functools.partial(project, k, 1, onward), 1)
+    onward.consume(functools.partial(project, k, 1, onward, k.raw, k.qk, k.v), 1)
     k.saves.gathered(onward.held)
     k.saves.raw()
     k.saves.qk()
@@ -919,10 +931,10 @@
     tokens = 8 * size
     keys = tokens if is_first else FRAME_TOK
     sums = [
-        Total(spot, grad.at[rows], whole.at[rows], refs)
+        Total(spot, grad.at[rows], None if whole is None else whole.at[rows], refs)
         for (grad, whole), pieces in (
             ((k.down_grad, k.down_whole), zip(pieces_of(k.down_grad), k.down_total)),
-            ((k.up_grad, k.up_whole), zip(pieces_of(k.up_grad), k.up_total)),
+            ((k.up_grad, k.up_whole if is_first else None), zip(pieces_of(k.up_grad), k.up_total)),
         )
         for rows, refs in pieces
     ]
@@ -941,6 +953,7 @@
         gathered = pltpu.make_async_copy(k.gathered, k.shared, k.pick.at[0])
         gathered.start()
         out.add()
+        out.send_over()
         gathered.wait()
         qkv_weight_grad(k, k.shared)
         qkv.start()
@@ -983,7 +996,9 @@
     else:
         above.finish()
         qkv.add()
+        qkv.send_over()
         out.add_over()
+        out.spread()
     k.loads.down_weight.wait()
     k.loads.up_weight.wait()
     k.loads.slope.wait()
@@ -1038,10 +1053,14 @@
     second.wait()
     up_piece(0)
     up_piece(1)
+    if not is_first:
+        gathered = pltpu.make_async_copy(k.gathered_first, k.shared, k.pick.at[0])
+        gathered.start()
     onward.pass_on(0)
     leave_rows(1)
     if not is_first:
         qkv.add_over()
+        qkv.spread()
         out.relay()
     k.saves.middle_grad()
     if not is_first:
@@ -1069,7 +1088,7 @@
 
     def use(slot):
         grad = dot_rt(onward.held[slot], k.out_weight[...]).astype(BF).astype(F32)
-        slice_back(k, keys, 512, slot * size, size, grad)
+        slice_back(k, keys, 1024, slot * size, size, grad)
 
     def visit(step, carry):
         for stream in range(2):
@@ -1079,8 +1098,9 @@
         @pl.when(step == 0)
         def _():
             onward.pass_on(1)
-            sums[0].add()
-            sums[1].add()
+            for part in sums[:2]:
+                part.add()
+                part.send_over()
 
         for stream in range(2):
             onward.arrive_core(stream, step)
@@ -1089,6 +1109,7 @@
         @pl.when(step == 0)
         def _():
             sums[2].add()
+            sums[2].send_over()
             if not is_first:
                 qkv.relay()
                 early.step(1)
@@ -1096,19 +1117,24 @@
         @pl.when(step == 1)
         def _():
             sums[3].add()
+            sums[3].send_over()
             sums[0].add_over()
+            sums[0].spread()
             if not is_first:
                 early.step(2)
 
         @pl.when(step == 2)
         def _():
             sums[1].add_over()
+            sums[1].spread()
             if not is_first:
                 early.step(3)
 
         @pl.when(step == 3)
         def _():
             sums[2].add_over()
+            if is_first:
+                sums[2].spread()
             sums[0].relay()
             sums[1].relay()
             if not is_first:
@@ -1119,6 +1145,9 @@
     lax.fori_loop(0, 4, visit, 0)
     k.out_grad[...] = dot_lt(k.exact[...].astype(BF), wide(onward.held)).astype(BF)
     k.saves.out_grad()
+    if not is_first:
+        qkv.finish()
+        out.finish()
     k.loads.raw_in.wait()
     k.head_small[...] = jnp.zeros_like(k.head_small)
     qkv_rows = k.qkv_rows if is_first else k.above_qkv
@@ -1130,18 +1159,27 @@
     lax.fori_loop(0, 8, leave, 0)
     k.saves.grad_qkv(qkv_rows)
     onward.finish()
-    if not is_first:
-        early.step(5)
-    sums[3].add_over()
-    sums[2].relay()
-    sums[3].relay()
     if is_first:
         layer.arrive()
         layer.finish()
-    else:
-        sums += [qkv, out]
-    for total in sums:
-        total.finish()
+        sums[3].add_over()
+        sums[3].spread()
+        for part in sums[2:]:
+            part.relay()
+        for part in sums:
+            part.finish()
+        return
+    gathered.wait()
+    qkv_weight_grad(k, k.shared)
+    k.saves.qkv_grad_first(k.qkv_grad)
+    early.step(5)
+    sums[3].add_over()
+    for part, save in zip(sums[2:], (k.saves.up_share, k.saves.up_share_later)):
+        save(part.share)
+        part.finish_first()
+        part.finish_over()
+    for part in sums[:2]:
+        part.finish()
 
 
 def last_kernel(k):
@@ -1151,33 +1189,41 @@
     )
     scatter = Scatter(spot, k.local, k.one)
     out = Total(spot, k.out_grad_in, k.out_whole, k.out_total)
-    pieces = pieces_of(k.qkv_grad)
-    sums = [
-        Total(spot, k.qkv_grad.at[rows], k.qkv_whole.at[rows], refs) for rows, refs in zip(pieces, k.qkv_total)
+    qkv = Total(spot, k.qkv_grad, k.qkv_whole, k.qkv_total)
+    cut = k.up_share.shape[0] * 2
+    up = [
+        Total(spot, None, k.up_whole.at[pl.ds(0, cut)], [None, k.up_share, None, k.up_total.at[0]]),
+        Total(
+            spot,
+            None,
+            k.up_whole.at[pl.ds(cut, k.up_whole.shape[0] - cut)],
+            [None, k.up_share_later, None, k.up_total.at[1]],
+        ),
     ]
+    k.loads.qkv_grad.wait()
+    k.loads.out_grad_in.wait()
+    qkv.start()
     out.start()
     k.loads.qkv_weight.wait()
     k.loads.above_qkv.wait()
     scatter.produce(lambda slot, stream: dot_rt(k.above_qkv[slot, scatter.span(stream)], k.qkv_weight[...]))
+    k.loads.up_share.wait()
+    k.loads.up_share_later.wait()
+    for part in up:
+        part.spread()
     late = QuickSum(spot, k.late, k.late_sum)
-    k.loads.gathered.wait()
-    rows = wide(k.above_qkv)
-    cut = k.gathered.shape[2] // 2
-    k.qkv_grad[:cut] = dot_lt(k.gathered[:, :, :cut].reshape(rows.shape[0], cut), rows).astype(BF)
-    sums[0].start()
-    scatter.relay(1)
-    out.add()
-    k.qkv_grad[cut : 2 * cut] = dot_lt(k.gathered[:, :, cut:].reshape(rows.shape[0], cut), rows).astype(BF)
-    total = jnp.sum(rows.astype(F32), axis=0, keepdims=True)
-    row = lax.broadcasted_iota(jnp.int32, (k.qkv_grad.shape[0] - 2 * cut, k.qkv_grad.shape[1]), 0)
-    k.qkv_grad[2 * cut :] = jnp.where(row == 0, total, 0.0).astype(BF)
-    sums[1].start()
     lanes = 4 * HD
     k.late[...] = jnp.zeros_like(k.late)
     k.late[2:3, :lanes] = k.head_later[0:1]
     k.late[2:3, lanes : 2 * lanes] = k.head_later[1:2]
+    scatter.relay(1)
+    for part in (qkv, out):
+        part.add()
+        part.send_over()
     k.loads.hidden.wait()
     k.loads.middle_grad.wait()
+    for part in up:
+        part.relay()
     swaps = []
     for stream in range(2):
         span = scatter.span(stream)
@@ -1189,25 +1235,50 @@
         swap = Swap(spot, k.grad_in.at[span], k.input_grad.at[span], k.swaps[stream])
         swap.start()
         swaps.append(swap)
-        if stream == 0:
-            sums[0].add()
     late.start()
-    sums[1].add()
-    out.add_over()
+    for part in (qkv, out):
+        part.add_over()
+        part.spread()
     late.step()
-    sums[0].add_over()
+    qkv.relay()
     out.relay()
     late.end()
-    sums[1].add_over()
-    sums[0].relay()
-    sums[1].relay()
     for swap in swaps:
         swap.arrive()
         swap.finish()
-    for part in sums:
+    for part in (out, qkv):
         part.finish()
-    out.finish()
+    for part in up:
+        part.finish_spread()
     scatter.finish()
+
+
+def gather_results(k):
+    sums = (
+        (k.down, k.saves.down, (k.down_first, k.down_later), (k.loads.down_first, k.loads.down_later), None),
+        (k.up, k.saves.up, (k.up_first, k.up_later), (k.loads.up_first, k.loads.up_later), k.up_bias),
+        (k.out, k.saves.out, (k.out_first, k.out_later), (k.loads.out_first, k.loads.out_later), None),
+        (k.qkv, k.saves.qkv, (k.qkv_first, k.qkv_later), (k.loads.qkv_first, k.loads.qkv_later), k.qkv_bias),
+    )
+    for whole, save, parts, loads, bias in sums:
+        size = whole.shape[1]
+        for block in range(2):
+            loads[block].wait()
+            whole[block] = parts[block][:size].astype(F32)
+            if bias is not None:
+                bias[block : block + 1] = parts[block][size : size + 16][0:1].astype(F32)
+        save()
+    early, late = k.early[...], k.late[...]
+    gains = (late[0:1], early[10:11], early[12:13], early[8:9], early[14:15], early[2:3], early[4:5], early[0:1])
+    offsets = (late[1:2], early[11:12], early[13:14], early[9:10], early[15:16], early[3:4], early[5:6], early[1:2])
+    for number in range(8):
+        k.gain[number // 4, number % 4 : number % 4 + 1] = gains[number]
+        k.offset[number // 4, number % 4 : number % 4 + 1] = offsets[number]
+    for block, row in enumerate((late[2:3], early[16:17])):
+        for kind, ref in enumerate((k.head_gain, k.head_offset)):
+            for part in range(2):
+                start = kind * 4 * HD + part * 2 * HD
+                ref[block, part : part + 1] = row[:, start : start + HD] + row[:, start + HD : start + 2 * HD]
 
 
 class Own:
@@ -1273,7 +1344,7 @@
             return [find(part) for part in item] if isinstance(item, list) else held[item]
 
         k = types.SimpleNamespace(**{key: find(item) for key, item in layout.items()})
-        k.spot = Spot()
+        k.spot = None if number is None else Spot()
         saving = []
         loads, saves = {}, {}
 
@@ -1318,7 +1389,7 @@
         out_specs=[vmem if kind == INSIDE else outside for kind in kinds],
         scratch_shapes=shapes,
         compiler_params=pltpu.CompilerParams(
-            collective_id=number, has_side_effects=True, vmem_limit_bytes=VMEM_LIMIT
+            collective_id=number, has_side_effects=number is not None, vmem_limit_bytes=VMEM_LIMIT
         ),
     )(*operands)
     return types.SimpleNamespace(**dict(zip(out_keys, found)))
@@ -1355,9 +1426,6 @@
     def moved(weight):
         return shape(*weight.shape[1:], BF), APART
 
-    def flat(values):
-        return values.reshape(tokens, values.shape[2])
-
     biases = jnp.concatenate([qkv_bias, up_bias], axis=1).astype(F32)
     biases = jnp.pad(biases, ((0, 6), (0, 0)))
     weighting = visible[0].astype(F32) * (query_count[0].astype(F32) / QMAX)
@@ -1367,58 +1435,12 @@
     )
     norms = dict(gains=norm_gain, offsets=norm_offset)
     heads = dict(head_gains=head_gains, head_offsets=head_offsets)
-    qkv_outs = dict(
-        gathered=(shape(8, rows, width, BF), TARGET),
-        raw=(shape(8, rows, 2 * inner, F32), SAVED),
-        qk=(shape(8, rows, 2 * inner, BF), SAVED),
-        v=(shape(8, rows, inner, BF), SAVED),
-    )
-    entry = run(
-        first_kernel,
-        0,
-        dict(
-            frames=Outside(frames_in),
-            own_biases=biases,
-            qkv_own=Outside(qkv_weight),
-            out_own=Outside(out_weight),
-            up_own=Outside(up_weight),
-            **norms,
-            **heads,
-        ),
-        dict(
-            hidden=(shape(rows, width, BF), SAVED),
-            biases=(shape(*biases.shape, F32), INSIDE),
-            qkv_got=moved(qkv_weight),
-            out_got=moved(out_weight),
-            up_got=moved(up_weight),
-            **qkv_outs,
-        ),
-        dict(
-            gather=gather,
-            swaps=[Swap.scratch] * 3,
-            moves=[Move.scratch] * 3,
-            qkv_weight=pltpu.VMEM(qkv_weight.shape[1:], BF),
-            pick=DMA,
-        ),
-    )
-    biases = entry.biases
-    down_buffer = pltpu.VMEM(down_weight.shape[1:], BF)
-
-    def forward(is_last, came, **extra):
-        inputs, outputs, scratch = extra.pop("inputs"), extra.pop("outputs"), extra.pop("scratch")
+    def forward(is_last, inputs, outputs, scratch):
         block = 1 if is_last else 0
         return run(
             functools.partial(forward_kernel, is_last),
             1 + block,
-            dict(
-                qk_in=Load(flat(came.qk)),
-                v_in=Load(flat(came.v)),
-                hidden=Load(came.hidden),
-                down_own=Outside(down_weight),
-                biases=biases,
-                **norms,
-                **inputs,
-            ),
+            dict(up_own=Outside(up_weight), down_own=Outside(down_weight), **norms, **inputs),
             dict(
                 exact=(shape(tokens, inner, F32), SAVED),
                 query=(shape(2, tokens, inner, BF), SAVED),
@@ -1429,6 +1451,7 @@
                 slope=(shape(8, rows, units, BF), SAVED),
                 branch_two=(shape(rows, width, F32), SAVED),
                 state=(shape(rows, width, BF if is_last else F32), SAVED),
+                up_got=moved(up_weight),
                 down_got=moved(down_weight),
                 **outputs,
             ),
@@ -1439,42 +1462,67 @@
                 gather=gather,
                 pick=DMA((2,)),
                 mixed=pltpu.VMEM((tokens, inner), BF),
-                down_weight=down_buffer,
+                up_weight=pltpu.VMEM(up_weight.shape[1:], BF),
+                down_weight=pltpu.VMEM(down_weight.shape[1:], BF),
                 **scratch,
             ),
         )
 
     lower = forward(
         False,
-        entry,
-        inputs=dict(
-            out_weight=Own(out_weight, 0, entry.out_got),
-            up_weight=Own(up_weight, 0, entry.up_got),
+        dict(
+            frames=Outside(frames_in),
+            own_biases=biases,
             qkv_own=Outside(qkv_weight),
             out_own=Outside(out_weight),
+            cotangent=Outside(cotangent),
+            weighting=weighting,
             **heads,
         ),
-        outputs=dict(qkv_got=moved(qkv_weight), out_got=moved(out_weight), **qkv_outs),
-        scratch=dict(gather_next=gather, qkv_weight=pltpu.VMEM(qkv_weight.shape[1:], BF), moves=[Move.scratch] * 3),
-    )
-    between = types.SimpleNamespace(hidden=lower.state, **{key: getattr(lower, key) for key in qkv_outs})
+        dict(
+            hidden=(shape(rows, width, BF), SAVED),
+            biases=(shape(*biases.shape, F32), INSIDE),
+            cotangent_here=(shape(rows, width, BF), APART),
+            weighting_here=(shape(rows, 128, F32), APART),
+            qkv_got=moved(qkv_weight),
+            out_got=moved(out_weight),
+            qkv_got_later=moved(qkv_weight),
+            out_got_later=moved(out_weight),
+            gathered_first=(shape(8, rows, width, BF), TARGET),
+            raw_first=(shape(tokens, 2 * inner, F32), SAVED),
+            qk_in=(shape(tokens, 2 * inner, BF), SAVED),
+            v_in=(shape(tokens, inner, BF), SAVED),
+            gathered=(shape(8, rows, width, BF), TARGET),
+            raw=(shape(tokens, 2 * inner, F32), SAVED),
+            qk=(shape(tokens, 2 * inner, BF), SAVED),
+            v=(shape(tokens, inner, BF), SAVED),
+        ),
+        dict(
+            gather_first=gather,
+            gather_next=gather,
+            swaps=[Swap.scratch] * 5,
+            moves=[Move.scratch] * 6,
+            qkv_weight=pltpu.VMEM(qkv_weight.shape[1:], BF),
+            out_weight=pltpu.VMEM(out_weight.shape[1:], BF),
+        ),
+    )
+    entry = types.SimpleNamespace(
+        hidden=lower.hidden, gathered=lower.gathered_first, raw=lower.raw_first, qk=lower.qk_in, v=lower.v_in
+    )
+    between = types.SimpleNamespace(
+        hidden=lower.state, gathered=lower.gathered, raw=lower.raw, qk=lower.qk, v=lower.v
+    )
     upper = forward(
         True,
-        between,
-        inputs=dict(
-            out_weight=Own(out_weight, 1, lower.out_got),
-            up_own=Outside(up_weight),
-            cotangent=Outside(cotangent),
-            weighting=weighting,
+        dict(
+            qk_in=Load(between.qk),
+            v_in=Load(between.v),
+            hidden=Load(between.hidden),
+            biases=lower.biases,
+            out_weight=Own(out_weight, 1, lower.out_got_later),
         ),
-        outputs=dict(
-            up_got=moved(up_weight),
-            cotangent_here=(shape(rows, width, BF), APART),
-            weighting_here=(shape(rows, 128, F32), APART),
-        ),
-        scratch=dict(
-            swaps=[Swap.scratch] * 2, up_weight=pltpu.VMEM(up_weight.shape[1:], BF), moves=[Move.scratch] * 2
-        ),
+        dict(),
+        dict(moves=[Move.scratch] * 2),
     )
 
     qkv_grad = pltpu.VMEM((width + pad, 3 * inner), BF)
@@ -1501,20 +1549,19 @@
                 activated=Load(kept.activated),
                 second=Outside(kept.second),
                 out_weight=Own(out_weight, block, out_got),
-                qk_in=Load(flat(came.qk)),
-                v_in=Load(flat(came.v)),
+                qk_in=Load(came.qk),
+                v_in=Load(came.v),
                 query=Load(kept.query),
                 exact=Load(kept.exact),
-                raw_in=Load(flat(came.raw)),
+                raw_in=Load(came.raw),
                 gains=norm_gain,
                 head_gains=head_gains,
             ),
             dict(
                 middle_grad=(shape(rows, width, F32), SAVED),
                 grad_qkv=(shape(8, rows, 3 * inner, BF), TARGET),
+                down_whole=(shape(units, width, BF), APART),
                 out_grad=(shape(inner, width, BF), SAVED),
-                down_whole=(shape(units, width, BF), APART),
-                up_whole=(shape(width + pad, units, BF), APART),
                 small=(shape(8, width, F32), INSIDE),
                 head_small=(shape(2, 2 * inner, F32), INSIDE),
                 **outputs,
@@ -1546,27 +1593,31 @@
         between,
         upper,
         upper.up_got,
-        lower.out_got,
+        lower.out_got_later,
         dict(
-            cotangent=Load(upper.cotangent_here),
-            weighting=upper.weighting_here,
+            cotangent=Load(lower.cotangent_here),
+            weighting=lower.weighting_here,
             state=Outside(upper.state),
             middle=Load(upper.middle),
             branch=Load(upper.branch),
         ),
-        dict(layer_out=(shape(rows, width, BF), APART)),
+        dict(
+            layer_out=(shape(rows, width, BF), APART),
+            up_whole=(shape(width + pad, units, BF), APART),
+        ),
         dict(swap=Swap.scratch, qkv_rows=pltpu.VMEM((8, rows, 3 * inner), BF)),
     )
     lower_back = backward(
         False,
         entry,
         lower,
-        entry.up_got,
-        entry.out_got,
+        lower.up_got,
+        lower.out_got,
         dict(
             above_qkv=Load(upper_back.grad_qkv),
-            qkv_weight=Own(qkv_weight, 1, lower.qkv_got),
+            qkv_weight=Own(qkv_weight, 1, lower.qkv_got_later),
             gathered=Outside(between.gathered),
+            gathered_first=Outside(entry.gathered),
             above_hidden=Load(between.hidden),
             above_middle_grad=Load(upper_back.middle_grad),
             out_grad_in=upper_back.out_grad,
@@ -1575,7 +1626,14 @@
             small_first=upper_back.small,
             head_first=upper_back.head_small,
         ),
-        dict(early=(shape(24, width, F32), INSIDE), **qkv_whole, **out_whole),
+        dict(
+            early=(shape(24, width, F32), INSIDE),
+            up_share=(shape((width + pad) // 64 * 16, units, BF), TARGET),
+            up_share_later=(shape((width + pad) // 2 - (width + pad) // 64 * 16, units, BF), TARGET),
+            qkv_grad_first=(shape(width + pad, 3 * inner, BF), TARGET),
+            **qkv_whole,
+            **out_whole,
+        ),
         dict(
             early_sum=SmallSum.scratch(24, width),
             two=scatter,
@@ -1586,17 +1644,20 @@
         5,
         dict(
             above_qkv=Load(lower_back.grad_qkv),
-            qkv_weight=Own(qkv_weight, 0, entry.qkv_got),
-            gathered=Load(entry.gathered),
+            qkv_weight=Own(qkv_weight, 0, lower.qkv_got),
             hidden=Load(entry.hidden),
             middle_grad=Load(lower_back.middle_grad),
-            out_grad_in=lower_back.out_grad,
+            out_grad_in=Load(lower_back.out_grad),
+            qkv_grad=Load(lower_back.qkv_grad_first),
+            up_share=Load(lower_back.up_share),
+            up_share_later=Load(lower_back.up_share_later),
             gains=norm_gain,
             head_later=lower_back.head_small,
         ),
         dict(
             input_grad=(shape(rows, width, BF), APART),
             late=(shape(8, width, F32), INSIDE),
+            up_whole=(shape(width + pad, units, BF), APART),
             **qkv_whole,
             **out_whole,
         ),
@@ -1606,34 +1667,53 @@
             grad_in=pltpu.VMEM((rows, width), BF),
             swaps=[Swap.scratch] * 2,
             late_sum=QuickSum.scratch(8, width),
-            qkv_grad=qkv_grad,
-            qkv_total=in_pieces(width + pad, 3 * inner),
+            qkv_total=Total.scratch(width + pad, 3 * inner),
             **out_total,
+            up_total=DMA((2, 11)),
         ),
     )
-    early, late = lower_back.early, last.late
-    gains = [late[0], early[10], early[12], early[8], early[14], early[2], early[4], early[0]]
-    offsets = [late[1], early[11], early[13], early[9], early[15], early[3], early[5], early[1]]
-    head_sums = jnp.stack([late[2, : 8 * HD], early[16, : 8 * HD]]).reshape(2, 2, 2, 2, HD).sum(axis=3)
-
-    def joined(first, later, part):
-        return jnp.stack([first[part], later[part]]).astype(F32)
-
-    qkv_sums, up_sums = (last.qkv_whole, lower_back.qkv_whole), (lower_back.up_whole, upper_back.up_whole)
-    inside = slice(width)
+    found = run(
+        gather_results,
+        None,
+        dict(
+            down_first=Load(lower_back.down_whole),
+            down_later=Load(upper_back.down_whole),
+            up_first=Load(last.up_whole),
+            up_later=Load(upper_back.up_whole),
+            out_first=Load(last.out_whole),
+            out_later=Load(lower_back.out_whole),
+            qkv_first=Load(last.qkv_whole),
+            qkv_later=Load(lower_back.qkv_whole),
+            early=lower_back.early,
+            late=last.late,
+        ),
+        dict(
+            qkv=(shape(2, width, 3 * inner, F32), SAVED),
+            qkv_bias=(shape(2, 3 * inner, F32), INSIDE),
+            out=(shape(2, inner, width, F32), SAVED),
+            up=(shape(2, width, units, F32), SAVED),
+            up_bias=(shape(2, units, F32), INSIDE),
+            down=(shape(2, units, width, F32), SAVED),
+            gain=(shape(2, 4, width, F32), INSIDE),
+            offset=(shape(2, 4, width, F32), INSIDE),
+            head_gain=(shape(2, 2, HD, F32), INSIDE),
+            head_offset=(shape(2, 2, HD, F32), INSIDE),
+        ),
+        dict(),
+    )
     return (
         upper_back.layer_out[None],
         last.input_grad[None],
-        joined(*qkv_sums, inside),
-        joined(*qkv_sums, width),
-        joined(last.out_whole, lower_back.out_whole, inside),
-        joined(*up_sums, inside),
-        joined(*up_sums, width),
-        joined(lower_back.down_whole, upper_back.down_whole, inside),
-        jnp.stack(gains).reshape(2, 4, width),
-        jnp.stack(offsets).reshape(2, 4, width),
-        head_sums[:, 0],
-        head_sums[:, 1],
+        found.qkv,
+        found.qkv_bias,
+        found.out,
+        found.up,
+        found.up_bias,
+        found.down,
+        found.gain,
+        found.offset,
+        found.head_gain,
+        found.head_offset,
     )
 
 

time: 594 us -> 559 us (0.941)
  Pallas kernels: 559 us -> 541 us
  other arithmetic: 11.4 us -> 2.66 us
  local copies, waits for them, and re-layouts: 13.2 us -> 4.94 us
    pallas_call x6, Pallas kernels: 559 us -> 541 us  [run(): pl.pallas_call(whole, name=getattr(kernel, 'func', kernel).__name__, out_...]
    convert_element_type x6 -> x0, other arithmetic: 8.67 us -> none  [joined(): return jnp.stack([first[part], later[part]]).astype(F32)]
where the time goes in v3:
time: 559 us; the launch traced here: 550 us
  Pallas kernels  541 us (97%)
    pallas_call x6, Pallas kernels, run(): pl.pallas_call(whole, name=getattr(kernel, 'func', kernel).__name__, out_...  541 us

profile of v3, /device:TPU:0, one launch (start us, length us, event | category | flops | bytes accessed | tf_op | source)
XLA Modules:
  0.0 549.9 jit_solution(18261865192306436199)
XLA Ops:
  1.3 0.7 convert_multiply_fusion
  2.0 0.8 fusion.5
  2.7 0.8 fusion.4
  3.5 0.7 pad_maximum_fusion
  4.2 1.3 fusion.3.refs_5_
  5.5 0.8 broadcast_in_dim.12.refs_9_
  6.2 168.3 %forward_kernel.2 = (f32[2048,128]{1,0:T(8,128)}, bf16[2,2048,128]{2,1,0:T(8,128)(2,1)}, f32[256,1024]{1,0:T(8,128)}, f32[256,1024]{1,0:T(8,128)}, bf16[8,256,10...) custom-call(bf16[2,1024,512]{2,1,0:T(8,128)(2,1)} %refs_15_.1, ...), custom_call_target="tpu_custom_call" | custom-call | tf_op jit(solution)/shard_map/forward_kernel/pallas_call | solution.py:1384
  174.6 84.8 %forward_kernel.3 = (f32[2048,128]{1,0:T(8,128)}, bf16[2,2048,128]{2,1,0:T(8,128)(2,1)}, f32[256,1024]{1,0:T(8,128)}, f32[256,1024]{1,0:T(8,128)}, bf16[8,256,10...) custom-call(bf16[2,1024,512]{2,1,0:T(8,128)(2,1)} %refs_15_.1, ...), custom_call_target="tpu_custom_call" | custom-call | tf_op jit(solution)/shard_map/forward_kernel/pallas_call | solution.py:1384
  259.4 107.2 %backward_kernel.2 = (f32[256,1024]{1,0:T(8,128)}, bf16[8,256,384]{2,1,0:T(8,128)(2,1)}, bf16[512,1024]{1,0:T(8,128)(2,1)}, bf16[128,1024]{1,0:T(8,128)(2,1)}, f...) custom-call(bf16[256,1024]{1,0:T(8,128)(2,1)} %get-tuple-element.84.refs_0_, ...), custom_call_target="tpu_custom_call" | custom-call | tf_op jit(solution)/shard_map/backward_kernel/pallas_call | solution.py:1384
  366.6 123.8 %backward_kernel.3 = (f32[256,1024]{1,0:T(8,128)}, bf16[8,256,384]{2,1,0:T(8,128)(2,1)}, bf16[512,1024]{1,0:T(8,128)(2,1)}, bf16[128,1024]{1,0:T(8,128)(2,1)}, f...) custom-call(bf16[8,256,384]{2,1,0:T(8,128)(2,1)} %get-tuple-element., ...), custom_call_target="tpu_custom_call" | custom-call | tf_op jit(solution)/shard_map/backward_kernel/pallas_call | solution.py:1384
  490.3 48.5 %last_kernel.1 = (bf16[256,1024]{1,0:T(8,128)(2,1)}, f32[8,1024]{1,0:T(8,128)}, bf16[1056,512]{1,0:T(8,128)(2,1)}, bf16[1056,384]{1,0:T(8,128)(2,1)}, bf16[128,1024]{1,0:T(8,128)(2,1)}) custom-call(bf16[8,256,384]{2,1,0:T(8,128)(2,1)} %get-tuple-element.126.refs_0_, bf16[2,1024,384]{2,1,0:T(8,128)(2,1)} %refs_1_.7, ...), custom_call_target="tpu_custom_call" | custom-call | tf_op jit(solution)/shard_map/last_kernel/pallas_call | solution.py:1384
  538.8 0.0 copy-start
  538.8 8.0 %gather_results.1 = (f32[2,1024,384]{2,1,0:T(8,128)}, f32[2,384]{1,0:T(2,128)}, f32[2,128,1024]{2,1,0:T(8,128)}, f32[2,1024,512]{2,1,0:T(8,128)}, f32[2,512]{1,0...) custom-call(bf16[512,1024]{1,0:T(8,128)(2,1)} %get-tuple-element.136, ...), custom_call_target="tpu_custom_call" | custom-call | tf_op jit(solution)/shard_map/gather_results/pallas_call | solution.py:1384
  546.8 0.0 copy-done
  546.8 0.8 copy.29
  547.6 1.9 copy.30
Async XLA Ops:
  538.8 8.0 %copy-start = (bf16[256,1024]{1,0:T(8,128)(2,1)S(1)}, bf16[256,1024]{1,0:T(8,128)(2,1)}, u32[]{:S(2)}) copy-start(bf16[256,1024]{1,0:T(8,128)(2,1)} %get-tuple-element.103) | copy-start | bytes 1572868

commit v4 on v3

--- a/solution.py
+++ b/solution.py
@@ -696,8 +696,6 @@
         def _():
             out.relay(0)
             out.relay(1)
-            cotangent.start()
-            weighting.start()
 
         pl.when(index == 6)(lambda: up.relay(0))
         return carry
@@ -754,7 +752,7 @@
 
         else:
             pl.when(index == 1)(lambda: up.relay(1))
-            pl.when(index == 6)(lambda: down.relay(0))
+            pl.when(index == 6)(lambda: (down.relay(0), swaps[0].start(), swaps[1].start()) and None)
 
     first.produce(term_attention, before)
     k.saves.exact()
@@ -863,6 +861,7 @@
         ones = jnp.where(lane < (HD if head == 0 else 0) + 3, -1.0, 0.0)
         k.key_in[head, rows] = jnp.where(own, k.qk_in[rows, 2 * HD :].astype(F32), ones).astype(BF)
         k.value_in[head, rows] = jnp.where(own, k.v_in[rows].astype(F32), ones).astype(BF)
+    k.key_turned[:, rows] = k.qk_in[rows, 2 * HD :].astype(F32).T.astype(BF)
 
 
 def slice_back(k, keys, block_keys, start, size, grad):
@@ -887,7 +886,7 @@
         key_rows = pl.ds(pl.multiple_of(first + index * block_keys, block_keys), block_keys)
         for head in range(2):
             own = lanes_of_head((size, width), head)
-            own_keys = lanes_of_head((block_keys, width), head)
+            mine = pl.ds(head * HD, HD)
             query = k.query[head, rows]
             grad_rows = k.grad_in[head]
             key = k.key_in[head, key_rows]
@@ -896,11 +895,11 @@
             zeros = jnp.zeros((size, width), BF)
             k.grads[key_rows, 2 * width :] += dot(probs.astype(BF), jnp.where(own, grad_rows, zeros))
             k.grads[key_rows, width : 2 * width] += dot(back, jnp.where(own, query, zeros))
-            k.query_grad[...] += dot_lt(back, jnp.where(own_keys, key, jnp.zeros((block_keys, width), BF)))
+            k.query_grad[mine] += dot(k.key_turned[mine, key_rows], back)
         return carry
 
     lax.fori_loop(0, keys // block_keys, visit, 0)
-    k.grads[rows, :width] = k.query_grad[...]
+    k.grads[rows, :width] = k.query_grad[...].T
 
 
 def leave_heads(k, level, rows, target):
@@ -1254,6 +1253,10 @@
 
 
 def gather_results(k):
+    k.loads.layer_in.wait()
+    k.saves.layer_out(k.layer_in)
+    k.loads.grad_in.wait()
+    k.saves.input_grad(k.grad_in)
     sums = (
         (k.down, k.saves.down, (k.down_first, k.down_later), (k.loads.down_first, k.loads.down_later), None),
         (k.up, k.saves.up, (k.up_first, k.up_later), (k.loads.up_first, k.loads.up_later), k.up_bias),
@@ -1582,7 +1585,8 @@
                 key_in=pltpu.VMEM((2, tokens, inner), BF),
                 value_in=pltpu.VMEM((2, tokens, inner), BF),
                 grad_in=pltpu.VMEM((2, rows, inner), BF),
-                query_grad=pltpu.VMEM((rows, inner), F32),
+                query_grad=pltpu.VMEM((inner, rows), F32),
+                key_turned=pltpu.VMEM((inner, tokens), BF),
                 grads=pltpu.VMEM((tokens, 3 * inner), F32),
                 **scratch,
             ),
@@ -1676,6 +1680,8 @@
         gather_results,
         None,
         dict(
+            layer_in=Load(upper_back.layer_out),
+            grad_in=Load(last.input_grad),
             down_first=Load(lower_back.down_whole),
             down_later=Load(upper_back.down_whole),
             up_first=Load(last.up_whole),
@@ -1698,12 +1704,14 @@
             offset=(shape(2, 4, width, F32), INSIDE),
             head_gain=(shape(2, 2, HD, F32), INSIDE),
             head_offset=(shape(2, 2, HD, F32), INSIDE),
+            layer_out=(shape(rows, width, BF), TARGET),
+            input_grad=(shape(rows, width, BF), TARGET),
         ),
         dict(),
     )
     return (
-        upper_back.layer_out[None],
-        last.input_grad[None],
+        found.layer_out[None],
+        found.input_grad[None],
         found.qkv,
         found.qkv_bias,
         found.out,

time: 559 us -> 553 us (0.989)
  no operation moved by 1% of the time
where the time goes in v4:
time: 553 us; the launch traced here: 543 us
  Pallas kernels  536 us (97%)
    pallas_call x6, Pallas kernels, run(): pl.pallas_call(whole, name=getattr(kernel, 'func', kernel).__name__, out_...  536 us

profile of v4, /device:TPU:0, one launch (start us, length us, event | category | flops | bytes accessed | tf_op | source)
XLA Modules:
  0.0 543.0 jit_solution(12291072997323170827)
XLA Ops:
  1.3 0.7 convert_multiply_fusion
  2.0 0.8 fusion.5
  2.7 0.8 fusion.4
  3.5 0.7 pad_maximum_fusion
  4.2 1.3 fusion.3.refs_5_
  5.5 0.8 broadcast_in_dim.12.refs_9_
  6.2 162.5 %forward_kernel.2 = (f32[2048,128]{1,0:T(8,128)}, bf16[2,2048,128]{2,1,0:T(8,128)(2,1)}, f32[256,1024]{1,0:T(8,128)}, f32[256,1024]{1,0:T(8,128)}, bf16[8,256,10...) custom-call(bf16[2,1024,512]{2,1,0:T(8,128)(2,1)} %refs_15_.1, ...), custom_call_target="tpu_custom_call" | custom-call | tf_op jit(solution)/shard_map/forward_kernel/pallas_call | solution.py:1387
  168.7 85.8 %forward_kernel.3 = (f32[2048,128]{1,0:T(8,128)}, bf16[2,2048,128]{2,1,0:T(8,128)(2,1)}, f32[256,1024]{1,0:T(8,128)}, f32[256,1024]{1,0:T(8,128)}, bf16[8,256,10...) custom-call(bf16[2,1024,512]{2,1,0:T(8,128)(2,1)} %refs_15_.1, ...), custom_call_target="tpu_custom_call" | custom-call | tf_op jit(solution)/shard_map/forward_kernel/pallas_call | solution.py:1387
  254.5 107.2 %backward_kernel.2 = (f32[256,1024]{1,0:T(8,128)}, bf16[8,256,384]{2,1,0:T(8,128)(2,1)}, bf16[512,1024]{1,0:T(8,128)(2,1)}, bf16[128,1024]{1,0:T(8,128)(2,1)}, f...) custom-call(bf16[256,1024]{1,0:T(8,128)(2,1)} %get-tuple-element.86.refs_0_, ...), custom_call_target="tpu_custom_call" | custom-call | tf_op jit(solution)/shard_map/backward_kernel/pallas_call | solution.py:1387
  361.7 123.6 %backward_kernel.3 = (f32[256,1024]{1,0:T(8,128)}, bf16[8,256,384]{2,1,0:T(8,128)(2,1)}, bf16[512,1024]{1,0:T(8,128)(2,1)}, bf16[128,1024]{1,0:T(8,128)(2,1)}, f...) custom-call(bf16[8,256,384]{2,1,0:T(8,128)(2,1)} %get-tuple-element., ...), custom_call_target="tpu_custom_call" | custom-call | tf_op jit(solution)/shard_map/backward_kernel/pallas_call | solution.py:1387
  485.3 48.8 %last_kernel.1 = (bf16[256,1024]{1,0:T(8,128)(2,1)}, f32[8,1024]{1,0:T(8,128)}, bf16[1056,512]{1,0:T(8,128)(2,1)}, bf16[1056,384]{1,0:T(8,128)(2,1)}, bf16[128,1024]{1,0:T(8,128)(2,1)}) custom-call(bf16[8,256,384]{2,1,0:T(8,128)(2,1)} %get-tuple-element.128.refs_0_, bf16[2,1024,384]{2,1,0:T(8,128)(2,1)} %refs_1_.7, ...), custom_call_target="tpu_custom_call" | custom-call | tf_op jit(solution)/shard_map/last_kernel/pallas_call | solution.py:1387
  534.2 8.4 %gather_results.1 = (f32[2,1024,384]{2,1,0:T(8,128)}, f32[2,384]{1,0:T(2,128)}, f32[2,128,1024]{2,1,0:T(8,128)}, f32[2,1024,512]{2,1,0:T(8,128)}, f32[2,512]{1,0...) custom-call(bf16[256,1024]{1,0:T(8,128)(2,1)} %get-tuple-element.105, ...), custom_call_target="tpu_custom_call" | custom-call | tf_op jit(solution)/shard_map/gather_results/pallas_call | solution.py:1387
